TPU v7x, 32 devices: a whole 2x2x4 slice. The times are simulated.
32 devices in a mesh: dp: 8 (over y, x, core), tensor: 4 (over z).
Axes of the slice: x: 2, y: 2, z: 4, core: 2. Of those that a mesh axis runs over, the one named last changes fastest.
Arguments:
- tokens: bfloat16 [8, 2048, 1024], P('dp', 'tensor'), may hold values from -6 to 6
- cotangent: bfloat16 [8, 2048, 1024], P('dp', 'tensor'), may hold values from -6 to 6
- doc_ids: int32 [8, 2048], P('dp'), may hold values from 0 to 21, as said below
- adapter_pick: int32 [8], P('dp'), may hold values from 0 to 7, as said below
- norm_gain: float32 [1024], replicated, may hold values from 0.25 to 1.75
- gate_x_weight: bfloat16 [1024, 2, 2048], P('dp', None, 'tensor'), may hold values from -0.1875 to 0.1875
- bc_weight: bfloat16 [1024, 256], P('dp'), may hold values from -0.1875 to 0.1875
- dt_weight: bfloat16 [1024, 32], P('dp', 'tensor'), may hold values from -0.1875 to 0.1875
- conv_x_weight: float32 [4, 2048], P(None, 'tensor'), may hold values from -3 to 3
- conv_bc_weight: float32 [4, 256], replicated, may hold values from -3 to 3
- conv_x_bias: float32 [2048], P('tensor'), may hold values from -3 to 3
- conv_bc_bias: float32 [256], replicated, may hold values from -3 to 3
- dt_bias: float32 [32], P('tensor'), may hold values from -6 to -2
- a_log: float32 [32], P('tensor'), may hold values from 0 to 2.77
- skip_gain: float32 [32], P('tensor'), may hold values from 0.5 to 1.5
- inner_gain: float32 [2048], P('tensor'), may hold values from 0.25 to 1.75
- out_weight: bfloat16 [2048, 1024], P('tensor', 'dp'), may hold values from -0.125 to 0.125
- in_down: bfloat16 [8, 1024, 16], P(None, 'dp'), may hold values from -0.1875 to 0.1875
- in_up: bfloat16 [8, 16, 2, 32, 64], P(None, None, None, 'tensor', 'dp'), may hold values from -1.5 to 1.5
- out_down: bfloat16 [8, 32, 64, 16], P(None, 'tensor', 'dp'), may hold values from -0.125 to 0.125
- out_up: bfloat16 [8, 16, 1024], P(None, None, 'dp'), may hold values from -1.5 to 1.5
Outputs:
- mixed: float32 [8, 2048, 1024], P('dp', 'tensor')
- tokens_grad: float32 [8, 2048, 1024], P('dp', 'tensor')
- grad_in_down: float32 [8, 1024, 16], P(None, 'dp')
- grad_in_up: float32 [8, 16, 2, 32, 64], P(None, None, None, 'tensor', 'dp')
- grad_out_down: float32 [8, 32, 64, 16], P(None, 'tensor', 'dp')
- grad_out_up: float32 [8, 16, 1024], P(None, None, 'dp')
Inputs may be any that keep to these rules, and one draw needn't show every extreme that they name: `doc_ids`: within each sequence the document numbers start at 0 and rise by one at each document start. Every document has 60 to 800 tokens except the last of a sequence, which may be cut shorter; of the first two documents of each sequence one has 800 tokens and the other 60. `adapter_pick`: each adapter serves exactly 1 sequence.
All inputs are finite; a program needn't handle non-finite values.
Results may differ from a plain program's by a relative error of at most 0.0059.
Values may be sent and summed in bfloat16 or wider, within the bound.
No kernel may reach another device: no remote copies, remote signals or barrier semaphores. Data moves between devices by JAX's collectives and lax.ppermute only.
A program may use at most 192 MiB of HBM per device.

v0:
```python
from functools import partial

import jax
import jax.numpy as jnp
from jax import lax
from jax.sharding import PartitionSpec as P

GROUP = 256


exact_product = lax.Precision.HIGHEST
epsilon = 1e-05


def causal_conv(inputs, seg_ids, kernel, offset):
    length = inputs.shape[0]
    summed = kernel[-1] * inputs + offset
    for shift_by in range(1, kernel.shape[0]):
        earlier = jnp.pad(inputs, ((shift_by, 0), (0, 0)))[:length]
        earlier_seg = jnp.pad(seg_ids, (shift_by, 0), constant_values=-1)[:length]
        summed = (
            summed
            + kernel[-1 - shift_by]
            * earlier
            * (earlier_seg == seg_ids).astype(jnp.float32)[:, None]
        )
    return summed


def scan_block(decays, carry, pieces):
    carry_state, last_seg = carry
    values, dt_vals, inputs_b, inputs_c, seg_ids = pieces
    log_sums = jnp.cumsum(dt_vals * decays[None, :], axis=0)
    positions = jnp.arange(seg_ids.shape[0])
    allowed = (seg_ids[:, None] == seg_ids[None, :]) & (positions[:, None] >= positions[None, :])
    log_gaps = jnp.where(allowed[:, :, None], log_sums[:, None, :] - log_sums[None, :, :], 0.0)
    weights = jnp.exp(log_gaps) * allowed[:, :, None].astype(jnp.float32)
    scores = jnp.dot(
        inputs_c, inputs_b.T, precision=exact_product, preferred_element_type=jnp.float32
    )
    mixing = weights * scores[:, :, None] * dt_vals[None, :, :]
    within = jnp.einsum("ijh,jhp->ihp", mixing, values, precision=exact_product)
    carried = (seg_ids == last_seg).astype(jnp.float32)
    across = jnp.einsum("in,hpn->ihp", inputs_c, carry_state, precision=exact_product)
    across = across * (jnp.exp(log_sums) * carried[:, None])[:, :, None]
    final_seg = seg_ids[-1]
    to_state = jnp.exp(log_sums[-1][None, :] - log_sums) * dt_vals
    to_state = to_state * (seg_ids == final_seg).astype(jnp.float32)[:, None]
    new_part = jnp.einsum("jh,jn,jhp->hpn", to_state, inputs_b, values, precision=exact_product)
    keep_state = (final_seg == last_seg).astype(jnp.float32)
    carry_state = new_part + carry_state * (jnp.exp(log_sums[-1]) * keep_state)[:, None, None]
    return ((carry_state, final_seg), within + across)


def run_ssd(values, dt_vals, decays, inputs_b, inputs_c, seg_ids, block_len):
    length, head_count, head_size = values.shape
    blocks = length // block_len
    state_dim = inputs_b.shape[1]
    pieces = (
        values.reshape(blocks, block_len, head_count, head_size),
        dt_vals.reshape(blocks, block_len, head_count),
        inputs_b.reshape(blocks, block_len, state_dim),
        inputs_c.reshape(blocks, block_len, state_dim),
        seg_ids.reshape(blocks, block_len),
    )
    initial = (jnp.zeros((head_count, head_size, state_dim), jnp.float32), jnp.array(-1, jnp.int32))
    ignored, outputs = lax.scan(jax.checkpoint(partial(scan_block, decays)), initial, pieces)
    return outputs.reshape(length, head_count, head_size)


def mix_one(constants, zx_rows, bc_rows, dt_rows, seg_ids):
    conv_x_weight, conv_bc_weight, conv_x_bias, conv_bc_bias, dt_bias, decays, skip_gain = constants
    length = zx_rows.shape[0]
    local_inner = conv_x_weight.shape[1]
    head_count = dt_bias.shape[0]
    gate_z = zx_rows[:, :local_inner]
    values = jax.nn.silu(causal_conv(zx_rows[:, local_inner:], seg_ids, conv_x_weight, conv_x_bias))
    values = values.reshape(length, head_count, local_inner // head_count)
    state_in = jax.nn.silu(causal_conv(bc_rows, seg_ids, conv_bc_weight, conv_bc_bias))
    state_dim = state_in.shape[1] // 2
    dt_vals = jax.nn.softplus(dt_rows + dt_bias)
    heads_out = run_ssd(
        values, dt_vals, decays, state_in[:, :state_dim], state_in[:, state_dim:], seg_ids, GROUP
    )
    heads_out = heads_out + skip_gain[None, :, None] * values
    return heads_out.reshape(length, local_inner) * jax.nn.silu(gate_z)


def pick_tables(one_hot, table):
    return jnp.tensordot(one_hot, table.astype(jnp.float32), axes=1, precision=exact_product)


def spread_tables(one_hot, per_seq):
    return jnp.tensordot(one_hot.T, per_seq, axes=1, precision=exact_product)


def shards(
    tokens,
    cotangent,
    doc_ids,
    adapter_pick,
    norm_gain,
    gate_x_weight,
    bc_weight,
    dt_weight,
    conv_x_weight,
    conv_bc_weight,
    conv_x_bias,
    conv_bc_bias,
    dt_bias,
    a_log,
    skip_gain,
    inner_gain,
    out_weight,
    in_down,
    in_up,
    out_down,
    out_up,
):
    gathered = (
        lax.all_gather(gate_x_weight, "dp", axis=0, tiled=True),
        lax.all_gather(bc_weight, "dp", axis=0, tiled=True),
        lax.all_gather(dt_weight, "dp", axis=0, tiled=True),
        lax.all_gather(out_weight, "dp", axis=1, tiled=True),
        lax.all_gather(in_down, "dp", axis=1, tiled=True),
        lax.all_gather(in_up, "dp", axis=4, tiled=True),
        lax.all_gather(out_down, "dp", axis=2, tiled=True),
        lax.all_gather(out_up, "dp", axis=2, tiled=True),
    )
    (
        zx_full,
        input_output_matrix,
        timestep_whole,
        output_whole,
        down_in_all,
        up_in_all,
        down_out_all,
        up_out_all,
    ) = gathered
    seq_count, own_len, model_width = tokens.shape
    tensor_size = lax.axis_size("tensor")
    local_inner = zx_full.shape[2]
    rank_size = down_in_all.shape[2]
    inner_total = local_inner * tensor_size
    adapter_count = down_in_all.shape[0]
    one_hot = (adapter_pick[:, None] == jnp.arange(adapter_count)[None, :]).astype(jnp.float32)
    own_start = lax.axis_index("tensor") * own_len
    down_projection_input = pick_tables(one_hot, down_in_all)
    up_in = pick_tables(one_hot, up_in_all).reshape(seq_count, rank_size, 2 * local_inner)
    down_out = pick_tables(one_hot, down_out_all).reshape(seq_count, local_inner, rank_size)
    up_projection_output = pick_tables(one_hot, up_out_all)
    tokens_wide = tokens.astype(jnp.float32)
    row_scale = lax.rsqrt(jnp.mean(tokens_wide * tokens_wide, axis=2, keepdims=True) + epsilon)
    normed_own = (tokens_wide * row_scale * norm_gain).astype(jnp.bfloat16)
    normed_rows = lax.all_gather(normed_own, "tensor", axis=1, tiled=True)
    rank_in = jnp.einsum(
        "vcm,vmi->vci",
        normed_rows,
        down_projection_input.astype(jnp.bfloat16),
        preferred_element_type=jnp.float32,
    )
    zx_proj = jnp.dot(
        normed_rows,
        zx_full.reshape(zx_full.shape[0], 2 * local_inner),
        preferred_element_type=jnp.float32,
    )
    zx_proj = zx_proj + jnp.einsum("slr,sre->sle", rank_in, up_in, precision=exact_product)
    bc_proj = jnp.dot(normed_rows, input_output_matrix, preferred_element_type=jnp.float32)
    dt_proj = jnp.dot(normed_rows, timestep_whole, preferred_element_type=jnp.float32)
    constants = (
        conv_x_weight,
        conv_bc_weight,
        conv_x_bias,
        conv_bc_bias,
        dt_bias,
        -jnp.exp(a_log),
        skip_gain,
    )

    def mixer(zx_in, bc_in, dt_in):
        return jax.vmap(partial(mix_one, constants))(zx_in, bc_in, dt_in, doc_ids)

    gated, pullback = jax.vjp(mixer, zx_proj, bc_proj, dt_proj)
    local_squares = jnp.sum(gated * gated, axis=2)
    total_squares = lax.psum(local_squares, "tensor")
    inner_scale = lax.rsqrt(total_squares / inner_total + epsilon)[:, :, None]
    normed_inner = gated * inner_scale * inner_gain
    rank_portion = jnp.einsum("sle,ser->slr", normed_inner, down_out, precision=exact_product)
    rank_output = lax.psum(rank_portion, "tensor")
    low_inner = normed_inner.astype(jnp.bfloat16)
    partial_results = jnp.dot(low_inner, output_whole, preferred_element_type=jnp.float32)
    partial_results = partial_results + jnp.einsum(
        "gao,got->gat", rank_portion, up_projection_output, precision=exact_product
    )
    mixed = (
        lax.psum_scatter(partial_results, "tensor", scatter_dimension=1, tiled=True) + tokens_wide
    )
    cotangent_whole = lax.all_gather(cotangent, "tensor", axis=1, tiled=True)
    g_rank_out = jnp.einsum(
        "izm,inm->izn",
        cotangent_whole,
        up_projection_output.astype(jnp.bfloat16),
        preferred_element_type=jnp.float32,
    )
    inner_gradient = jnp.einsum(
        "xom,rm->xor", cotangent_whole, output_whole, preferred_element_type=jnp.float32
    )
    inner_gradient = inner_gradient + jnp.einsum(
        "slr,ser->sle", g_rank_out, down_out, precision=exact_product
    )
    seq_out_up = jnp.einsum(
        "xqp,xqj->xpj",
        rank_output,
        cotangent_whole,
        precision=exact_product,
        preferred_element_type=jnp.float32,
    )
    seq_out_down = jnp.einsum("sle,slr->ser", normed_inner, g_rank_out, precision=exact_product)
    local_dot = jnp.sum(inner_gradient * inner_gain * gated, axis=2)
    total_dot = lax.psum(local_dot, "tensor")
    g_gated = (
        inner_gradient * inner_gain * inner_scale
        - gated * inner_scale**3 * (total_dot / inner_total)[:, :, None]
    )
    g_proj, g_bc, g_dt = pullback(g_gated)
    low_proj = g_proj.astype(jnp.bfloat16)
    reduced_timestep = g_dt.astype(jnp.bfloat16)
    wide_proj = low_proj.astype(jnp.float32)
    seq_in_up = jnp.einsum("slr,sle->sre", rank_in, wide_proj, precision=exact_product)
    g_rank_part = jnp.einsum("sle,sre->slr", wide_proj, up_in, precision=exact_product)
    rank_input_gradient = lax.psum(g_rank_part, "tensor")
    seq_in_down = jnp.einsum(
        "tmq,tmi->tqi",
        normed_rows,
        rank_input_gradient,
        precision=exact_product,
        preferred_element_type=jnp.float32,
    )
    summand_list = jnp.einsum(
        "qpb,cb->qpc",
        low_proj,
        zx_full.reshape(zx_full.shape[0], 2 * local_inner),
        preferred_element_type=jnp.float32,
    )
    summand_list = summand_list + jnp.einsum(
        "gwv,ov->gwo", reduced_timestep, timestep_whole, preferred_element_type=jnp.float32
    )
    normed_gradient, owned_input_output_gradient = (
        lax.psum_scatter(summand_list, "tensor", scatter_dimension=1, tiled=True),
        lax.psum_scatter(g_bc, "tensor", scatter_dimension=1, tiled=True),
    )
    owned_rank_input = lax.dynamic_slice_in_dim(rank_input_gradient, own_start, own_len, 1)
    normed_gradient = normed_gradient + jnp.einsum(
        "fby,py->fbp",
        owned_input_output_gradient.astype(jnp.bfloat16),
        input_output_matrix,
        preferred_element_type=jnp.float32,
    )
    normed_gradient = normed_gradient + jnp.einsum(
        "azj,awj->azw", owned_rank_input, down_projection_input, precision=exact_product
    )
    row_dot = jnp.sum(normed_gradient * norm_gain * tokens_wide, axis=2, keepdims=True)
    tokens_grad = (
        cotangent.astype(jnp.float32)
        + row_scale * norm_gain * normed_gradient
        - tokens_wide * row_scale**3 * row_dot / model_width
    )
    grad_in_down = spread_tables(one_hot, seq_in_down)
    grad_in_up = spread_tables(one_hot, seq_in_up).reshape(up_in_all.shape)
    grad_out_down = spread_tables(one_hot, seq_out_down).reshape(down_out_all.shape)
    grad_out_up = spread_tables(one_hot, seq_out_up)
    grad_in_down, grad_in_up, grad_out_down, grad_out_up = (
        lax.psum_scatter(grad_in_down, "dp", scatter_dimension=1, tiled=True),
        lax.psum_scatter(grad_in_up, "dp", scatter_dimension=4, tiled=True),
        lax.psum_scatter(grad_out_down, "dp", scatter_dimension=2, tiled=True),
        lax.psum_scatter(grad_out_up, "dp", scatter_dimension=2, tiled=True),
    )
    return (mixed, tokens_grad, grad_in_down, grad_in_up, grad_out_down, grad_out_up)


def solution(mesh):
    placed = (
        P("dp", "tensor", None),
        P("dp", "tensor", None),
        P("dp", None),
        P("dp"),
        P(),
        P("dp", None, "tensor"),
        P("dp", None),
        P("dp", "tensor"),
        P(None, "tensor"),
        P(),
        P("tensor"),
        P(),
        P("tensor"),
        P("tensor"),
        P("tensor"),
        P("tensor"),
        P("tensor", "dp"),
        P(None, "dp", None),
        P(None, None, None, "tensor", "dp"),
        P(None, "tensor", "dp", None),
        P(None, None, "dp"),
    )
    return jax.shard_map(
        shards,
        mesh=mesh,
        in_specs=placed,
        out_specs=(
            P("dp", "tensor", None),
            P("dp", "tensor", None),
            P(None, "dp", None),
            P(None, None, None, "tensor", "dp"),
            P(None, "tensor", "dp", None),
            P(None, None, "dp"),
        ),
        check_vma=False,
    )
```

profile of v0, /device:TPU:1, one launch (start us, length us, event | category | flops | bytes accessed | tf_op | source)
XLA Modules:
  0.0 1276.3 jit_solution(9781743509045451346)
XLA Ops:
  14.7 11.3 all_gather.33
  26.5 20.3 %all_gather.34 = bf16[8,16,2,8,64]{1,4,3,2,0:T(8,128)(2,1)S(1)} all-gather(bf16[8,16,2,8,8]{1,4,3,2,0:T(8,128)(2,1)S(1)} %copy-done.37), channel_id=1, replica_groups=mesh['dp'=8,'tensor'=4] {'dp'}, dimensions={4}, use_global_device_ids=true | all-gather | bytes 294912 | tf_op jit(solution)/shard_map/all_gather | solution.py:126
  48.7 9.9 all_gather.35
  58.7 7.8 all_gather.31
  67.1 11.7 all_gather.37
  78.8 8.5 all_gather.38
  93.7 34.1 %all-gather.5.cloned.1.call-done = bf16[1,2048,1024]{2,1,0:T(8,128)(2,1)} async-done(((bf16[1,512,1024]{2,1,0:T(8,128)(2,1)}), bf16[1,2048,1024]{2,1,0:T(8,128)(2,1)}) %all-gather.5.cloned.1.call-update) | async-done | bytes 4194320 | tf_op jit(solution)/shard_map/all_gather | solution.py:155
  137.5 7.2 add_bitcast_fusion.2
  153.5 7.0 reshape.1533
  160.5 6.8 copy.114
  181.0 144.5 %while.43 = (s32[]{:T(128)}, f32[1,8,64,128]{3,2,1,0:T(8,128)S(1)}, s32[1]{0:T(128)}, f32[8,1,256,8,64]{2,4,3,1,0:T(8,128)}, f32[8,1,8,64,128]{4,3,2,1,0:T(8,128...) while((s32[]{:T(128)}, f32[1,8,64,128]{3,2,1,0:T(8,128)S(1)}, ...), condition=%wide.region_4.5_spmd.clone, body=%wide.region_1.4_spmd.clone.sunk | while | flops 909849600 | bytes 5807563 | solution.py:67
  325.5 6.9 copy.151
  332.4 7.7 reshape.1530
  348.8 10.6 fusion.154
  359.4 12.5 all-reduce.21
  371.9 7.0 fusion.161
  379.0 13.0 %fusion.207 = (f32[1,2048,512]{2,1,0:T(8,128)}, f32[1,2048,512]{2,1,0:T(8,128)}, f32[512,2048]{0,1:T(8,128)}) fusion(f32[2048]{0:T(1024)S(1)} %bitcast.771, f32[1,2048,512]{2,1,0:T(8,128)S(1)} %copy-done.2, f32[2048]{0:T(1024)S(1)} %multiply_multiply_fusion.8, f32[2048,512]{1,0:T(8,128)} %get-tuple-element.762, f32[2048]{0:T(1024)S(1)} %bitcast.747, ...), kind=kLoop, calls=%fused_computation.294 | loop fusion | flops 25165824 | bytes 33591296 | tf_op jit(solution)/shard_map/transpose(jvp(vmap()))/mul | solution.py:86
  392.0 7.1 reshape.1531
  399.1 6.8 copy.125
  411.2 252.4 %while.44 = (s32[]{:T(128)}, f32[1,8,64,128]{3,2,1,0:T(8,128)S(1)}, f32[8,1,256,8,64]{2,4,3,1,0:T(8,128)}, f32[8,1,256,8]{2,3,1,0:T(8,128)}, f32[8,1,256,128]{3,...) while((s32[]{:T(128)}, f32[1,8,64,128]{3,2,1,0:T(8,128)S(1)}, ...), condition=%wide.region_22.23_spmd.clone, body=%wide.region_10.22_spmd.clone.sunk | while | flops 2126758912 | bytes 19179176 | solution.py:67
  663.6 7.0 copy.154
  670.6 7.5 reshape.1532
  703.5 9.0 add_bitcast_fusion.1
  718.1 7.9 fusion.152
  737.5 6.5 copy.129
  778.7 19.9 %reduce-scatter.12.cloned.1.call-done = f32[1,512,256]{2,1,0:T(8,128)} async-done(((f32[1,2048,256]{2,1,0:T(8,128)}), f32[1,512,256]{2,1,0:T(8,128)}) %reduce-scatter.12.cloned.1.call-update) | async-done | bytes 524304 | tf_op jit(solution)/shard_map/reduce_scatter | solution.py:250
  798.6 146.2 %reduce-scatter.10.cloned.1.call-done = f32[1,512,1024]{2,1,0:T(8,128)} async-done(((f32[1,2048,1024]{2,1,0:T(8,128)}), f32[1,512,1024]{2,1,0:T(8,128)}) %reduce-scatter.10.cloned.1.call-update) | async-done | bytes 2097168 | tf_op jit(solution)/shard_map/reduce_scatter | solution.py:249
  948.0 144.4 %reduce-scatter.8.cloned.1.call-done = f32[1,512,1024]{2,1,0:T(8,128)} async-done(((f32[1,2048,1024]{2,1,0:T(8,128)}), f32[1,512,1024]{2,1,0:T(8,128)}) %reduce-scatter.8.cloned.1.call-update) | async-done | bytes 2097168 | tf_op jit(solution)/shard_map/reduce_scatter | solution.py:196
  1097.1 41.3 %reduce-scatter.18.cloned.1.call-done = f32[8,8,8,16]{3,2,1,0:T(8,128)} async-done(((f32[8,8,64,16]{3,2,1,0:T(8,128)}), f32[8,8,8,16]{3,2,1,0:T(8,128)}) %reduce-scatter.18.cloned.1.call-update) | async-done | bytes 32784 | tf_op jit(solution)/shard_map/reduce_scatter | solution.py:275
  1138.4 55.5 %reduce-scatter.16.cloned.1.call-done = f32[8,16,2,8,8]{1,4,3,2,0:T(8,128)} async-done(((f32[8,16,2,8,64]{1,4,3,2,0:T(8,128)}), f32[8,16,2,8,8]{1,4,3,2,0:T(8,128)}) %reduce-scatter.16.cloned.1.call-update) | async-done | bytes 65552 | tf_op jit(solution)/shard_map/reduce_scatter | solution.py:274
  1193.9 37.3 %reduce-scatter.14.cloned.1.call-done = f32[8,128,16]{1,2,0:T(8,128)} async-done(((f32[8,1024,16]{1,2,0:T(8,128)}), f32[8,128,16]{1,2,0:T(8,128)}) %reduce-scatter.14.cloned.1.call-update) | async-done | bytes 65552 | tf_op jit(solution)/shard_map/reduce_scatter | solution.py:273
  1231.2 38.0 %reduce-scatter.20.cloned.1.call-done = f32[8,16,128]{2,1,0:T(8,128)} async-done(((f32[8,16,1024]{2,1,0:T(8,128)}), f32[8,16,128]{2,1,0:T(8,128)}) %reduce-scatter.20.cloned.1.call-update) | async-done | bytes 65552 | tf_op jit(solution)/shard_map/reduce_scatter | solution.py:276
  (888 shorter events, 522.3 us)
Async XLA Ops:
  7.2 83.0 %all-gather.7.cloned.1.call-start = ((), (), s32[]{:S(2)}) async-start(), calls=%async_computation.8 | async-start | bytes 2359296 | tf_op jit(solution)/shard_map/all_gather | solution.py:121
  7.9 119.9 %all-gather.5.cloned.1.call-start = ((), (), s32[]{:S(2)}) async-start(), calls=%async_computation.7 | async-start | bytes 5242880 | tf_op jit(solution)/shard_map/all_gather | solution.py:155
  12.7 327.5 %all-gather.11.cloned.1.call-start = ((), (), s32[]{:S(2)}) async-start(), calls=%async_computation.11 | async-start | bytes 5242880 | tf_op jit(solution)/shard_map/all_gather | solution.py:198
  13.4 65.4 %copy-start.55 = (bf16[8,16,128]{2,1,0:T(8,128)(2,1)S(1)}, bf16[8,16,128]{2,1,0:T(8,128)(2,1)}, u32[]{:S(2)}) copy-start(bf16[8,16,128]{2,1,0:T(8,128)(2,1)} %param.45) | copy-start | bytes 98308
  13.4 73.9 %copy-start.86 = (f32[8]{0:T(128)S(1)}, f32[8]{0:T(128)}, u32[]{:S(2)}) copy-start(f32[8]{0:T(128)} %param.39) | copy-start | bytes 100
  13.4 330.2 %all-gather.9.cloned.1.call-start = ((), (), s32[]{:S(2)}) async-start(), calls=%async_computation.9 | async-start | bytes 1179648 | tf_op jit(solution)/shard_map/all_gather | solution.py:124
  26.4 101.3 %copy-start.13 = (f32[1,1024,16]{2,1,0:T(8,128)}, f32[1,1024,16]{2,1,0:T(8,128)S(1)}, u32[]{:S(2)}) copy-start(f32[1,1024,16]{2,1,0:T(8,128)S(1)} %copy.139) | copy-start | bytes 196612
  48.6 122.2 %copy-start.40 = (f32[1,2048]{1,0:T(1,128)}, f32[1,2048]{1,0:T(1,128)S(1)}, u32[]{:S(2)}) copy-start(f32[1,2048]{1,0:T(1,128)S(1)} %get-tuple-element.749) | copy-start | bytes 24580
  48.6 122.2 %copy-start.42 = (f32[1,2048]{1,0:T(1,128)}, f32[1,2048]{1,0:T(1,128)S(1)}, u32[]{:S(2)}) copy-start(f32[1,2048]{1,0:T(1,128)S(1)} %get-tuple-element.750) | copy-start | bytes 24580
  48.6 122.2 %copy-start.44 = (f32[1,2048]{1,0:T(1,128)}, f32[1,2048]{1,0:T(1,128)S(1)}, u32[]{:S(2)}) copy-start(f32[1,2048]{1,0:T(1,128)S(1)} %get-tuple-element.751) | copy-start | bytes 24580
  48.7 99.4 %copy-start.58 = (f32[1,512]{1,0:T(1,128)}, f32[1,512]{1,0:T(1,128)S(1)}, u32[]{:S(2)}) copy-start(f32[1,512]{1,0:T(1,128)S(1)} %get-tuple-element.747) | copy-start | bytes 6148
  48.7 99.4 %copy-start.60 = (f32[1,512]{1,0:T(1,128)}, f32[1,512]{1,0:T(1,128)S(1)}, u32[]{:S(2)}) copy-start(f32[1,512]{1,0:T(1,128)S(1)} %get-tuple-element.748) | copy-start | bytes 6148
  48.7 99.4 %copy-start.64 = (f32[1,512]{1,0:T(1,128)}, f32[1,512]{1,0:T(1,128)S(1)}, u32[]{:S(2)}) copy-start(f32[1,512]{1,0:T(1,128)S(1)} %get-tuple-element.745) | copy-start | bytes 6148
  48.7 99.3 %copy-start.66 = (f32[1,512]{1,0:T(1,128)}, f32[1,512]{1,0:T(1,128)S(1)}, u32[]{:S(2)}) copy-start(f32[1,512]{1,0:T(1,128)S(1)} %get-tuple-element.746) | copy-start | bytes 6148
  58.6 108.7 %copy-start.18 = (bf16[1024,256]{1,0:T(8,128)(2,1)}, bf16[1024,256]{1,0:T(8,128)(2,1)S(1)}, u32[]{:S(2)}) copy-start(bf16[1024,256]{1,0:T(8,128)(2,1)S(1)} %all_gather.35) | copy-start | bytes 1572868
  58.7 112.2 %copy-start.71 = (f32[1,256]{1,0:T(1,128)}, f32[1,256]{1,0:T(1,128)S(1)}, u32[]{:S(2)}) copy-start(f32[1,256]{1,0:T(1,128)S(1)} %get-tuple-element.754) | copy-start | bytes 3076
  58.7 112.2 %copy-start.73 = (f32[1,256]{1,0:T(1,128)}, f32[1,256]{1,0:T(1,128)S(1)}, u32[]{:S(2)}) copy-start(f32[1,256]{1,0:T(1,128)S(1)} %get-tuple-element.755) | copy-start | bytes 3076
  58.7 112.2 %copy-start.75 = (f32[1,256]{1,0:T(1,128)}, f32[1,256]{1,0:T(1,128)S(1)}, u32[]{:S(2)}) copy-start(f32[1,256]{1,0:T(1,128)S(1)} %get-tuple-element.753) | copy-start | bytes 3076
  58.7 112.2 %copy-start.77 = (f32[1,256]{1,0:T(1,128)}, f32[1,256]{1,0:T(1,128)S(1)}, u32[]{:S(2)}) copy-start(f32[1,256]{1,0:T(1,128)S(1)} %get-tuple-element.752) | copy-start | bytes 3076
  66.5 108.6 %copy-start.46 = (bf16[1024,8]{0,1:T(8,128)(2,1)}, bf16[1024,8]{0,1:T(8,128)(2,1)S(1)}, u32[]{:S(2)}) copy-start(bf16[1024,8]{0,1:T(8,128)(2,1)S(1)} %all_gather.31) | copy-start | bytes 49156
  712.5 52.1 %all-reduce.25.cloned.1.call-start = ((), (), s32[]{:S(2)}) async-start(), calls=%async_computation.18 | async-start | bytes 524288 | tf_op jit(solution)/shard_map/psum | solution.py:231
  713.1 85.5 %reduce-scatter.12.cloned.1.call-start = ((), (), s32[]{:S(2)}) async-start(), calls=%async_computation.13 | async-start | bytes 2621440 | tf_op jit(solution)/shard_map/reduce_scatter | solution.py:250
  718.1 226.7 %reduce-scatter.10.cloned.1.call-start = ((), (), s32[]{:S(2)}) async-start(), calls=%async_computation.12 | async-start | bytes 10485760 | tf_op jit(solution)/shard_map/reduce_scatter | solution.py:249
  730.7 361.7 %reduce-scatter.8.cloned.1.call-start = ((), (), s32[]{:S(2)}) async-start(), calls=%async_computation.10 | async-start | bytes 10485760 | tf_op jit(solution)/shard_map/reduce_scatter | solution.py:196
  731.4 407.0 %reduce-scatter.18.cloned.1.call-start = ((), (), s32[]{:S(2)}) async-start(), calls=%async_computation.16 | async-start | bytes 2359296 | tf_op jit(solution)/shard_map/reduce_scatter | solution.py:275
  756.4 437.5 %reduce-scatter.16.cloned.1.call-start = ((), (), s32[]{:S(2)}) async-start(), calls=%async_computation.15 | async-start | bytes 4718592 | tf_op jit(solution)/shard_map/reduce_scatter | solution.py:274
  764.5 466.7 %reduce-scatter.14.cloned.1.call-start = ((), (), s32[]{:S(2)}) async-start(), calls=%async_computation.14 | async-start | bytes 589824 | tf_op jit(solution)/shard_map/reduce_scatter | solution.py:273
  769.5 175.3 %copy-start.8 = (bf16[1,512,1024]{2,1,0:T(8,128)(2,1)S(1)}, bf16[1,512,1024]{2,1,0:T(8,128)(2,1)}, u32[]{:S(2)}) copy-start(bf16[1,512,1024]{2,1,0:T(8,128)(2,1)} %param.25) | copy-start | bytes 3145732
  769.5 175.3 %copy-start.51 = (f32[1024]{0:T(1024)S(1)}, f32[1024]{0:T(1024)}, u32[]{:S(2)}) copy-start(f32[1024]{0:T(1024)} %param.29) | copy-start | bytes 12292
  769.5 499.7 %reduce-scatter.20.cloned.1.call-start = ((), (), s32[]{:S(2)}) async-start(), calls=%async_computation.17 | async-start | bytes 589824 | tf_op jit(solution)/shard_map/reduce_scatter | solution.py:276
  778.7 313.7 %copy-start.57 = (f32[512]{0:T(512)S(1)}, f32[512]{0:T(512)}, u32[]{:S(2)}) copy-start(f32[512]{0:T(512)} %copy-done.56) | copy-start | bytes 6148
  778.7 313.7 %copy-start.79 = (f32[512]{0:T(512)S(1)}, f32[512]{0:T(512)}, u32[]{:S(2)}) copy-start(f32[512]{0:T(512)} %get-tuple-element.756) | copy-start | bytes 6148
  (124 other events, 1113.3 us)
Sparse Core Ops, SparseCore 0:
  9.9 34.4 all-gather.6
  45.9 81.7 all-gather.4
  129.3 79.2 all-gather.10
  210.4 22.5 all-gather.8
  715.4 35.9 all-reduce.24
  753.7 44.8 reduce-scatter.11
  800.9 143.8 reduce-scatter.9
  947.1 145.2 reduce-scatter.7
  1096.2 42.0 reduce-scatter.17
  1142.5 51.3 reduce-scatter.15
  1197.6 33.6 reduce-scatter.13
  1235.0 34.1 reduce-scatter.19
where the time goes:
time: 1290 us; the launch traced here: 1280 us
  waiting for transfers between devices  520 us (40%)
  matrix products  282 us (22%)
  local copies, waits for them, and re-layouts  186 us (14%)
  other arithmetic  168 us (13%)
  blocking collectives  81.9 us (6%)
  loops' own time  21.4 us (2%)
  between operations  16.1 us (1%)
    reduce_scatter x1, waiting for transfers between devices, shards(): lax.psum_scatter(summand_list, 'tensor', scatter_dimension=1, tiled=True)  146 us
    reduce_scatter x1, waiting for transfers between devices, shards(): lax.psum_scatter(partial_results, 'tensor', scatter_dimension=1, tiled=True)  144 us
    dot_general x24, matrix products, scan_block(): within = jnp.einsum('ijh,jhp->ihp', mixing, values, precision=exact_product)  98.9 us
    reduce_scatter x1, waiting for transfers between devices, shards(): lax.psum_scatter(grad_in_up, 'dp', scatter_dimension=4, tiled=True)  55.5 us
    another operation x81, other arithmetic  54.3 us
    squeeze x48, local copies, waits for them, and re-layouts, run_ssd(): lax.scan(jax.checkpoint(partial(scan_block, decays)), initial, pieces)  42.2 us
    reduce_scatter x1, waiting for transfers between devices, shards(): lax.psum_scatter(grad_out_down, 'dp', scatter_dimension=2, tiled=True)  41.3 us
    reduce_scatter x1, waiting for transfers between devices, shards(): lax.psum_scatter(grad_out_up, 'dp', scatter_dimension=2, tiled=True)  38 us
  transfers between devices with their start and end apart: 12, of which 8 were waited for; matrix products, arithmetic and copies ran while one was open for 23% of the time, Pallas kernels for 0%

commit v1 on v0

v1 whole, which is shorter than its diff:
```python
import math

import jax
import jax.numpy as jnp
from jax import lax
from jax.experimental import pallas as pl
from jax.experimental.pallas import tpu as pltpu
from jax.sharding import PartitionSpec as P

epsilon = 1e-05
chunk = 128
lanes = 128
doc_most = 800
edge = 16
f32, bf16 = jnp.float32, jnp.bfloat16
exact = lax.Precision.HIGHEST
vmem_bytes = 48 * 1024 * 1024


def dot(a, b):
    return jnp.dot(a, b, preferred_element_type=f32)


def dot_nt(a, b):
    return lax.dot_general(a, b, (((1,), (1,)), ((), ())), preferred_element_type=f32)


def dot_tn(a, b):
    return lax.dot_general(a, b, (((0,), (0,)), ((), ())), preferred_element_type=f32)


def halves(x):
    high = x.astype(bf16)
    return high, (x - high.astype(f32)).astype(bf16)


def pieces(x, count):
    out = []
    for _ in range(count):
        part = lax.reduce_precision(x, 8, 7)
        out.append(part.astype(bf16))
        x = x - part
    return jnp.concatenate(out, axis=-1)


def dot2(x, w):
    high, low = halves(x)
    return dot(high, w) + dot(low, w)


def dot2_nt(x, w):
    high, low = halves(x)
    return dot_nt(high, w) + dot_nt(low, w)


def dot2_tn(x, w):
    high, low = halves(x)
    return dot_tn(high, w) + dot_tn(low, w)


def tile_lanes(m, width):
    return m if width == lanes else jnp.concatenate([m] * (width // lanes), axis=1)


def silu_parts(u):
    s = 1.0 / (1.0 + jnp.exp(-u))
    return u * s, s * (1.0 + u * (1.0 - s))


def weight_block(refs):
    out = []
    for own, other in ((refs[0], refs[1]), (refs[2], refs[3])):
        cols = own.shape[-1]
        out.append((own[...].reshape(-1, cols), other[...].reshape(-1, cols)))
    return out


def times_weight(left, refs, put):
    for j, (own, other) in enumerate(weight_block(refs)):
        k = own.shape[0]
        cols = own.shape[1]
        put(slice(j * cols, (j + 1) * cols), dot(left[:, :k], own) + dot(left[:, k : 2 * k], other))


def add_times_transposed(acc, low, refs):
    (own_a, other_a), (own_b, other_b) = weight_block(refs)
    k, cols = own_a.shape
    a, b = low[:, :cols], low[:, cols:]
    acc[:, :k] += dot_nt(a, own_a) + dot_nt(b, own_b)
    acc[:, k : 2 * k] += dot_nt(a, other_a) + dot_nt(b, other_b)


def bring_order(sel, source, target):
    for k in range(8):
        at = pl.multiple_of(sel[k] * lanes, lanes)
        target[:, k * lanes : (k + 1) * lanes] = source[:, pl.ds(at, lanes)]


def rows_of(c):
    return slice(c * chunk, (c + 1) * chunk)


def proj_kernel(sel, normed, own_a, oth_a, own_b, oth_b, ranks, a_up, params, masks, dt2, eo2, ex, b_t,
                u_out, sc_out, f_out, left, xs, moved):
    @pl.when(pl.program_id(0) == 0)
    def _():
        bring_order(sel, normed, left)

    def put(cols, value):
        xs[:, cols] = value + dot(ranks[...], a_up[:, cols])

    times_weight(left, (own_a, oth_a, own_b, oth_b), put)
    own, width = u_out.shape
    step = min(width, 256)
    for c in range(own // chunk):
        rows = rows_of(c)
        for n in range(width // step):
            cols = slice(n * step, (n + 1) * step)
            cur = xs[edge + c * chunk - 8 : edge + (c + 1) * chunk, cols]
            total = params[3:4, cols] * cur[8:] + params[4:5, cols]
            for k in range(1, 4):
                shifted = pltpu.roll(cur, k, 0)[8:]
                total = total + params[3 - k : 4 - k, cols] * (
                    shifted * tile_lanes(masks[k - 1, rows, :], step)
                )
            u_out[rows, cols] = total
            value = total / (1.0 + jnp.exp(-total))
            scaled = (dot(dt2[rows, :], ex[:, cols]) * value).astype(bf16)
            sc_out[rows, cols] = scaled
            moved[rows, cols] = (dot(eo2[rows, :], ex[:, cols]) * scaled.astype(f32)).astype(bf16)
    f_out[...] = dot(b_t[...], moved[...]).astype(bf16)


def pair_parts(lcol, cums_t, p):
    lc = lcol[:, p * 2 * lanes : (p + 1) * 2 * lanes]
    lr = jnp.concatenate([cums_t[2 * p : 2 * p + 1, :], cums_t[2 * p + 1 : 2 * p + 2, :]], axis=1)
    return jnp.exp2(jnp.minimum(lc - lr, 0.0))


def two_heads(v, head_size):
    lane = lax.broadcasted_iota(jnp.int32, v.shape, 1)
    zero = jnp.zeros_like(v)
    return jnp.concatenate([jnp.where(lane < head_size, v, zero), jnp.where(lane < head_size, zero, v)], 0)


def within_kernel(sc, cums3, cums_t, scores, exl, y_out):
    own, width = y_out.shape
    for c in range(own // chunk):
        rows = rows_of(c)
        lcol = dot(cums3[rows, :], exl[...])
        allowed = tile_lanes(scores[c], 2 * lanes)
        for p in range(width // lanes):
            e = pair_parts(lcol, cums_t[0, c], p)
            m = (e * allowed).astype(bf16)
            cols = slice(p * lanes, (p + 1) * lanes)
            y_out[rows, cols] = dot(m, two_heads(sc[rows, cols], lanes // 2))


def gate_kernel(sel, normed, own_a, oth_a, own_b, oth_b, ranks, a_up, params, yw, u, sc, s_in, ei2, eo2,
                keep, ex, b_t, in_c, y_out, z_out, gated_out, states, sumsq, left):
    @pl.when(pl.program_id(0) == 0)
    def _():
        bring_order(sel, normed, left)
        sumsq[...] = jnp.zeros_like(sumsq)

    def put(cols, value):
        z_out[:, cols] = value + dot(ranks[...], a_up[:, cols])

    times_weight(left, (own_a, oth_a, own_b, oth_b), put)
    own, width = y_out.shape
    step = min(width, 256)
    for n in range(width // step):
        cols = slice(n * step, (n + 1) * step)
        s = s_in[:, cols]
        for c in range(own // chunk):
            rows = rows_of(c)
            low_s = s.astype(bf16)
            states[c, :, cols] = low_s
            y = yw[rows, cols] + dot(ei2[rows, :], ex[:, cols]) * dot(in_c[rows, :], low_s)
            y_out[rows, cols] = y
            v, _ = silu_parts(u[rows, cols])
            g, _ = silu_parts(z_out[rows, cols])
            gated = (y + params[6:7, cols] * v) * g
            gated_out[rows, cols] = gated
            sq = gated * gated
            part = sq[:, :lanes]
            for i in range(1, step // lanes):
                part = part + sq[:, i * lanes : (i + 1) * lanes]
            sumsq[rows, :] += part
            moved = (dot(eo2[rows, :], ex[:, cols]) * sc[rows, cols].astype(f32)).astype(bf16)
            s = s * keep[c : c + 1, cols] + dot(b_t[:, rows], moved)


def row_scale_of(sumsq, inner):
    return lax.rsqrt(jnp.sum(sumsq, axis=1, keepdims=True) / inner + epsilon)


def out_kernel(sel, gated, own_a, oth_a, own_b, oth_b, params, sumsq, cot, tokens, b_up, b_down,
               gg_out, mixed, p_down, p_up, dots, acc, cots, g_rank, rank, low, *, inner):
    g = pl.program_id(0)

    @pl.when(g == 0)
    def _():
        bring_order(sel, cot, cots)
        g_rank[...] = dot_nt(cot[...], b_up[...])
        acc[...] = jnp.zeros_like(acc)
        rank[...] = jnp.zeros_like(rank)
        dots[...] = jnp.zeros_like(dots)

    own, width = gg_out.shape
    scale = row_scale_of(sumsq[...], inner)

    def put(cols, value):
        gg = (value + dot2(g_rank[...], b_down[:, cols])) * params[5:6, cols]
        gg_out[:, cols] = gg
        prod = gg * gated[:, cols]
        for i in range(prod.shape[1] // lanes):
            dots[...] += prod[:, i * lanes : (i + 1) * lanes]

    times_weight(cots, (own_a, oth_a, own_b, oth_b), put)
    normed_inner = gated[...] * scale * params[5:6, :]
    high, rest = halves(normed_inner)
    low[...] = high
    rank[...] += dot_nt(high, b_down[...]) + dot_nt(rest, b_down[...])
    r_high, r_low = halves(g_rank[...])
    p_down[...] = dot_tn(r_high, high) + dot_tn(r_low, high) + dot_tn(r_high, rest)
    add_times_transposed(acc, low, (own_a, oth_a, own_b, oth_b))

    @pl.when(g == pl.num_programs(0) - 1)
    def _():
        p_up[...] = dot2_tn(rank[...], cot[...])
        mixed[...] = tokens[...].astype(f32) + dot2(rank[...], b_up[...])
        for k in range(8):
            at = pl.ds(pl.multiple_of(sel[k] * lanes, lanes), lanes)
            mixed[:, at] += acc[:, k * lanes : (k + 1) * lanes]


def split_kernel(gg, gated, y, u, z, params, sumsq, dots, ei2, ex, c_t, gh_out, lz_out, g_out, moved, *, inner):
    own, width = gh_out.shape
    scale = row_scale_of(sumsq[...], inner)
    coef = scale * scale * scale * (jnp.sum(dots[...], axis=1, keepdims=True) / inner)
    step = min(width, 256)
    for c in range(own // chunk):
        rows = rows_of(c)
        sc, co = scale[rows], coef[rows]
        for n in range(width // step):
            cols = slice(n * step, (n + 1) * step)
            g_gated = gg[rows, cols] * sc - gated[rows, cols] * co
            v, _ = silu_parts(u[rows, cols])
            gate, slope = silu_parts(z[rows, cols])
            heads = y[rows, cols] + params[6:7, cols] * v
            lz_out[rows, cols] = (g_gated * heads * slope).astype(bf16)
            gh = g_gated * gate
            gh_out[rows, cols] = gh
            moved[rows, cols] = (dot(ei2[rows, :], ex[:, cols]) * gh).astype(bf16)
    g_out[...] = dot(c_t[...], moved[...]).astype(bf16)


def back_within_kernel(gh, y, sc, cums3, cums_t, scores, exl, red, dv_out, ds_out, ahead, prod):
    g = pl.program_id(0)

    @pl.when(g == 0)
    def _():
        ds_out[...] = jnp.zeros_like(ds_out)
        ahead[...] = jnp.zeros_like(ahead)

    own, width = dv_out.shape
    for c in range(own // chunk):
        rows = rows_of(c)
        lcol = dot(cums3[rows, :], exl[...])
        allowed = tile_lanes(scores[c], 2 * lanes)
        ds = jnp.zeros((chunk, lanes), f32)
        for p in range(width // lanes):
            cols = slice(p * lanes, (p + 1) * lanes)
            e = pair_parts(lcol, cums_t[0, c], p)
            m = (e * allowed).astype(bf16)
            v = sc[rows, cols]
            dy = gh[rows, cols]
            high, low = halves(dy)
            both = two_heads(v, lanes // 2)
            dm = dot_nt(high, both) + dot_nt(low, both)
            eds = e * dm
            ds = ds + eds[:, :lanes] + eds[:, lanes:]
            dvb = dot_tn(m, high) + dot_tn(m, low)
            lane = lax.broadcasted_iota(jnp.int32, (chunk, lanes), 1)
            dv = jnp.where(lane < lanes // 2, dvb[:chunk], dvb[chunk:])
            dv_out[rows, cols] = dv
            prod[:, cols] = y[rows, cols] * dy - v.astype(f32) * dv
        ds_out[c] += ds
        ahead[rows, :] += dot2(prod[...], red[...])


def back_state_kernel(gs_in, states, gh, sc, dv, u, params, in_b, in_c, b_t, c_t, dt2, ei2, eo2, keep, ex, red,
                      ds, ahead, allowed, u_bc, dt_slope, decays,
                      gu_out, gbc_out, ldt_out, db, dc, behind, direct, carry, prod):
    g = pl.program_id(0)

    @pl.when(g == 0)
    def _():
        for ref in (db, dc, behind, direct, carry):
            ref[...] = jnp.zeros_like(ref)

    own, width = gu_out.shape
    step = min(width, 256)
    blocks = own // chunk
    for n in range(width // step):
        cols = slice(n * step, (n + 1) * step)
        gs = gs_in[:, cols]
        for c in reversed(range(blocks)):
            rows = rows_of(c)
            low_g = gs.astype(bf16)
            kept = keep[c : c + 1, cols]
            low_s = states[c, :, cols]
            scaled = sc[rows, cols].astype(f32)
            eo = dot(eo2[rows, :], ex[:, cols])
            dvs = eo * dot(in_b[rows, :], low_g)
            db[rows, :] += dot_nt((eo * scaled).astype(bf16), low_g)
            dy = gh[rows, cols]
            moved = (dot(ei2[rows, :], ex[:, cols]) * dy).astype(bf16)
            dc[rows, :] += dot_nt(moved, low_s)
            carried = jnp.sum(low_s.astype(f32) * gs, axis=0, keepdims=True) * kept
            carry[c : c + 1, :] += dot2(jnp.broadcast_to(carried, (8, step)), red[cols, :])[:1]
            gs = gs * kept + dot(c_t[:, rows], moved)
            g_sc = dv[rows, cols] + dvs
            v, slope = silu_parts(u[rows, cols])
            behind[rows, :] += dot2(scaled * dvs, red[cols, :])
            direct[rows, :] += dot2(v * g_sc, red[cols, :])
            g_v = dot(dt2[rows, :], ex[:, cols]) * g_sc + params[6:7, cols] * dy
            gu_out[rows, cols] = g_v * slope

    @pl.when(g == pl.num_programs(0) - 1)
    def _():
        i = lax.broadcasted_iota(jnp.int32, (chunk, chunk), 0)
        j = lax.broadcasted_iota(jnp.int32, (chunk, chunk), 1)
        at_most = jnp.where(i <= j, 1.0, 0.0).astype(bf16)
        below = jnp.where(j < i, 1.0, 0.0).astype(bf16)
        for c in range(blocks):
            rows = rows_of(c)

            def sums(tri, x):
                high, mid = halves(x)
                low = (x - high.astype(f32) - mid.astype(f32)).astype(bf16)
                return dot(tri, high) + dot(tri, mid) + dot(tri, low)

            g_logs = sums(at_most, ahead[rows, :]) + sums(below, behind[rows, :]) + carry[c : c + 1, :]
            heads = dt_slope.shape[1]
            g_dt = (direct[rows, :] + g_logs * decays[...])[:, :heads] * dt_slope[rows, :]
            ldt_out[rows, :] = g_dt.astype(bf16)
            g_scores = ds[c] * allowed[c]
            low_ds = g_scores.astype(bf16)
            gc = dc[rows, :] + dot(low_ds, in_b[rows, :])
            gb = db[rows, :] + dot_tn(low_ds, in_c[rows, :])
            g_bc = jnp.concatenate([gb, gc], axis=1)
            _, slope = silu_parts(u_bc[rows, :])
            gbc_out[rows, :] = g_bc * slope


def in_z_kernel(sel, lz, own_a, oth_a, own_b, oth_b, a_up, rank_in, acc, g_rank, p_up):
    @pl.when(pl.program_id(0) == 0)
    def _():
        acc[...] = jnp.zeros_like(acc)
        g_rank[...] = jnp.zeros_like(g_rank)

    g_rank[...] += dot_nt(lz[...], a_up[...])
    p_up[...] = dot2_tn(rank_in[...], lz[...])
    add_times_transposed(acc, lz, (own_a, oth_a, own_b, oth_b))


def conv_back(cur, params, masks, rows, width):
    total = params[3:4, :] * cur[:chunk]
    for k in range(1, 4):
        shifted = pltpu.roll(cur, cur.shape[0] - k, 0)[:chunk]
        total = total + params[3 - k : 4 - k, :] * (shifted * tile_lanes(masks[k - 1, rows, :], width))
    return total


def in_x_kernel(sel, gu, halo, own_a, oth_a, own_b, oth_b, a_up, rank_in, params, masks, acc_z, g_rank_z,
                gbc, halo_bc, params_bc, w_bc, ldt, w_dt, a_down, normed, tokens, cot, norm_gain,
                grad, p_up, p_down, acc, g_rank, low, lbc, small):
    g = pl.program_id(0)

    @pl.when(g == 0)
    def _():
        acc[...] = acc_z[...]
        g_rank[...] = g_rank_z[...]

    own, width = gu.shape
    step = min(width, 256)
    blocks = own // chunk
    for c in range(blocks):
        rows = rows_of(c)
        for n in range(width // step):
            cols = slice(n * step, (n + 1) * step)
            if c < blocks - 1:
                cur = gu[c * chunk : (c + 1) * chunk + 8, cols]
            else:
                cur = jnp.concatenate([gu[rows, cols], halo[:, cols].astype(f32)[:8]], axis=0)
            low[rows, cols] = conv_back(cur, params[:, cols], masks, rows, step).astype(bf16)
    g_rank[...] += dot_nt(low[...], a_up[...])
    p_up[...] = dot2_tn(rank_in[...], low[...])
    add_times_transposed(acc, low, (own_a, oth_a, own_b, oth_b))

    @pl.when(g == pl.num_programs(0) - 1)
    def _():
        for c in range(blocks):
            rows = rows_of(c)
            if c < blocks - 1:
                cur = gbc[c * chunk : (c + 1) * chunk + 8, :]
            else:
                cur = jnp.concatenate([gbc[rows, :], halo_bc[...].astype(f32)[:8]], axis=0)
            lbc[rows, :] = conv_back(cur, params_bc[...], masks, rows, gbc.shape[1]).astype(bf16)
        small[...] = (
            dot_nt(lbc[...], w_bc[...]) + dot_nt(ldt[...], w_dt[...]) + dot2_nt(g_rank[...], a_down[...])
        )
        p_down[...] = dot2_tn(g_rank[...], normed[...])
        for k in range(8):
            at = pl.ds(pl.multiple_of(sel[k] * lanes, lanes), lanes)
            small[:, at] += acc[:, k * lanes : (k + 1) * lanes]
        for c in range(blocks):
            rows = rows_of(c)
            wide = tokens[rows, :].astype(f32)
            size = wide.shape[1]
            scale = lax.rsqrt(jnp.sum(wide * wide, axis=1, keepdims=True) / size + epsilon)
            g_norm = small[rows, :] * norm_gain[...]
            row_dot = jnp.sum(g_norm * wide, axis=1, keepdims=True)
            grad[rows, :] = (
                cot[rows, :].astype(f32) + g_norm * scale - wide * (scale * scale * scale * row_dot / size)
            )


def up(x):
    n = lax.axis_size("tensor")
    return lax.ppermute(x, "tensor", [(i, i + 1) for i in range(n - 1)])


def down(x):
    n = lax.axis_size("tensor")
    return lax.ppermute(x, "tensor", [(i + 1, i) for i in range(n - 1)])


def around_tensor(x):
    n = lax.axis_size("tensor")
    return jnp.stack(
        [x] + [lax.ppermute(x, "tensor", [(i, (i + s) % n) for i in range(n)]) for s in range(1, n)]
    )


def swap(x, bit):
    n = lax.axis_size("dp")
    return lax.ppermute(x, "dp", [(i, i ^ (1 << bit)) for i in range(n)])


def all_dp(x):
    n = lax.axis_size("dp")
    cur = x[None]
    for bit in range(n.bit_length() - 1):
        cur = jnp.concatenate([cur, swap(cur, bit)])
    return jnp.take(cur, jnp.arange(n) ^ lax.axis_index("dp"), axis=0)


def gather_weight(x):
    n, tp = lax.axis_size("dp"), lax.axis_size("tensor")
    rows, cols = x.shape
    half = cols // 2
    if rows % lanes == 0:
        placed = around_tensor(x)
        bits = list(range(1, n.bit_length() - 1))
        out = []
        for j in range(2):
            cur = placed[:, :, j * half : (j + 1) * half]
            cur = cur.reshape((1,) * len(bits) + cur.shape)
            for bit in bits if j == 0 else bits[::-1]:
                cur = jnp.concatenate([cur, swap(cur, bit)], axis=len(bits) - bit)
            cur = cur.reshape(-1, tp, rows, half)
            out += [cur, swap(cur, 0)]
        return out
    whole = lax.all_gather(x, ("dp", "tensor")).reshape(n, tp, rows, cols)
    whole = whole.transpose(1, 0, 2, 3).reshape(tp, 2, n * rows // 2, 2, half)
    return [whole[:, i, :, j][None] for j in range(2) for i in range(2)]


def shards(
    tokens,
    cotangent,
    doc_ids,
    adapter_pick,
    norm_gain,
    gate_x_weight,
    bc_weight,
    dt_weight,
    conv_x_weight,
    conv_bc_weight,
    conv_x_bias,
    conv_bc_bias,
    dt_bias,
    a_log,
    skip_gain,
    inner_gain,
    out_weight,
    in_down,
    in_up,
    out_down,
    out_up,
):
    dp_size, tp_size = lax.axis_size("dp"), lax.axis_size("tensor")
    both = ("dp", "tensor")
    seq_count, own, width = tokens.shape
    assert seq_count == 1 and width == 8 * lanes
    group = gate_x_weight.shape[2]
    inner = group * tp_size
    heads_part = dt_weight.shape[1]
    heads = heads_part * tp_size
    head_size = inner // heads
    assert head_size * 2 == lanes
    state = bc_weight.shape[1] // 2
    rank = in_down.shape[2]
    adapters = in_down.shape[0]
    hops = min(1 + (doc_most - 2) // own, tp_size - 1)
    blocks = own // chunk
    place, mine = lax.axis_index("tensor"), lax.axis_index("dp")

    d_rows = gate_x_weight.shape[0]
    if d_rows % lanes == 0:
        order = jnp.concatenate([jnp.arange(0, dp_size, 2), jnp.arange(1, dp_size, 2)]) ^ mine
        places = (place - jnp.arange(tp_size)) % tp_size
    else:
        order, places = jnp.arange(8), jnp.arange(tp_size)
    sel = jnp.concatenate([order, places]).astype(jnp.int32)

    wide_rows = jnp.concatenate(
        [conv_x_weight, conv_x_bias[None], inner_gain[None], jnp.repeat(skip_gain, head_size)[None],
         jnp.zeros((1, group), f32)]
    )
    flat = jnp.concatenate([wide_rows.reshape(-1), dt_bias, a_log, dt_weight.astype(f32).reshape(-1)])
    flat = around_tensor(flat)[(place - jnp.arange(tp_size)) % tp_size]
    cut0 = wide_rows.size
    params = flat[:, :cut0].reshape(tp_size, 8, group).transpose(1, 0, 2).reshape(8, inner)
    dt_shift = flat[:, cut0 : cut0 + heads_part].reshape(heads)
    decays = -jnp.exp(flat[:, cut0 + heads_part : cut0 + 2 * heads_part].reshape(heads))
    dt_cols = flat[:, cut0 + 2 * heads_part :].reshape(tp_size, d_rows, heads_part).transpose(1, 0, 2)
    small_w = jnp.concatenate([bc_weight, dt_cols.reshape(d_rows, heads).astype(bf16)], axis=1)
    small_w = all_dp(small_w).reshape(width, 2 * state + heads)
    w_bc, w_dt = small_w[:, : 2 * state], small_w[:, 2 * state :]

    picks = all_dp(adapter_pick).reshape(-1)
    one_hot = (picks[:, None] == jnp.arange(adapters)[None, :]).astype(bf16)
    sizes = [math.prod(t.shape[1:]) for t in (in_down, in_up, out_down, out_up)]
    tables = jnp.concatenate([t.reshape(adapters, -1) for t in (in_down, out_up, in_up, out_down)], 1)
    sent = jnp.dot(one_hot, tables, preferred_element_type=f32).astype(bf16)
    own_tables = lax.all_to_all(sent, "dp", 0, 0, tiled=True)
    cut = sizes[0] + sizes[3]
    a_down = own_tables[:, : sizes[0]].reshape(width, rank)
    b_up = own_tables[:, sizes[0] : cut].reshape(dp_size, rank, -1)
    b_up = b_up.transpose(1, 0, 2).reshape(rank, width)
    inner_tables = around_tensor(own_tables[:, cut:])[(place - jnp.arange(tp_size)) % tp_size]
    p_part = in_up.shape[4]
    a_up = inner_tables[:, :, : sizes[1]].reshape(tp_size, dp_size, rank, 2, heads_part, p_part)
    a_up = a_up.transpose(2, 3, 0, 4, 1, 5).reshape(rank, 2, inner)
    b_down = inner_tables[:, :, sizes[1] :].reshape(tp_size, dp_size, heads_part, p_part, rank)
    b_down = b_down.transpose(4, 0, 2, 1, 3).reshape(rank, inner)
    up_z, up_x = a_up[:, 0], a_up[:, 1]
    up_z2, up_x2 = jnp.concatenate([up_z, up_z]), jnp.concatenate([up_x, up_x])

    w_x = gather_weight(gate_x_weight[:, 1])
    w_z = gather_weight(gate_x_weight[:, 0])
    w_out = gather_weight(out_weight.T)

    docs = doc_ids[0]
    padded = jnp.concatenate([jnp.full((4,), -1, jnp.int32), docs, jnp.full((4,), -2, jnp.int32)])
    near = lax.dynamic_slice_in_dim(padded, place * own, own + 8)
    seg = near[4 : 4 + own]

    def masks_at(sign):
        rows = [(near[4 + sign * k : 4 + sign * k + own] == seg).astype(f32) for k in range(1, 4)]
        return jnp.broadcast_to(jnp.stack(rows)[:, :, None], (3, own, lanes))

    masks, masks_after = masks_at(-1), masks_at(1)
    before_seg, last_seg = near[3], near[own + 3]
    seg_c = seg.reshape(blocks, chunk)
    before_c = jnp.concatenate([before_seg[None], seg_c[:-1, -1]])
    last_c = seg_c[:, -1]
    at = jnp.arange(chunk)
    tril = (at[:, None] >= at[None, :]).astype(f32)
    allowed = (seg_c[:, :, None] == seg_c[:, None, :]).astype(f32) * tril

    wide = tokens[0].astype(f32)
    row_scale = lax.rsqrt(jnp.mean(wide * wide, axis=1, keepdims=True) + epsilon)
    normed = (wide * row_scale * norm_gain).astype(bf16)
    normed_ext = jnp.concatenate([up(normed[-edge:]), normed])
    rank_in = dot(normed_ext, a_down)
    ranks = pieces(rank_in, 2)
    bc_ext = dot(normed_ext, w_bc)
    dt_raw = dot(normed, w_dt) + dt_shift
    u_bc = conv_bc_weight[3] * bc_ext[edge:] + conv_bc_bias
    for k in range(1, 4):
        u_bc = u_bc + conv_bc_weight[3 - k] * (bc_ext[edge - k : edge - k + own] * masks[k - 1, :, :1])
    state_in = jax.nn.silu(u_bc)
    in_b, in_c = state_in[:, :state].astype(bf16), state_in[:, state:].astype(bf16)
    b_t, c_t = in_b.T, in_c.T
    scores = jnp.einsum(
        "cin,cjn->cij",
        in_c.reshape(blocks, chunk, state),
        in_b.reshape(blocks, chunk, state),
        preferred_element_type=f32,
    )
    scores = scores * allowed
    dt = jax.nn.softplus(dt_raw)
    dt_slope = jax.nn.sigmoid(dt_raw)

    logs = (dt * decays) * math.log2(math.e)
    cums = jnp.einsum("ij,cjh->cih", tril, logs.reshape(blocks, chunk, heads), precision=exact)
    ends = cums[:, -1]
    prior = jnp.concatenate([jnp.zeros((1, heads), f32), jnp.cumsum(ends, axis=0)[:-1]])
    whole_end = prior[-1] + ends[-1]
    cums_own = (cums + prior[:, None]).reshape(own, heads)
    e_in_own = jnp.exp2(cums_own) * (seg == before_seg).astype(f32)[:, None]
    e_out_own = jnp.exp2(whole_end - cums_own) * (seg == last_seg).astype(f32)[:, None]
    keep_own = jnp.exp2(whole_end) * (before_seg == last_seg).astype(f32)
    e_in = jnp.exp2(cums) * (seg_c == before_c[:, None]).astype(f32)[:, :, None]
    e_out = jnp.exp2(ends[:, None] - cums) * (seg_c == last_c[:, None]).astype(f32)[:, :, None]
    keep = jnp.exp2(ends) * (before_c == last_c).astype(f32)[:, None]
    keep = jnp.repeat(keep, head_size, axis=1)
    keep_row = jnp.repeat(keep_own, head_size)[None]
    dt2, ei_own2, eo_own2 = pieces(dt, 2), pieces(e_in_own, 2), pieces(e_out_own, 2)
    ei2, eo2 = pieces(e_in.reshape(own, heads), 2), pieces(e_out.reshape(own, heads), 2)
    cums3 = pieces(cums.reshape(own, heads), 3)
    cums_t = cums.reshape(blocks, chunk, tp_size, heads_part).transpose(2, 0, 3, 1)

    def spread(width_each, copies):
        head = jnp.arange(heads)[:, None]
        cols = jnp.arange(heads * width_each)[None, :] // width_each
        return jnp.tile((head == cols).astype(bf16), (copies, 1))

    ex, exl = spread(head_size, 2), spread(lanes, 3)
    red = (jnp.arange(inner)[:, None] // head_size == jnp.arange(lanes)[None, :]).astype(bf16)

    def full(*shape):
        return pl.BlockSpec(shape, lambda g, *s: (0,) * len(shape))

    def cols(rows, size=group):
        return pl.BlockSpec((rows, size), lambda g, *s: (0, g))

    def weight(w):
        q, _, rows, half = w.shape
        return pl.BlockSpec((q, 1, rows, half), lambda g, s: (0, s[8 + g], 0, 0))

    def call(kernel, out, in_specs, out_specs, scratch, prefetch, flops, moved):
        return pl.pallas_call(
            kernel,
            out_shape=[jax.ShapeDtypeStruct(s, d) for s, d in out],
            grid_spec=pltpu.PrefetchScalarGridSpec(
                num_scalar_prefetch=prefetch,
                grid=(tp_size,),
                in_specs=in_specs,
                out_specs=out_specs,
                scratch_shapes=scratch,
            ),
            compiler_params=pltpu.CompilerParams(
                dimension_semantics=("arbitrary",), vmem_limit_bytes=vmem_bytes
            ),
            cost_estimate=pl.CostEstimate(flops=flops, bytes_accessed=moved, transcendentals=0),
        )

    big = (own, inner)
    ext = own + edge
    mat = 2 * own * width * inner
    mega = 1 << 20
    chunk_rows = pl.BlockSpec((1, blocks, heads_part, chunk), lambda g, *s: (g, 0, 0, 0))
    w_specs = [weight(w) for w in w_x]
    p_spec = cols(8)
    u, scaled, sent_state = call(
        proj_kernel,
        [(big, f32), (big, bf16), ((state, inner), bf16)],
        [full(ext, width)] + w_specs
        + [full(ext, 2 * rank), cols(2 * rank), p_spec, full(3, own, lanes), full(own, 2 * heads),
           full(own, 2 * heads), cols(2 * heads), full(state, own)],
        [cols(own), cols(own), cols(state)],
        [pltpu.VMEM((ext, width), bf16), pltpu.VMEM((ext, group), f32), pltpu.VMEM((own, group), bf16)],
        1, mat, 12 * mega,
    )(sel, normed_ext, *w_x, ranks, up_x2, params, masks, dt2, eo_own2, ex, b_t)

    def pass_on(x, step):
        moving, total = x, jnp.zeros(x.shape, f32)
        for hop in range(hops):
            moving = step(moving)
            total = total + moving.astype(f32)
            if hop < hops - 1:
                moving = (moving.astype(f32) * keep_row).astype(bf16)
        return total

    state_first = pass_on(sent_state, up)

    within_specs = [cols(own), full(own, 3 * heads), chunk_rows, full(blocks, chunk, chunk),
                    cols(3 * heads, heads_part * lanes)]
    (y_within,) = call(
        within_kernel, [(big, f32)], within_specs, [cols(own)], [], 0, mat, 6 * mega
    )(scaled, cums3, cums_t, scores, exl)

    y, z, gated, states, sumsq = call(
        gate_kernel,
        [(big, f32), (big, f32), (big, f32), ((blocks, state, inner), bf16), ((own, lanes), f32)],
        [full(own, width)] + w_specs
        + [full(own, 2 * rank), cols(2 * rank), p_spec, cols(own), cols(own), cols(own), cols(state),
           full(own, 2 * heads), full(own, 2 * heads), cols(blocks), cols(2 * heads), full(state, own),
           full(own, state)],
        [cols(own), cols(own), cols(own),
         pl.BlockSpec((blocks, state, group), lambda g, *s: (0, 0, g)), full(own, lanes)],
        [pltpu.VMEM((own, width), bf16)],
        1, mat, 24 * mega,
    )(sel, normed, *w_z, ranks[edge:], up_z2, params, y_within, u, scaled, state_first, ei2, eo2, keep, ex,
      b_t, in_c)

    def with_inner(kernel):
        def body(*refs):
            return kernel(*refs, inner=inner)

        return body

    cot, tok = cotangent[0], tokens[0]
    gg, mixed, p_out_down, p_out_up, dots = call(
        with_inner(out_kernel),
        [(big, f32), ((own, width), f32), ((rank, inner), f32), ((rank, width), f32), ((own, lanes), f32)],
        [cols(own)] + w_specs
        + [p_spec, full(own, lanes), full(own, width), full(own, width), full(rank, width), cols(rank)],
        [cols(own), full(own, width), cols(rank), full(rank, width), full(own, lanes)],
        [pltpu.VMEM((own, width), f32), pltpu.VMEM((own, width), bf16), pltpu.VMEM((own, rank), f32),
         pltpu.VMEM((own, rank), f32), pltpu.VMEM((own, group), bf16)],
        1, 2 * mat, 14 * mega,
    )(sel, gated, *w_out, params, sumsq, cot, tok, b_up, b_down)

    g_heads, low_z, sent_grad = call(
        with_inner(split_kernel),
        [(big, f32), (big, bf16), ((state, inner), bf16)],
        [cols(own)] * 5
        + [p_spec, full(own, lanes), full(own, lanes), full(own, 2 * heads), cols(2 * heads), full(state, own)],
        [cols(own), cols(own), cols(state)],
        [pltpu.VMEM((own, group), bf16)],
        0, mat // 8, 28 * mega,
    )(gg, gated, y, u, z, params, sumsq, dots, ei_own2, ex, c_t)
    g_state_last = pass_on(sent_grad, down)

    d_within, d_scores, ahead = call(
        back_within_kernel,
        [(big, f32), ((blocks, chunk, chunk), f32), ((own, lanes), f32)],
        [cols(own), cols(own)] + within_specs + [pl.BlockSpec((group, lanes), lambda g, *s: (g, 0))],
        [cols(own), full(blocks, chunk, chunk), full(own, lanes)],
        [pltpu.VMEM((chunk, group), f32)],
        0, 2 * mat, 14 * mega,
    )(g_heads, y, scaled, cums3, cums_t, scores, exl, red)

    rank_own = rank_in[edge:]
    acc_z, g_rank_z, p_up_z = call(
        in_z_kernel,
        [((own, width), f32), ((own, rank), f32), ((rank, inner), f32)],
        [cols(own)] + w_specs + [cols(rank), full(own, rank)],
        [full(own, width), full(own, rank), cols(rank)],
        [],
        1, mat, 8 * mega,
    )(sel, low_z, *w_z, up_z, rank_own)

    decay_row = jnp.pad(decays, (0, lanes - heads))[None]
    g_u, g_u_bc, low_dt = call(
        back_state_kernel,
        [(big, f32), ((own, 2 * state), f32), ((own, heads), bf16)],
        [cols(state), pl.BlockSpec((blocks, state, group), lambda g, *s: (0, 0, g)), cols(own), cols(own),
         cols(own), cols(own), p_spec, full(own, state), full(own, state), full(state, own), full(state, own),
         full(own, 2 * heads), full(own, 2 * heads), full(own, 2 * heads), cols(blocks), cols(2 * heads),
         pl.BlockSpec((group, lanes), lambda g, *s: (g, 0)), full(blocks, chunk, chunk), full(own, lanes),
         full(blocks, chunk, chunk), full(own, 2 * state), full(own, heads), full(1, lanes)],
        [cols(own), full(own, 2 * state), full(own, heads)],
        [pltpu.VMEM((own, state), f32), pltpu.VMEM((own, state), f32), pltpu.VMEM((own, lanes), f32),
         pltpu.VMEM((own, lanes), f32), pltpu.VMEM((8, lanes), f32), pltpu.VMEM((8, lanes), f32)],
        0, mat, 24 * mega,
    )(g_state_last, states, g_heads, scaled, d_within, u, params, in_b, in_c, b_t, c_t, dt2, ei2, eo2, keep,
      ex, red, d_scores, ahead, allowed, u_bc, dt_slope, decay_row)

    halo = down(jnp.concatenate([g_u[:edge], g_u_bc[:edge]], axis=1).astype(bf16))
    params_bc = jnp.concatenate([conv_bc_weight, jnp.zeros((4, 2 * state), f32)])
    tokens_grad, p_up_x, p_in_down = call(
        in_x_kernel,
        [((own, width), f32), ((rank, inner), f32), ((rank, width), f32)],
        [cols(own), cols(edge)] + w_specs
        + [cols(rank), full(own, rank), p_spec, full(3, own, lanes), full(own, width), full(own, rank),
           full(own, 2 * state), full(edge, 2 * state), full(8, 2 * state), full(width, 2 * state),
           full(own, heads), full(width, heads), full(width, rank), full(own, width), full(own, width),
           full(own, width), full(1, width)],
        [full(own, width), cols(rank), full(rank, width)],
        [pltpu.VMEM((own, width), f32), pltpu.VMEM((own, rank), f32), pltpu.VMEM((own, group), bf16),
         pltpu.VMEM((own, 2 * state), bf16), pltpu.VMEM((own, width), f32)],
        1, mat, 14 * mega,
    )(sel, g_u, halo[:, :inner], *w_x, up_x, rank_own, params, masks_after, acc_z, g_rank_z, g_u_bc,
      halo[:, inner:], params_bc, w_bc, low_dt, w_dt, a_down, normed, tok, cot, norm_gain[None])

    def deliver(parts):
        parts = jnp.concatenate(parts, axis=2).astype(bf16).reshape(dp_size * tp_size, -1)
        arrived = lax.all_to_all(parts, both, 0, 0, tiled=True)
        arrived = arrived.reshape(dp_size, tp_size, -1).astype(f32).sum(1)
        return jnp.dot(one_hot.astype(f32).T, arrived, precision=exact)

    def by_width(part):
        part = part.reshape(rank, dp_size, 1, -1).transpose(1, 2, 0, 3)
        return jnp.broadcast_to(part, (dp_size, tp_size) + part.shape[2:]).reshape(dp_size, tp_size, -1)

    def by_inner(part):
        part = part.reshape(rank, -1, tp_size, heads_part, dp_size, p_part)
        return part.transpose(4, 2, 0, 1, 3, 5).reshape(dp_size, tp_size, -1)

    out_grads = deliver([by_width(p_out_up), by_inner(p_out_down)])
    in_grads = deliver([by_width(p_in_down), by_inner(jnp.stack([p_up_z, p_up_x], axis=1))])
    grad_out_up = out_grads[:, : sizes[3]].reshape(out_up.shape)
    grad_out_down = out_grads[:, sizes[3] :].reshape(adapters, rank, heads_part, p_part).transpose(0, 2, 3, 1)
    grad_in_down = in_grads[:, : sizes[0]].reshape(adapters, rank, d_rows).transpose(0, 2, 1)
    grad_in_up = in_grads[:, sizes[0] :].reshape(in_up.shape)
    return (mixed[None], tokens_grad[None], grad_in_down, grad_in_up, grad_out_down, grad_out_up)


def solution(mesh):
    placed = (
        P("dp", "tensor", None),
        P("dp", "tensor", None),
        P("dp", None),
        P("dp"),
        P(),
        P("dp", None, "tensor"),
        P("dp", None),
        P("dp", "tensor"),
        P(None, "tensor"),
        P(),
        P("tensor"),
        P(),
        P("tensor"),
        P("tensor"),
        P("tensor"),
        P("tensor"),
        P("tensor", "dp"),
        P(None, "dp", None),
        P(None, None, None, "tensor", "dp"),
        P(None, "tensor", "dp", None),
        P(None, None, "dp"),
    )
    return jax.shard_map(
        shards,
        mesh=mesh,
        in_specs=placed,
        out_specs=(
            P("dp", "tensor", None),
            P("dp", "tensor", None),
            P(None, "dp", None),
            P(None, None, None, "tensor", "dp"),
            P(None, "tensor", "dp", None),
            P(None, None, "dp"),
        ),
        check_vma=False,
    )
```

time: 1290 us -> 405 us (0.31)
  waiting for transfers between devices: 520 us -> 30.3 us
  matrix products: 282 us -> 5.64 us
  Pallas kernels: 0 us -> 108 us
  other arithmetic: 168 us -> 73.1 us
  local copies, waits for them, and re-layouts: 186 us -> 92.7 us
  blocking collectives: 81.9 us -> 0 us
  starting transfers between devices: 0.7 us -> 81.5 us
  loops' own time: 21.4 us -> 0 us
    reduce_scatter x7 -> x0, waiting for transfers between devices: 483 us -> none  [the longest x1 146 us: shards(): lax.psum_scatter(summand_list, 'tensor', scatter_dimension=1, tiled=True)]
    dot_general x135 -> x8, matrix products: 282 us -> 5.64 us  [the longest x3 2.81 us: dot(): return jnp.dot(a, b, preferred_element_type=f32)]
    pallas_call x0 -> x9, Pallas kernels: none -> 108 us  [the longest x1 15.4 us: shards(): call(with_inner(out_kernel), [(big, f32), ((own, width), f32), ((rank, in...]
    all_gather x6 -> x0, blocking collectives: 69.5 us -> none  [the longest x1 20.3 us: shards(): lax.all_gather(in_up, 'dp', axis=4, tiled=True)]
    ppermute x0 -> x45, starting transfers between devices: none -> 60 us  [the longest x24 28.2 us: swap(): return lax.ppermute(x, 'dp', [(i, i ^ 1 << bit) for i in range(n)])]
    another operation x89 -> x12, other arithmetic: 54.5 us -> 5.33 us  [the longest x5 2.2 us: around_tensor(): jnp.stack([x] + [lax.ppermute(x, 'tensor', [(i, (i + s) % n) for i in ran...]
    mul x64 -> x6, other arithmetic: 50.6 us -> 4.92 us  [the longest x2 2.08 us: shards(): keep = jnp.exp2(ends) * (before_c == last_c).astype(f32)[:, None]]
    squeeze x48 -> x0, local copies, waits for them, and re-layouts: 42.2 us -> none  [run_ssd(): lax.scan(jax.checkpoint(partial(scan_block, decays)), initial, pieces)]
  transfers between devices with their start and end apart: 12 -> 48, of which waited for: 8 -> 9; matrix products, arithmetic and copies ran while one was open for 23% -> 35% of each run, Pallas kernels for 0% -> 17%
where the time goes in v1:
time: 405 us; the launch traced here: 397 us
  Pallas kernels  108 us (27%)
  local copies, waits for them, and re-layouts  92.7 us (23%)
  starting transfers between devices  81.5 us (20%)
  other arithmetic  73.1 us (18%)
  waiting for transfers between devices  30.3 us (7%)
  matrix products  5.64 us (1%)
  between operations  5.08 us (1%)
    ppermute x24, starting transfers between devices, swap(): return lax.ppermute(x, 'dp', [(i, i ^ 1 << bit) for i in range(n)])  28.2 us
    unnamed x275, local copies, waits for them, and re-layouts  25.4 us
    concatenate x12, other arithmetic, gather_weight(): cur = jnp.concatenate([cur, swap(cur, bit)], axis=len(bits) - bit)  19.5 us
    ppermute x15, starting transfers between devices, around_tensor(): lax.ppermute(x, 'tensor', [(i, (i + s) % n) for i in range(n)])  19.2 us
    pallas_call x1, Pallas kernels, shards(): call(with_inner(out_kernel), [(big, f32), ((own, width), f32), ((rank, in...  15.4 us
    all_to_all x2, starting transfers between devices, deliver(): arrived = lax.all_to_all(parts, both, 0, 0, tiled=True)  15.2 us
    pallas_call x1, Pallas kernels, shards(): call(gate_kernel, [(big, f32), (big, f32), (big, f32), ((blocks, state, i...  15.1 us
    pallas_call x1, Pallas kernels, shards(): call(back_state_kernel, [(big, f32), ((own, 2 * state), f32), ((own, head...  14.5 us
  transfers between devices with their start and end apart: 48, of which 9 were waited for; matrix products, arithmetic and copies ran while one was open for 35% of the time, Pallas kernels for 17%

profile of v1, /device:TPU:1, one launch (start us, length us, event | category | flops | bytes accessed | tf_op | source)
XLA Modules:
  0.0 396.8 jit_solution(4060522733377240604)
XLA Ops:
  2.3 4.2 %collective-permute-start.2 = (bf16[128,512]{1,0:T(8,128)(2,1)S(1)}, bf16[128,512]{1,0:T(8,128)(2,1)S(1)}, u32[]{:S(2)}, u32[]{:S(2)}) collective-permute-start(bf16[128,512]{1,0:T(8,128)(2,1)S(1)} %bitcast.289), channel_id=1, source_target_pairs={{0,3},{1,0},{2,1},{3,2},{4,7},{5,4},{6,5},{7,6},{8,11},{9,8},{10,9... | collective-permute-start | bytes 393224 | tf_op jit(solution)/shard_map/ppermute | solution.py:444
  42.1 6.3 %all-to-all-start = ((bf16[8,2,3584]{2,1,0:T(2,128)(2,1)}), bf16[8,2,3584]{2,1,0:T(2,128)(2,1)S(1)}, u32[]{:S(2)}, u32[]{:S(2)}) async-start(bf16[8,2,3584]{2,1,0:T(2,128)(2,1)} %reshape.693), calls=%async_computation | async-start | bytes 229376 | tf_op jit(solution)/shard_map/all_to_all | solution.py:550
  50.4 2.7 collective-permute-start.21
  68.4 2.6 collective-permute-start.29
  71.0 3.0 collective-permute-start.15
  76.0 5.9 %collective-permute-done.34 = bf16[128,512]{0,1:T(8,128)(2,1)S(1)} collective-permute-done((bf16[128,512]{0,1:T(8,128)(2,1)S(1)}, bf16[128,512]{0,1:T(8,128)(2,1)S(1)}, u32[]{:S(2)}, u32[]{:S(2)}) %collective-permute-start.34) | collective-permute-done | bytes 131104 | tf_op jit(solution)/shard_map/ppermute | solution.py:444
  90.8 3.4 reshape.605
  130.8 8.6 %collective-permute-done.23 = bf16[1,2,4,128,256]{4,3,2,1,0:T(8,128)(2,1)} collective-permute-done((bf16[1,2,4,128,256]{4,3,2,1,0:T(8,128)(2,1)}, bf16[1,2,4,128,256]{4,3,2,1,0:T(8,128)(2,1)}, u32[]{:S(2)}, u32[]{:S(2)}) %collective-permute-start.23) | collective-permute-done | bytes 524320 | tf_op jit(solution)/shard_map/ppermute | solution.py:450
  140.7 6.6 %collective-permute-start.24 = (bf16[4,4,128,256]{3,2,1,0:T(8,128)(2,1)S(1)}, bf16[4,4,128,256]{3,2,1,0:T(8,128)(2,1)}, u32[]{:S(2)}, u32[]{:S(2)}) collective-permute-start(bf16[4,4,128,256]{3,2,1,0:T(8,128)(2,1)S(1)} %bitcast.250), channel_id=1, source_target_pairs={{0,4},{4,0},{8,12},{12,8},{16,20},{20,16},{24,28},{28,24},{1,5},{5... | collective-permute-start | bytes 3145736 | tf_op jit(solution)/shard_map/ppermute | solution.py:450
  164.0 11.8 %shard_map.244 = (f32[512,2048]{1,0:T(8,128)}, bf16[512,2048]{1,0:T(8,128)(2,1)}, bf16[128,2048]{1,0:T(8,128)(2,1)}) custom-call(s32[12]{0:T(128)S(1)} %pad_add_fusion.sel.refs_0_, bf16[528,1024]{1,0:T(8,128)(2,1)} %copy-done.63, bf16[4,4,128,256]{3,2,1,0:T(8,128)(2,1)S(1)} %bitcast.251, bf16[4,4,128,256]{3,2,1,0:T(8,128)(2,1)} %collective-permute-done.24.oth_a, ...), custom_call_target="tpu_custom_call" | custom-call | flops 2147483648 | bytes 12582912 | tf_op jit(solution)/shard_map/pallas_call | solution.py:671
  178.1 2.4 pad_maximum_fusion.1
  186.2 2.5 collective-permute-done.31
  190.3 5.0 %collective-permute-start.32 = (bf16[128,2048]{1,0:T(8,128)(2,1)}, bf16[128,2048]{1,0:T(8,128)(2,1)}, u32[]{:S(2)}, u32[]{:S(2)}) collective-permute-start(bf16[128,2048]{1,0:T(8,128)(2,1)} %fusion.4), channel_id=1, source_target_pairs={{0,1},{1,2},{2,3},{4,5},{5,6},{6,7},{8,9},{9,10},{10,11},{12,13},{... | collective-permute-start | bytes 1572872 | tf_op jit(solution)/shard_map/ppermute | solution.py:433
  197.4 2.4 copy.282
  212.8 5.5 %shard_map.245.yw = f32[512,2048]{1,0:T(8,128)} custom-call(bf16[512,2048]{1,0:T(8,128)(2,1)S(1)} %copy-done.1, bf16[512,96]{1,0:T(8,128)(2,1)S(1)} %copy-done.52, f32[4,4,8,128]{3,2,1,0:T(8,128)S(1)} %copy-done.56, f32[4,128,128]{2,1,0:T(8,128)S(1)} %copy-done.47, bf16[96,4096]{1,0:T(8,128)(2,1)S(1)} %bitcast.268), custom_call_target="tpu_custom_call" | custom-call | flops 2147483648 | bytes 6291456 | tf_op jit(solution)/shard_map/pallas_call | solution.py:695
  220.8 15.1 %shard_map.246 = (f32[512,2048]{1,0:T(8,128)}, f32[512,2048]{1,0:T(8,128)}, f32[512,2048]{1,0:T(8,128)}, bf16[4,128,2048]{2,1,0:T(8,128)(2,1)}, f32[512,128]{1,0:T(8,128)S(1)}) custom-call(s32[12]{0:T(128)S(1)} %pad_add_fusion.sel.refs_0_, bf16[512,1024]{1,0:T(8,128)(2,1)S(1)} %fusion.3.normed, bf16[4,4,128,256]{3,2,1,0:T(8,128)(2,1)} %bitcast.7.own_a, ...), custom_call_target="tpu_custom_call" | custom-call | flops 2147483648 | bytes 25165824 | tf_op jit(solution)/shard_map/pallas_call | solution.py:699
  236.0 15.4 %shard_map.247 = (f32[512,2048]{1,0:T(8,128)}, f32[512,1024]{1,0:T(8,128)}, f32[16,2048]{1,0:T(8,128)S(1)}, f32[16,1024]{1,0:T(8,128)S(1)}, f32[512,128]{1,0:T(8,128)S(1)}) custom-call(s32[12]{0:T(128)S(1)} %pad_add_fusion.sel.refs_0_, f32[512,2048]{1,0:T(8,128)} %get-tuple-element.37.refs_1_, bf16[4,4,128,256]{3,2,1,0:T(8,128)(2,1)} %bitcast.76.refs_2_, ...), custom_call_target="tpu_custom_call" | custom-call | flops 4294967296 | bytes 14680064 | tf_op jit(solution)/shard_map/pallas_call | solution.py:720
  251.5 10.8 %shard_map.248 = (f32[512,2048]{1,0:T(8,128)}, bf16[512,2048]{1,0:T(8,128)(2,1)S(1)}, bf16[128,2048]{1,0:T(8,128)(2,1)}) custom-call(f32[512,2048]{1,0:T(8,128)} %get-tuple-element.40.refs_0_, f32[512,2048]{1,0:T(8,128)} %get-tuple-element.37.refs_1_, f32[512,2048]{1,0:T(8,128)} %get-tuple-element.41.refs_2_.y, f32[512,2048]{1,0:T(8,128)} %get-tuple-element.35.u.refs_3_, ...), custom_call_target="tpu_custom_call" | custom-call | flops 268435456 | bytes 29360128 | tf_op jit(solution)/shard_map/pallas_call | solution.py:731
  269.9 3.4 concatenate.206
  276.4 2.9 collective-permute-done.42
  284.4 2.3 reduce.17
  288.5 7.2 %all-to-all-start.2 = ((bf16[32,2,1536]{2,1,0:T(2,128)(2,1)}), bf16[32,2,1536]{2,1,0:T(2,128)(2,1)}, u32[]{:S(2)}, u32[]{:S(2)}) async-start(bf16[32,2,1536]{2,1,0:T(2,128)(2,1)} %reshape.697), calls=%async_computation.2 | async-start | bytes 393216 | tf_op jit(solution)/shard_map/all_to_all | solution.py:796
  299.5 12.9 %shard_map.249 = (f32[512,2048]{1,0:T(8,128)}, f32[4,128,128]{2,1,0:T(8,128)S(1)}, f32[512,128]{1,0:T(8,128)S(1)}) custom-call(f32[512,2048]{1,0:T(8,128)} %get-tuple-element.46.gh, f32[512,2048]{1,0:T(8,128)} %get-tuple-element.41.refs_2_.y, bf16[512,2048]{1,0:T(8,128)(2,1)S(1)} %copy-done.2, bf16[512,96]{1,0:T(8,128)(2,1)S(1)} %copy-done.53, ...), custom_call_target="tpu_custom_call" | custom-call | flops 4294967296 | bytes 14680064 | tf_op jit(solution)/shard_map/pallas_call | solution.py:742
  314.2 14.5 %shard_map.250 = (f32[512,2048]{1,0:T(8,128)}, f32[512,256]{1,0:T(8,128)S(1)}, bf16[512,32]{1,0:T(8,128)(2,1)S(1)}) custom-call(f32[128,2048]{1,0:T(8,128)S(1)} %convert_add_fusion.gs_in, bf16[4,128,2048]{2,1,0:T(8,128)(2,1)} %get-tuple-element.45.states, f32[512,2048]{1,0:T(8,128)} %get-tuple-element.46.gh, bf16[512,2048]{1,0:T(8,128)(2,1)} %get-tuple-element.34.sc, ...), custom_call_target="tpu_custom_call" | custom-call | flops 2147483648 | bytes 25165824 | tf_op jit(solution)/shard_map/pallas_call | solution.py:762
  333.3 8.1 %shard_map.251 = (f32[512,1024]{1,0:T(8,128)}, f32[512,16]{1,0:T(8,128)S(1)}, f32[16,2048]{1,0:T(8,128)S(1)}) custom-call(s32[12]{0:T(128)S(1)} %pad_add_fusion.sel.refs_0_, bf16[512,2048]{1,0:T(8,128)(2,1)} %copy-done.61, bf16[4,4,128,256]{3,2,1,0:T(8,128)(2,1)} %bitcast.7.own_a, bf16[4,4,128,256]{3,2,1,0:T(8,128)(2,1)} %collective-permute-done.5.oth_a, ...), custom_call_target="tpu_custom_call" | custom-call | flops 2147483648 | bytes 8388608 | tf_op jit(solution)/shard_map/pallas_call | solution.py:752
  343.9 2.2 reshape.698
  348.7 14.3 %shard_map.252 = (f32[512,1024]{1,0:T(8,128)}, f32[16,2048]{1,0:T(8,128)S(1)}, f32[16,1024]{1,0:T(8,128)S(1)}) custom-call(s32[12]{0:T(128)S(1)} %pad_add_fusion.sel.refs_0_, f32[512,2048]{1,0:T(8,128)} %get-tuple-element.50.gu, bf16[16,2048]{1,0:T(8,128)(2,1)S(1)} %slice.284.halo, bf16[4,4,128,256]{3,2,1,0:T(8,128)(2,1)S(1)} %bitcast.252, ...), custom_call_target="tpu_custom_call" | custom-call | flops 2147483648 | bytes 14680064 | tf_op jit(solution)/shard_map/pallas_call | solution.py:779
  363.3 2.3 maximum_bitcast_fusion
  365.6 2.7 copy.291
  368.3 3.0 concatenate.203
  373.1 8.0 %all-to-all-start.1 = ((bf16[32,2,2048]{2,1,0:T(2,128)(2,1)}), bf16[32,2,2048]{2,1,0:T(2,128)(2,1)S(1)}, u32[]{:S(2)}, u32[]{:S(2)}) async-start(bf16[32,2,2048]{2,1,0:T(2,128)(2,1)} %reshape.695), calls=%async_computation.1 | async-start | bytes 524288 | tf_op jit(solution)/shard_map/all_to_all | solution.py:796
  384.7 6.5 %all-to-all-done.1 = bf16[32,2,2048]{2,1,0:T(2,128)(2,1)S(1)} async-done(((bf16[32,2,2048]{2,1,0:T(2,128)(2,1)}), bf16[32,2,2048]{2,1,0:T(2,128)(2,1)S(1)}, u32[]{:S(2)}, u32[]{:S(2)}) %all-to-all-start.1) | async-done | bytes 262176 | tf_op jit(solution)/shard_map/all_to_all | solution.py:796
  (554 shorter events, 187.2 us)
Async XLA Ops:
  2.3 60.7 %collective-permute-start.2 = (bf16[128,512]{1,0:T(8,128)(2,1)S(1)}, bf16[128,512]{1,0:T(8,128)(2,1)S(1)}, u32[]{:S(2)}, u32[]{:S(2)}) collective-permute-start(bf16[128,512]{1,0:T(8,128)(2,1)S(1)} %bitcast.289), channel_id=1, source_target_pairs={{0,3},{1,0},{2,1},{3,2},{4,7},{5,4},{6,5},{7,6},{8,11},{9,8},{10,9... | collective-permute-start | bytes 393224 | tf_op jit(solution)/shard_map/ppermute | solution.py:444
  6.5 58.3 %collective-permute-start.1 = (bf16[128,512]{1,0:T(8,128)(2,1)S(1)}, bf16[128,512]{1,0:T(8,128)(2,1)S(1)}, u32[]{:S(2)}, u32[]{:S(2)}) collective-permute-start(bf16[128,512]{1,0:T(8,128)(2,1)S(1)} %bitcast.290), channel_id=1, source_target_pairs={{0,2},{1,3},{2,0},{3,1},{4,6},{5,7},{6,4},{7,5},{8,10},{9,11},{10,... | collective-permute-start | bytes 393224 | tf_op jit(solution)/shard_map/ppermute | solution.py:444
  9.7 38.7 %collective-permute-start.18 = (f32[5136]{0:T(1024)S(1)}, f32[5136]{0:T(1024)S(1)}, u32[]{:S(2)}, u32[]{:S(2)}) collective-permute-start(f32[5136]{0:T(1024)S(1)} %concatenate.175), channel_id=1, source_target_pairs={{0,3},{1,0},{2,1},{3,2},{4,7},{5,4},{6,5},{7,6},{8,11},{9,8},{10,9... | collective-permute-start | bytes 61640 | tf_op jit(solution)/shard_map/ppermute | solution.py:444
  9.9 38.5 %collective-permute-start.17 = (f32[5136]{0:T(1024)S(1)}, f32[5136]{0:T(1024)S(1)}, u32[]{:S(2)}, u32[]{:S(2)}) collective-permute-start(f32[5136]{0:T(1024)S(1)} %concatenate.175), channel_id=1, source_target_pairs={{0,2},{1,3},{2,0},{3,1},{4,6},{5,7},{6,4},{7,5},{8,10},{9,11},{10,... | collective-permute-start | bytes 61640 | tf_op jit(solution)/shard_map/ppermute | solution.py:444
  12.1 18.7 %collective-permute-start.10 = (s32[1,1]{0,1:T(1,128)}, s32[1,1]{0,1:T(1,128)}, u32[]{:S(2)}, u32[]{:S(2)}) collective-permute-start(s32[1,1]{0,1:T(1,128)} %bitcast.10), channel_id=1, source_target_pairs={{0,4},{4,0},{8,12},{12,8},{16,20},{20,16},{24,28},{28,24},{1,5},{5... | collective-permute-start | bytes 20 | tf_op jit(solution)/shard_map/ppermute | solution.py:450
  42.1 17.4 %all-to-all-start = ((bf16[8,2,3584]{2,1,0:T(2,128)(2,1)}), bf16[8,2,3584]{2,1,0:T(2,128)(2,1)S(1)}, u32[]{:S(2)}, u32[]{:S(2)}) async-start(bf16[8,2,3584]{2,1,0:T(2,128)(2,1)} %reshape.693), calls=%async_computation | async-start | bytes 229376 | tf_op jit(solution)/shard_map/all_to_all | solution.py:550
  48.4 17.9 %collective-permute-start = (bf16[128,512]{1,0:T(8,128)(2,1)S(1)}, bf16[128,512]{1,0:T(8,128)(2,1)}, u32[]{:S(2)}, u32[]{:S(2)}) collective-permute-start(bf16[128,512]{1,0:T(8,128)(2,1)S(1)} %bitcast.291), channel_id=1, source_target_pairs={{0,1},{1,2},{2,3},{3,0},{4,5},{5,6},{6,7},{7,4},{8,9},{9,10},{10,1... | collective-permute-start | bytes 393224 | tf_op jit(solution)/shard_map/ppermute | solution.py:444
  50.4 17.7 %collective-permute-start.21 = (bf16[128,512]{1,0:T(8,128)(2,1)S(1)}, bf16[128,512]{1,0:T(8,128)(2,1)}, u32[]{:S(2)}, u32[]{:S(2)}) collective-permute-start(bf16[128,512]{1,0:T(8,128)(2,1)S(1)} %bitcast.293), channel_id=1, source_target_pairs={{0,3},{1,0},{2,1},{3,2},{4,7},{5,4},{6,5},{7,6},{8,11},{9,8},{10,9... | collective-permute-start | bytes 393224 | tf_op jit(solution)/shard_map/ppermute | solution.py:444
  66.3 15.6 %collective-permute-start.34 = (bf16[128,512]{0,1:T(8,128)(2,1)S(1)}, bf16[128,512]{0,1:T(8,128)(2,1)S(1)}, u32[]{:S(2)}, u32[]{:S(2)}) collective-permute-start(bf16[128,512]{0,1:T(8,128)(2,1)S(1)} %bitcast.305), channel_id=1, source_target_pairs={{0,2},{1,3},{2,0},{3,1},{4,6},{5,7},{6,4},{7,5},{8,10},{9,11},{10,... | collective-permute-start | bytes 393224 | tf_op jit(solution)/shard_map/ppermute | solution.py:444
  68.0 14.4 %collective-permute-start.33 = (bf16[128,512]{0,1:T(8,128)(2,1)S(1)}, bf16[128,512]{0,1:T(8,128)(2,1)S(1)}, u32[]{:S(2)}, u32[]{:S(2)}) collective-permute-start(bf16[128,512]{0,1:T(8,128)(2,1)S(1)} %bitcast.306), channel_id=1, source_target_pairs={{0,1},{1,2},{2,3},{3,0},{4,5},{5,6},{6,7},{7,4},{8,9},{9,10},{10,1... | collective-permute-start | bytes 393224 | tf_op jit(solution)/shard_map/ppermute | solution.py:444
  68.4 32.4 %collective-permute-start.29 = (bf16[2,128,288]{2,1,0:T(8,128)(2,1)}, bf16[2,128,288]{2,1,0:T(8,128)(2,1)}, u32[]{:S(2)}, u32[]{:S(2)}) collective-permute-start(bf16[2,128,288]{2,1,0:T(8,128)(2,1)} %pad_maximum_fusion.20), channel_id=1, source_target_pairs={{0,8},{4,12},{8,0},{12,4},{16,24},{20,28},{24,16},{28,20},{1,9},{5... | collective-permute-start | bytes 442376 | tf_op jit(solution)/shard_map/ppermute | solution.py:450
  82.4 20.6 %collective-permute-start.3 = (bf16[1,1,4,128,256]{4,3,2,1,0:T(8,128)(2,1)}, bf16[1,1,4,128,256]{4,3,2,1,0:T(8,128)(2,1)}, u32[]{:S(2)}, u32[]{:S(2)}) collective-permute-start(bf16[1,1,4,128,256]{4,3,2,1,0:T(8,128)(2,1)} %get-tuple-element.113), channel_id=1, source_target_pairs={{0,8},{4,12},{8,0},{12,4},{16,24},{20,28},{24,16},{28,20},{1,9},{5... | collective-permute-start | bytes 786440 | tf_op jit(solution)/shard_map/ppermute | solution.py:450
  85.1 20.2 %collective-permute-start.6 = (bf16[1,1,4,128,256]{4,3,2,1,0:T(8,128)(2,1)S(1)}, bf16[1,1,4,128,256]{4,3,2,1,0:T(8,128)(2,1)}, u32[]{:S(2)}, u32[]{:S(2)}) collective-permute-start(bf16[1,1,4,128,256]{4,3,2,1,0:T(8,128)(2,1)S(1)} %get-tuple-element.112), channel_id=1, source_target_pairs={{0,16},{4,20},{8,24},{12,28},{16,0},{20,4},{24,8},{28,12},{1,17},{... | collective-permute-start | bytes 786440 | tf_op jit(solution)/shard_map/ppermute | solution.py:450
  86.2 22.0 %collective-permute-start.22 = (bf16[1,1,4,128,256]{4,3,2,1,0:T(8,128)(2,1)}, bf16[1,1,4,128,256]{4,3,2,1,0:T(8,128)(2,1)}, u32[]{:S(2)}, u32[]{:S(2)}) collective-permute-start(bf16[1,1,4,128,256]{4,3,2,1,0:T(8,128)(2,1)} %get-tuple-element.111), channel_id=1, source_target_pairs={{0,8},{4,12},{8,0},{12,4},{16,24},{20,28},{24,16},{28,20},{1,9},{5... | collective-permute-start | bytes 786440 | tf_op jit(solution)/shard_map/ppermute | solution.py:450
  87.1 23.3 %collective-permute-start.25 = (bf16[1,1,4,128,256]{4,3,2,1,0:T(8,128)(2,1)}, bf16[1,1,4,128,256]{4,3,2,1,0:T(8,128)(2,1)}, u32[]{:S(2)}, u32[]{:S(2)}) collective-permute-start(bf16[1,1,4,128,256]{4,3,2,1,0:T(8,128)(2,1)} %get-tuple-element.110), channel_id=1, source_target_pairs={{0,16},{4,20},{8,24},{12,28},{16,0},{20,4},{24,8},{28,12},{1,17},{... | collective-permute-start | bytes 786440 | tf_op jit(solution)/shard_map/ppermute | solution.py:450
  108.2 69.8 %collective-permute-start.4 = (bf16[1,2,4,128,256]{4,3,2,1,0:T(8,128)(2,1)}, bf16[1,2,4,128,256]{4,3,2,1,0:T(8,128)(2,1)}, u32[]{:S(2)}, u32[]{:S(2)}) collective-permute-start(bf16[1,2,4,128,256]{4,3,2,1,0:T(8,128)(2,1)} %pad_maximum_fusion.9), channel_id=1, source_target_pairs={{0,16},{4,20},{8,24},{12,28},{16,0},{20,4},{24,8},{28,12},{1,17},{... | collective-permute-start | bytes 1572872 | tf_op jit(solution)/shard_map/ppermute | solution.py:450
  110.5 70.5 %collective-permute-start.7 = (bf16[2,1,4,128,256]{4,3,2,1,0:T(8,128)(2,1)}, bf16[2,1,4,128,256]{4,3,2,1,0:T(8,128)(2,1)}, u32[]{:S(2)}, u32[]{:S(2)}) collective-permute-start(bf16[2,1,4,128,256]{4,3,2,1,0:T(8,128)(2,1)} %pad_maximum_fusion.10), channel_id=1, source_target_pairs={{0,8},{4,12},{8,0},{12,4},{16,24},{20,28},{24,16},{28,20},{1,9},{5... | collective-permute-start | bytes 1572872 | tf_op jit(solution)/shard_map/ppermute | solution.py:450
  112.4 26.9 %collective-permute-start.23 = (bf16[1,2,4,128,256]{4,3,2,1,0:T(8,128)(2,1)}, bf16[1,2,4,128,256]{4,3,2,1,0:T(8,128)(2,1)}, u32[]{:S(2)}, u32[]{:S(2)}) collective-permute-start(bf16[1,2,4,128,256]{4,3,2,1,0:T(8,128)(2,1)} %pad_maximum_fusion.12), channel_id=1, source_target_pairs={{0,16},{4,20},{8,24},{12,28},{16,0},{20,4},{24,8},{28,12},{1,17},{... | collective-permute-start | bytes 1572872 | tf_op jit(solution)/shard_map/ppermute | solution.py:450
  114.7 32.6 %collective-permute-start.26 = (bf16[2,1,4,128,256]{4,3,2,1,0:T(8,128)(2,1)}, bf16[2,1,4,128,256]{4,3,2,1,0:T(8,128)(2,1)}, u32[]{:S(2)}, u32[]{:S(2)}) collective-permute-start(bf16[2,1,4,128,256]{4,3,2,1,0:T(8,128)(2,1)} %pad_maximum_fusion.13), channel_id=1, source_target_pairs={{0,8},{4,12},{8,0},{12,4},{16,24},{20,28},{24,16},{28,20},{1,9},{5... | collective-permute-start | bytes 1572872 | tf_op jit(solution)/shard_map/ppermute | solution.py:450
  116.8 66.4 %collective-permute-start.37 = (bf16[1,2,4,128,256]{3,4,2,1,0:T(8,128)(2,1)}, bf16[1,2,4,128,256]{3,4,2,1,0:T(8,128)(2,1)}, u32[]{:S(2)}, u32[]{:S(2)}) collective-permute-start(bf16[1,2,4,128,256]{3,4,2,1,0:T(8,128)(2,1)} %pad_maximum_fusion.15), channel_id=1, source_target_pairs={{0,16},{4,20},{8,24},{12,28},{16,0},{20,4},{24,8},{28,12},{1,17},{... | collective-permute-start | bytes 1572872 | tf_op jit(solution)/shard_map/ppermute | solution.py:450
  140.7 20.0 %collective-permute-start.24 = (bf16[4,4,128,256]{3,2,1,0:T(8,128)(2,1)S(1)}, bf16[4,4,128,256]{3,2,1,0:T(8,128)(2,1)}, u32[]{:S(2)}, u32[]{:S(2)}) collective-permute-start(bf16[4,4,128,256]{3,2,1,0:T(8,128)(2,1)S(1)} %bitcast.250), channel_id=1, source_target_pairs={{0,4},{4,0},{8,12},{12,8},{16,20},{20,16},{24,28},{28,24},{1,5},{5... | collective-permute-start | bytes 3145736 | tf_op jit(solution)/shard_map/ppermute | solution.py:450
  160.7 34.6 %collective-permute-start.40 = (bf16[2,1,4,128,256]{3,4,2,1,0:T(8,128)(2,1)}, bf16[2,1,4,128,256]{3,4,2,1,0:T(8,128)(2,1)}, u32[]{:S(2)}, u32[]{:S(2)}) collective-permute-start(bf16[2,1,4,128,256]{3,4,2,1,0:T(8,128)(2,1)} %pad_maximum_fusion.16), channel_id=1, source_target_pairs={{0,8},{4,12},{8,0},{12,4},{16,24},{20,28},{24,16},{28,20},{1,9},{5... | collective-permute-start | bytes 1572872 | tf_op jit(solution)/shard_map/ppermute | solution.py:450
  180.4 40.2 %collective-permute-start.5 = (bf16[4,4,128,256]{3,2,1,0:T(8,128)(2,1)}, bf16[4,4,128,256]{3,2,1,0:T(8,128)(2,1)}, u32[]{:S(2)}, u32[]{:S(2)}) collective-permute-start(bf16[4,4,128,256]{3,2,1,0:T(8,128)(2,1)} %bitcast.7.own_a), channel_id=1, source_target_pairs={{0,4},{4,0},{8,12},{12,8},{16,20},{20,16},{24,28},{28,24},{1,5},{5... | collective-permute-start | bytes 3145736 | tf_op jit(solution)/shard_map/ppermute | solution.py:450
  183.1 37.5 %collective-permute-start.8 = (bf16[4,4,128,256]{3,2,1,0:T(8,128)(2,1)}, bf16[4,4,128,256]{3,2,1,0:T(8,128)(2,1)}, u32[]{:S(2)}, u32[]{:S(2)}) collective-permute-start(bf16[4,4,128,256]{3,2,1,0:T(8,128)(2,1)} %bitcast.9.own_b), channel_id=1, source_target_pairs={{0,4},{4,0},{8,12},{12,8},{16,20},{20,16},{24,28},{28,24},{1,5},{5... | collective-permute-start | bytes 3145736 | tf_op jit(solution)/shard_map/ppermute | solution.py:450
  185.7 50.3 %collective-permute-start.38 = (bf16[4,4,128,256]{3,2,1,0:T(8,128)(2,1)}, bf16[4,4,128,256]{3,2,1,0:T(8,128)(2,1)}, u32[]{:S(2)}, u32[]{:S(2)}) collective-permute-start(bf16[4,4,128,256]{3,2,1,0:T(8,128)(2,1)} %bitcast.76.refs_2_), channel_id=1, source_target_pairs={{0,4},{4,0},{8,12},{12,8},{16,20},{20,16},{24,28},{28,24},{1,5},{5... | collective-permute-start | bytes 3145736 | tf_op jit(solution)/shard_map/ppermute | solution.py:450
  190.3 28.1 %collective-permute-start.32 = (bf16[128,2048]{1,0:T(8,128)(2,1)}, bf16[128,2048]{1,0:T(8,128)(2,1)}, u32[]{:S(2)}, u32[]{:S(2)}) collective-permute-start(bf16[128,2048]{1,0:T(8,128)(2,1)} %fusion.4), channel_id=1, source_target_pairs={{0,1},{1,2},{2,3},{4,5},{5,6},{6,7},{8,9},{9,10},{10,11},{12,13},{... | collective-permute-start | bytes 1572872 | tf_op jit(solution)/shard_map/ppermute | solution.py:433
  199.8 36.1 %collective-permute-start.41 = (bf16[4,4,128,256]{3,2,1,0:T(8,128)(2,1)}, bf16[4,4,128,256]{3,2,1,0:T(8,128)(2,1)}, u32[]{:S(2)}, u32[]{:S(2)}) collective-permute-start(bf16[4,4,128,256]{3,2,1,0:T(8,128)(2,1)} %bitcast.266), channel_id=1, source_target_pairs={{0,4},{4,0},{8,12},{12,8},{16,20},{20,16},{24,28},{28,24},{1,5},{5... | collective-permute-start | bytes 3145736 | tf_op jit(solution)/shard_map/ppermute | solution.py:450
  263.6 15.7 %collective-permute-start.42 = (bf16[128,2048]{1,0:T(8,128)(2,1)}, bf16[128,2048]{1,0:T(8,128)(2,1)}, u32[]{:S(2)}, u32[]{:S(2)}) collective-permute-start(bf16[128,2048]{1,0:T(8,128)(2,1)} %get-tuple-element.44), channel_id=1, source_target_pairs={{1,0},{2,1},{3,2},{5,4},{6,5},{7,6},{9,8},{10,9},{11,10},{13,12},{... | collective-permute-start | bytes 1572872 | tf_op jit(solution)/shard_map/ppermute | solution.py:438
  281.2 31.3 %collective-permute-start.43 = (bf16[128,2048]{1,0:T(8,128)(2,1)}, bf16[128,2048]{1,0:T(8,128)(2,1)}, u32[]{:S(2)}, u32[]{:S(2)}) collective-permute-start(bf16[128,2048]{1,0:T(8,128)(2,1)} %fusion.5), channel_id=1, source_target_pairs={{1,0},{2,1},{3,2},{5,4},{6,5},{7,6},{9,8},{10,9},{11,10},{13,12},{... | collective-permute-start | bytes 1572872 | tf_op jit(solution)/shard_map/ppermute | solution.py:438
  288.5 55.4 %all-to-all-start.2 = ((bf16[32,2,1536]{2,1,0:T(2,128)(2,1)}), bf16[32,2,1536]{2,1,0:T(2,128)(2,1)}, u32[]{:S(2)}, u32[]{:S(2)}) async-start(bf16[32,2,1536]{2,1,0:T(2,128)(2,1)} %reshape.697), calls=%async_computation.2 | async-start | bytes 393216 | tf_op jit(solution)/shard_map/all_to_all | solution.py:796
  331.7 14.4 %collective-permute-start.44 = (bf16[16,2304]{1,0:T(8,128)(2,1)}, bf16[16,2304]{1,0:T(8,128)(2,1)}, u32[]{:S(2)}, u32[]{:S(2)}) collective-permute-start(bf16[16,2304]{1,0:T(8,128)(2,1)} %pad_maximum_fusion.31), channel_id=1, source_target_pairs={{1,0},{2,1},{3,2},{5,4},{6,5},{7,6},{9,8},{10,9},{11,10},{13,12},{... | collective-permute-start | bytes 221192 | tf_op jit(solution)/shard_map/ppermute | solution.py:438
  373.1 18.2 %all-to-all-start.1 = ((bf16[32,2,2048]{2,1,0:T(2,128)(2,1)}), bf16[32,2,2048]{2,1,0:T(2,128)(2,1)S(1)}, u32[]{:S(2)}, u32[]{:S(2)}) async-start(bf16[32,2,2048]{2,1,0:T(2,128)(2,1)} %reshape.695), calls=%async_computation.1 | async-start | bytes 524288 | tf_op jit(solution)/shard_map/all_to_all | solution.py:796
  (143 other events, 1426.0 us)

commit v2 on v1

v2 whole, which is shorter than its diff:
```python
import math

import jax
import jax.numpy as jnp
import numpy as np
from jax import lax
from jax.experimental import pallas as pl
from jax.experimental.pallas import tpu as pltpu
from jax.sharding import PartitionSpec as P

epsilon = 1e-05
chunk = 128
lanes = 128
doc_most = 800
edge = 16
f32, bf16 = jnp.float32, jnp.bfloat16
exact = lax.Precision.HIGHEST
vmem_bytes = 48 * 1024 * 1024


def dot(a, b):
    return jnp.dot(a, b, preferred_element_type=f32)


def dot_nt(a, b):
    return lax.dot_general(a, b, (((1,), (1,)), ((), ())), preferred_element_type=f32)


def dot_tn(a, b):
    return lax.dot_general(a, b, (((0,), (0,)), ((), ())), preferred_element_type=f32)


def halves(x):
    high = x.astype(bf16)
    return high, (x - high.astype(f32)).astype(bf16)


def pieces(x, count):
    out = []
    for _ in range(count):
        part = lax.reduce_precision(x, 8, 7)
        out.append(part.astype(bf16))
        x = x - part
    return jnp.concatenate(out, axis=-1)


def dot2(x, w):
    high, low = halves(x)
    return dot(high, w) + dot(low, w)


def dot2_nt(x, w):
    high, low = halves(x)
    return dot_nt(high, w) + dot_nt(low, w)


def dot2_tn(x, w):
    high, low = halves(x)
    return dot_tn(high, w) + dot_tn(low, w)


def tile_lanes(m, width):
    return m if width == lanes else jnp.concatenate([m] * (width // lanes), axis=1)


def sigmoid(u):
    return 0.5 + 0.5 * jnp.tanh(0.5 * u)


def silu(u):
    return u * sigmoid(u)


def silu_parts(u):
    s = sigmoid(u)
    v = u * s
    return v, s + v * (1.0 - s)


korder = (0, 2, 4, 6, 1, 3, 5, 7)


def weight_pieces(refs, at=0):
    if len(refs) == 1:
        return [refs[0][...].reshape(-1, refs[0].shape[-1])]
    a01, a23, c01, c23 = (refs[4 * at + j] for j in range(4))
    if at == 0:
        parts = [a01[0, 0], a01[1, 0], a23[0, 0], a23[1, 0], c01[0, 0], c01[1, 0], c23[0, 0], c23[1, 0]]
    else:
        parts = [a01[0, 0], a23[0, 0], a01[1, 0], a23[1, 0], c01[0, 0], c23[0, 0], c01[1, 0], c23[1, 0]]
    return [jnp.concatenate(parts[j : j + 2], axis=0) for j in range(0, 8, 2)]


def with_weight(refs, body, half):
    if len(refs) == 1:
        body(weight_pieces(refs))
        return
    if isinstance(half, int):
        body(weight_pieces(refs * 2, half))
        return

    @pl.when(half == 0)
    def _():
        body(weight_pieces(refs, 0))

    @pl.when(half == 1)
    def _():
        body(weight_pieces(refs, 1))


def times(left, parts):
    total, k = None, 0
    for w in parts:
        term = dot(left[:, k : k + w.shape[0]], w)
        total = term if total is None else total + term
        k += w.shape[0]
    return total


def add_times_transposed(acc, low, parts):
    k = 0
    for w in parts:
        acc[:, k : k + w.shape[0]] += dot_nt(low, w)
        k += w.shape[0]


def rows_of(c):
    return slice(c * chunk, (c + 1) * chunk)


def sums3(tri, x):
    high, mid = halves(x)
    low = (x - high.astype(f32) - mid.astype(f32)).astype(bf16)
    return dot(tri, high) + dot(tri, mid) + dot(tri, low)


def parts_of(x, count):
    out = []
    for _ in range(count):
        part = x.astype(bf16)
        out.append(part)
        x = x - part.astype(f32)
    return jnp.concatenate(out, axis=1)


def table_of(x, count):
    parts = parts_of(x, count)
    return jnp.concatenate([parts, jnp.zeros((x.shape[0], lanes - parts.shape[1]), bf16)], axis=1)


def column(row):
    return jnp.broadcast_to(row, (lanes, lanes)).T


def prep_kernel(sel, tokens, halo, norm_gain, small, dt_t, inner_t, place, params, params_bc, segs, ex, no_out,
                normed, ranks, ranks_own, tables, bc_out, bct_out, scores, rows_out, cums_t, keep, ups, wides, w_bc,
                masks, ext, *, rank, state, moved_blocks):
    own, width = tokens.shape
    blocks = own // chunk
    tp, _, group = params.shape
    heads = dt_t.shape[0]
    part = heads // tp
    bc_rows = 2 * lanes
    turn, pick, bound, small_at = 8 + tp, sel[8 + 2 * tp], 9 + 2 * tp, 9 + 2 * tp + 2 * blocks

    for c in range(blocks):
        wide = tokens[rows_of(c), :].astype(f32)
        scale = lax.rsqrt(jnp.sum(wide * wide, axis=1, keepdims=True) / width + epsilon)
        ext[edge + c * chunk : edge + (c + 1) * chunk, :] = (wide * scale * norm_gain[...]).astype(bf16)
    ext[:edge, :] = halo[...]
    for j in range(8):
        k = korder[j]
        at = pl.ds(pl.multiple_of(sel[k] * lanes, lanes), lanes)
        cols = slice(j * lanes, (j + 1) * lanes)
        no_out[:, cols] = ext[:, at]
        at = sel[small_at + j]
        wides[:, cols] = small[at, pl.ds(pl.multiple_of(bc_rows + pick * 2 * rank, 2 * rank), 2 * rank), :]
        w_bc[j * lanes : (j + 1) * lanes, :state] = small[at, :lanes, :]
        w_bc[j * lanes : (j + 1) * lanes, state:] = small[at, lanes : 2 * lanes, :]
    normed[...] = ext[edge:, :]
    ranks[...] = parts_of(dot_nt(ext[...], wides[:rank, :]), 2)
    ranks_own[...] = ranks[edge:, :]
    bc = dot(ext[...], w_bc[...])

    hp = place.shape[1]
    for s in range(tp):
        cols = slice(s * group, (s + 1) * group)
        z = x = d = None
        for k in range(inner_t.shape[1]):
            where = place[sel[korder[k]]] if moved_blocks else place[k]
            piece = inner_t[sel[turn + s], k]
            terms = (dot(piece[:rank, :hp], where), dot(piece[:rank, hp : 2 * hp], where),
                     dot(piece[rank:, :hp], where))
            z, x, d = terms if z is None else (z + terms[0], x + terms[1], d + terms[2])
        z, x = z.astype(bf16), x.astype(bf16)
        ups[:, cols] = jnp.concatenate([z, z, x, x, d.astype(bf16)], axis=0)

    i = lax.broadcasted_iota(jnp.int32, (chunk, chunk), 0)
    j = lax.broadcasted_iota(jnp.int32, (chunk, chunk), 1)
    tril = jnp.where(j <= i, 1.0, 0.0)
    segs_at = []
    for c in range(blocks):
        rows = rows_of(c)
        seg = column(segs[3, c : c + 1, :])
        segs_at.append(seg[:, :heads])
        for k in range(1, 4):
            masks[k - 1, rows, :] = jnp.where(column(segs[3 - k, c : c + 1, :]) == seg, 1.0, 0.0)
            masks[k + 2, rows, :] = jnp.where(column(segs[3 + k, c : c + 1, :]) == seg, 1.0, 0.0)
        cur = bc[edge + c * chunk - 8 : edge + (c + 1) * chunk]
        total = params_bc[3:4, :] * cur[8:] + params_bc[4:5, :]
        for k in range(1, 4):
            shifted = pltpu.roll(cur, k, 0)[8:]
            total = total + params_bc[3 - k : 4 - k, :] * (
                shifted * tile_lanes(masks[k - 1, rows, :], 2 * state)
            )
        rows_out[rows, : 2 * state] = total
        value = silu(total)
        inb, inc = value[:, :state], value[:, state:]
        bc_out[rows, :] = value.astype(bf16)
        bct_out[:state, rows] = inb.T.astype(bf16)
        bct_out[state:, rows] = inc.T.astype(bf16)
        okay = jnp.where(seg == segs[3, c : c + 1, :], tril, 0.0)
        scores[1, c] = okay
        scores[0, c] = dot_nt(inc.astype(bf16), inb.astype(bf16)) * okay

    bias = jnp.concatenate([params[sel[turn + s], 7:8, :part] for s in range(tp)], axis=1)
    a_log = jnp.concatenate([params[sel[turn + s], 7:8, part : 2 * part] for s in range(tp)], axis=1)
    decays = -jnp.exp(a_log)
    raw = dot_nt(ext[edge:, :], dt_t[...]) + bias
    dt = jnp.maximum(raw, 0.0) + jnp.log1p(jnp.exp(-jnp.abs(raw)))
    rows_out[:, 2 * state :] = jnp.concatenate([sigmoid(raw), jnp.zeros((own, lanes - heads), f32)], axis=1)
    tables[:, :lanes] = table_of(dt, 2)
    logs = dt * decays * math.log2(math.e)
    bounds = [sel[bound + n].astype(f32) for n in range(2 * blocks)]
    before_seg, last_seg = bounds[0], bounds[-1]
    prior = jnp.zeros((1, heads), f32)
    all_cums, keeps = [], []
    tri = tril.astype(bf16)
    for c in range(blocks):
        rows = rows_of(c)
        before_c, last_c = bounds[2 * c], bounds[2 * c + 1]
        cums = sums3(tri, logs[rows])
        end = cums[chunk - 1 : chunk]
        seg = segs_at[c]
        tables[rows, 5 * lanes :] = table_of(cums, 3)
        flipped = jnp.concatenate([cums, jnp.zeros((chunk, lanes - heads), f32)], axis=1).T
        for s in range(tp):
            cums_t[s, c] = flipped[s * part : (s + 1) * part]
        tables[rows, 2 * lanes : 3 * lanes] = table_of(jnp.where(seg == before_c, jnp.exp2(cums), 0.0), 2)
        tables[rows, 3 * lanes : 4 * lanes] = table_of(jnp.where(seg == last_c, jnp.exp2(end - cums), 0.0), 2)
        keeps.append(jnp.where(before_c == last_c, jnp.exp2(end), 0.0))
        all_cums.append(cums + prior)
        prior = prior + end
    for c in range(blocks):
        rows = rows_of(c)
        seg = segs_at[c]
        tables[rows, 4 * lanes : 5 * lanes] = table_of(jnp.where(seg == before_seg, jnp.exp2(all_cums[c]), 0.0), 2)
        tables[rows, lanes : 2 * lanes] = table_of(jnp.where(seg == last_seg, jnp.exp2(prior - all_cums[c]), 0.0), 2)
    whole = jnp.where(before_seg == last_seg, jnp.exp2(prior), 0.0)
    table = jnp.concatenate(keeps + [jnp.zeros((7 - blocks, heads), f32), whole], axis=0)
    high, mid = halves(table)
    low = (table - high.astype(f32) - mid.astype(f32)).astype(bf16)
    spread = ex[:heads, :]
    keep[...] = dot(high, spread) + dot(mid, spread) + dot(low, spread)
    keep[6:7, :lanes] = jnp.concatenate([decays, jnp.zeros((1, lanes - heads), f32)], axis=1)


def pack_kernel(bc, dt_weight, in_down, out_up, in_up, out_down, pick, out):
    rows, two = bc.shape
    part = dt_weight.shape[0]
    count, rank, _ = in_down.shape
    at = 2 * rows
    out[:rows, :] = bc[:, : two // 2]
    out[rows:at, :] = bc[:, two // 2 :]
    for b in range(count):
        out[at + 2 * rank * b : at + 2 * rank * b + rank, :] = in_down[b]
        out[at + 2 * rank * b + rank : at + 2 * rank * (b + 1), :] = out_up[b]
    at += 2 * rank * count
    for b in range(count):
        out[at + 2 * rank * b : at + 2 * rank * b + rank, :] = in_up[b].astype(f32).T.astype(bf16)
        flipped = out_down[b].astype(f32).T
        out[at + 2 * rank * b + rank : at + 2 * rank * (b + 1), :] = jnp.concatenate(
            [flipped, jnp.zeros_like(flipped)], axis=1
        ).astype(bf16)
    at += 2 * rank * count
    wide = jnp.concatenate([dt_weight[...].astype(f32), jnp.zeros((16 - part, rows), f32)], axis=0)
    out[at : at + 16, :] = wide.astype(bf16)
    out[at + 16 : at + 32, :] = jnp.zeros((16, lanes), bf16) + pick[0].astype(f32).astype(bf16)


def proj_kernel(left, *refs, weights):
    refs, ws = refs[weights:], refs[:weights]
    ranks, a_up, params, masks, tables, ex, b_t, u_out, sc_out, f_out, xs, moved = refs

    def body(parts):
        xs[...] = times(left, parts) + dot(ranks[...], a_up[...])

    with_weight(ws, body, pl.program_id(0) // 2)
    own, width = u_out.shape
    step = min(width, 256)
    for c in range(own // chunk):
        rows = rows_of(c)
        for n in range(width // step):
            cols = slice(n * step, (n + 1) * step)
            cur = xs[edge + c * chunk - 8 : edge + (c + 1) * chunk, cols]
            total = params[0, 3:4, cols] * cur[8:] + params[0, 4:5, cols]
            for k in range(1, 4):
                shifted = pltpu.roll(cur, k, 0)[8:]
                total = total + params[0, 3 - k : 4 - k, cols] * (
                    shifted * tile_lanes(masks[k - 1, rows, :], step)
                )
            u_out[rows, cols] = total
            value = silu(total)
            scaled = (dot(tables[rows, :lanes], ex[:, cols]) * value).astype(bf16)
            sc_out[rows, cols] = scaled
            moved[rows, cols] = (dot(tables[rows, lanes:], ex[:, cols]) * scaled.astype(f32)).astype(bf16)
    f_out[...] = dot(b_t[...], moved[...]).astype(bf16)

def pair_parts(lcol, cums_t, p):
    lc = lcol[:, p * 2 * lanes : (p + 1) * 2 * lanes]
    lr = jnp.concatenate([cums_t[2 * p : 2 * p + 1, :], cums_t[2 * p + 1 : 2 * p + 2, :]], axis=1)
    return jnp.exp2(jnp.minimum(lc - lr, 0.0))


def two_heads(v, head_size):
    lane = lax.broadcasted_iota(jnp.int32, v.shape, 1)
    zero = jnp.zeros_like(v)
    return jnp.concatenate([jnp.where(lane < head_size, v, zero), jnp.where(lane < head_size, zero, v)], 0)


def within_kernel(sc, cums3, cums_t, scores, exl, y_out):
    own, width = y_out.shape
    for c in range(own // chunk):
        rows = rows_of(c)
        lcol = dot(cums3[rows, :], exl[...])
        allowed = tile_lanes(scores[0, c], 2 * lanes)
        for p in range(width // lanes):
            e = pair_parts(lcol, cums_t[0, c], p)
            m = (e * allowed).astype(bf16)
            cols = slice(p * lanes, (p + 1) * lanes)
            y_out[rows, cols] = dot(m, two_heads(sc[rows, cols], lanes // 2))


def row_scale_of(sumsq, inner):
    return lax.rsqrt(jnp.sum(sumsq, axis=1, keepdims=True) / inner + epsilon)


def put_width_parts(sent, value):
    rank = value.shape[0]
    dp, tp, _, _ = sent.shape
    size = value.shape[1] // dp
    for d in range(dp):
        piece = value[:, d * size : (d + 1) * size].astype(bf16)
        for t in range(tp):
            sent[d, t, :rank, :size] = piece


def put_inner_parts(sent, to, value, order, offset):
    rank = value.shape[0]
    dp = sent.shape[0]
    hp = value.shape[1] // dp
    moved = dot(value.astype(bf16), order[...]).astype(bf16)
    for d in range(dp):
        sent[d, to, rank : 2 * rank, offset : offset + hp] = moved[:, d * hp : (d + 1) * hp]


def middle_kernel(sel, left, *refs, weights, hops, inner):
    zs, outs, refs = refs[:weights], refs[weights : 2 * weights], refs[2 * weights :]
    s_ins, refs = refs[:hops], refs[hops:]
    (ranks, a_up, params, yw, u, sc, tables, own_in, keep, ex, b_t, c_t, in_c, cot, tokens, b_up, b_down, order,
     y_out, states, mixed, sent, gh_out, lz_out, g_out,
     heads, gate_z, gated, gg, sumsq, dots, acc, cots, g_rank, rank, low) = refs
    phase, g = pl.program_id(0), pl.program_id(1)
    last = pl.num_programs(1) - 1
    half = g // 2
    own, width = y_out.shape
    step = min(width, 256)
    blocks = own // chunk

    @pl.when((phase == 0) & (g == 0))
    def _():
        sumsq[...] = jnp.zeros_like(sumsq)
        acc[...] = jnp.zeros_like(acc)
        rank[...] = jnp.zeros_like(rank)
        dots[...] = jnp.zeros_like(dots)
        sent[...] = jnp.zeros_like(sent)
        for j in range(8):
            at = pl.ds(pl.multiple_of(sel[korder[j]] * lanes, lanes), lanes)
            cots[:, j * lanes : (j + 1) * lanes] = cot[:, at]
        g_rank[...] = dot_nt(cot[...], b_up[...])

    @pl.when(phase == 0)
    def _():
        def body(parts):
            gate_z[g] = times(left[left.shape[0] - own :, :], parts) + dot(ranks[...], a_up[...])

        with_weight(zs, body, half)
        for n in range(width // step):
            cols = slice(n * step, (n + 1) * step)
            new = []
            for c in range(blocks):
                rows = rows_of(c)
                moved = (dot(tables[rows, lanes:], ex[:, cols]) * sc[rows, cols].astype(f32)).astype(bf16)
                new.append(dot(b_t[:, rows], moved))
            s = sum(r[:, cols].astype(f32) for r in s_ins)
            for c in range(blocks):
                states[c, :, cols] = s.astype(bf16)
                s = s * keep[c : c + 1, cols] + new[c]
            for c in range(blocks):
                rows = rows_of(c)
                y = yw[rows, cols] + dot(tables[rows, :lanes], ex[:, cols]) * dot(in_c[rows, :], states[c, :, cols])
                y_out[rows, cols] = y
                head = y + params[0, 6:7, cols] * silu(u[rows, cols])
                heads[g, rows, cols] = head
                gd = head * silu(gate_z[g, rows, cols])
                gated[g, rows, cols] = gd
                sq = gd * gd
                total = sumsq[rows, :]
                for i in range(step // lanes):
                    total = total + sq[:, i * lanes : (i + 1) * lanes]
                sumsq[rows, :] = total

    @pl.when(phase == 1)
    def _():
        scale = row_scale_of(sumsq[...], inner)
        normed_inner = gated[g] * scale * params[0, 5:6, :]
        high, rest = halves(normed_inner)
        low[...] = high
        rank[...] += dot_nt(high, b_down[...]) + dot_nt(rest, b_down[...])
        r_high, r_low = halves(g_rank[...])
        p_down = dot_tn(r_high, high) + dot_tn(r_low, high) + dot_tn(r_high, rest)
        put_inner_parts(sent, sel[8 + g], p_down, order, 0)

        def body(parts):
            value = (times(cots, parts) + dot2(g_rank[...], b_down[...])) * params[0, 5:6, :]
            gg[g] = value
            prod = value * gated[g]
            total = dots[...]
            for i in range(width // lanes):
                total = total + prod[:, i * lanes : (i + 1) * lanes]
            dots[...] = total
            add_times_transposed(acc, low[...], parts)

        with_weight(outs, body, half)

    @pl.when((phase == 1) & (g == last))
    def _():
        put_width_parts(sent, dot2_tn(rank[...], cot[...]))
        mixed[...] = tokens[...].astype(f32) + dot2(rank[...], b_up[...])
        for j in range(8):
            at = pl.ds(pl.multiple_of(sel[korder[j]] * lanes, lanes), lanes)
            mixed[:, at] += acc[:, j * lanes : (j + 1) * lanes]

    @pl.when(phase == 2)
    def _():
        scale = row_scale_of(sumsq[...], inner)
        coef = scale * scale * scale * (jnp.sum(dots[...], axis=1, keepdims=True) / inner)
        for c in range(blocks):
            rows = rows_of(c)
            sc_rows, co_rows = scale[rows], coef[rows]
            for n in range(width // step):
                cols = slice(n * step, (n + 1) * step)
                g_gated = gg[g, rows, cols] * sc_rows - gated[g, rows, cols] * co_rows
                gate, slope = silu_parts(gate_z[g, rows, cols])
                lz_out[rows, cols] = (g_gated * heads[g, rows, cols] * slope).astype(bf16)
                gh = g_gated * gate
                gh_out[rows, cols] = gh
                low[rows, cols] = (dot(own_in[rows, :], ex[:, cols]) * gh).astype(bf16)
        g_out[...] = dot(c_t[...], low[...]).astype(bf16)


def back_within_kernel(gh, y, sc, cums3, cums_t, scores, exl, red, dv_out, ds_out, ahead, prod):
    g = pl.program_id(0)

    @pl.when(g == 0)
    def _():
        ds_out[...] = jnp.zeros_like(ds_out)
        ahead[...] = jnp.zeros_like(ahead)

    own, width = dv_out.shape
    for c in range(own // chunk):
        rows = rows_of(c)
        lcol = dot(cums3[rows, :], exl[...])
        allowed = tile_lanes(scores[0, c], 2 * lanes)
        ds = jnp.zeros((chunk, lanes), f32)
        for p in range(width // lanes):
            cols = slice(p * lanes, (p + 1) * lanes)
            e = pair_parts(lcol, cums_t[0, c], p)
            m = (e * allowed).astype(bf16)
            v = sc[rows, cols]
            dy = gh[rows, cols]
            high, low = halves(dy)
            both = two_heads(v, lanes // 2)
            parts = jnp.concatenate([high, low], axis=1)
            dm = dot_nt(parts, jnp.concatenate([both, both], axis=1))
            eds = e * dm
            ds = ds + eds[:, :lanes] + eds[:, lanes:]
            dvb = dot_tn(m, high) + dot_tn(m, low)
            lane = lax.broadcasted_iota(jnp.int32, (chunk, lanes), 1)
            dv = jnp.where(lane < lanes // 2, dvb[:chunk], dvb[chunk:])
            dv_out[rows, cols] = dv
            prod[:, cols] = y[rows, cols] * dy - v.astype(f32) * dv
        ds_out[c] += ds
        ahead[rows, :] += dot2(prod[...], red[...])


def back_state_kernel(*refs, hops):
    grads_in, refs = refs[:hops], refs[hops:]
    (states, gh, sc, dv, u, params, bc, c_t, tables, keep, decays, ex, red, ds, ahead, allowed, rows_in, gu_out, gbc_out,
     ldt_out, edges, db, dc, behind, direct, carry) = refs
    state = c_t.shape[0]
    g = pl.program_id(0)

    @pl.when(g == 0)
    def _():
        for ref in (db, dc, behind, direct, carry):
            ref[...] = jnp.zeros_like(ref)

    own, width = gu_out.shape
    step = min(width, 256)
    blocks = own // chunk
    for n in range(width // step):
        cols = slice(n * step, (n + 1) * step)
        gs = sum(r[:, cols].astype(f32) for r in grads_in)
        for c in reversed(range(blocks)):
            rows = rows_of(c)
            low_g = gs.astype(bf16)
            kept = keep[c : c + 1, cols]
            low_s = states[c, :, cols]
            scaled = sc[rows, cols].astype(f32)
            eo = dot(tables[rows, 3 * lanes :], ex[:, cols])
            dvs = eo * dot(bc[rows, :state], low_g)
            db[rows, :] += dot_nt((eo * scaled).astype(bf16), low_g)
            dy = gh[rows, cols]
            moved = (dot(tables[rows, 2 * lanes : 3 * lanes], ex[:, cols]) * dy).astype(bf16)
            dc[rows, :] += dot_nt(moved, low_s)
            carried = jnp.sum(low_s.astype(f32) * gs, axis=0, keepdims=True) * kept
            carry[c : c + 1, :] += dot2(jnp.broadcast_to(carried, (8, step)), red[cols, :])[:1]
            gs = gs * kept + dot(c_t[:, rows], moved)
            g_sc = dv[rows, cols] + dvs
            v, slope = silu_parts(u[rows, cols])
            behind[rows, :] += dot2(scaled * dvs, red[cols, :])
            direct[rows, :] += dot2(v * g_sc, red[cols, :])
            g_v = dot(tables[rows, :lanes], ex[:, cols]) * g_sc + params[0, 6:7, cols] * dy
            gu_out[rows, cols] = g_v * slope
            if c == 0:
                at = pl.ds(pl.multiple_of(g * width + n * step, lanes), step)
                edges[:, at] = (g_v * slope)[:edge].astype(bf16)

    @pl.when(g == pl.num_programs(0) - 1)
    def _():
        i = lax.broadcasted_iota(jnp.int32, (chunk, chunk), 0)
        j = lax.broadcasted_iota(jnp.int32, (chunk, chunk), 1)
        at_most = jnp.where(i <= j, 1.0, 0.0).astype(bf16)
        below = jnp.where(j < i, 1.0, 0.0).astype(bf16)
        decay_row = decays[6:7, :]
        for c in range(blocks):
            rows = rows_of(c)

            g_logs = sums3(at_most, ahead[rows, :]) + sums3(below, behind[rows, :]) + carry[c : c + 1, :]
            heads = ldt_out.shape[1]
            g_dt = (direct[rows, :] + g_logs * decay_row) * rows_in[rows, 2 * state :]
            ldt_out[rows, :] = g_dt[:, :heads].astype(bf16)
            g_scores = ds[c] * allowed[0, c]
            low_ds = g_scores.astype(bf16)
            gc = dc[rows, :] + dot(low_ds, bc[rows, :state])
            gb = db[rows, :] + dot_tn(low_ds, bc[rows, state:])
            g_bc = jnp.concatenate([gb, gc], axis=1)
            _, slope = silu_parts(rows_in[rows, : 2 * state])
            gbc_out[rows, :] = g_bc * slope
            if c == 0:
                edges[:, edges.shape[1] - g_bc.shape[1] :] = (g_bc * slope)[:edge].astype(bf16)


def in_z_kernel(lz, *refs, weights):
    ws, refs = refs[:weights], refs[weights:]
    a_up, ranks, acc, g_rank, p_up = refs

    @pl.when(pl.program_id(0) == 0)
    def _():
        acc[...] = jnp.zeros_like(acc)
        g_rank[...] = jnp.zeros_like(g_rank)

    size = g_rank.shape[1]
    g_rank[...] += dot_nt(lz[...], a_up[...])
    both = dot_tn(ranks[...], lz[...])
    p_up[0] = both[:size] + both[size:]
    with_weight(ws, lambda parts: add_times_transposed(acc, lz[...], parts), pl.program_id(0) // 2)


def conv_back(cur, params, masks, rows, width):
    total = params[3:4, :] * cur[:chunk]
    for k in range(1, 4):
        shifted = pltpu.roll(cur, cur.shape[0] - k, 0)[:chunk]
        total = total + params[3 - k : 4 - k, :] * (shifted * tile_lanes(masks[k - 1, rows, :], width))
    return total


def in_x_kernel(sel, gu, halo, a_up, ranks, params, masks, g_rank_z, p_up_z, order, normed, lx_out, g_rank, sent):
    g = pl.program_id(0)

    @pl.when(g == 0)
    def _():
        g_rank[...] = g_rank_z[...]
        sent[...] = jnp.zeros_like(sent)

    own, width = gu.shape
    step = min(width, 256)
    blocks = own // chunk
    for c in range(blocks):
        rows = rows_of(c)
        for n in range(width // step):
            cols = slice(n * step, (n + 1) * step)
            if c < blocks - 1:
                cur = gu[c * chunk : (c + 1) * chunk + 8, cols]
            else:
                cur = jnp.concatenate([gu[rows, cols], halo[:, cols].astype(f32)[:8]], axis=0)
            lx_out[rows, cols] = conv_back(cur, params[0, :, cols], masks, rows, step).astype(bf16)
    size = g_rank.shape[1]
    g_rank[...] += dot_nt(lx_out[...], a_up[...])
    both = dot_tn(ranks[...], lx_out[...])
    to = sel[8 + g]
    put_inner_parts(sent, to, p_up_z[0], order, 0)
    put_inner_parts(sent, to, both[:size] + both[size:], order, width // sent.shape[0])

    @pl.when(g == pl.num_programs(0) - 1)
    def _():
        put_width_parts(sent, dot2_tn(g_rank[...], normed[...]))


def tokens_kernel(sel, lx, *refs, weights):
    ws, refs = refs[:weights], refs[weights:]
    (acc_z, g_rank, gbc, halo_bc, params_bc, w_bc, ldt, dt_t, ad, masks, tokens, cot, norm_gain, grad, acc, lbc,
     g_norm) = refs
    g = pl.program_id(0)

    @pl.when(g == 0)
    def _():
        acc[...] = acc_z[...]

    with_weight(ws, lambda parts: add_times_transposed(acc, lx[...], parts), pl.program_id(0) // 2)

    @pl.when(g == pl.num_programs(0) - 1)
    def _():
        own, width = grad.shape
        blocks = own // chunk
        for c in range(blocks):
            rows = rows_of(c)
            if c < blocks - 1:
                cur = gbc[c * chunk : (c + 1) * chunk + 8, :]
            else:
                cur = jnp.concatenate([gbc[rows, :], halo_bc[...].astype(f32)[:8]], axis=0)
            lbc[rows, :] = conv_back(cur, params_bc[...], masks, rows, gbc.shape[1]).astype(bf16)
        g_norm[...] = (
            dot_nt(lbc[...], w_bc[...]) + dot(ldt[...], dt_t[...]) + dot2(g_rank[...], ad[...])
        )
        for j in range(8):
            at = pl.ds(pl.multiple_of(sel[korder[j]] * lanes, lanes), lanes)
            g_norm[:, at] += acc[:, j * lanes : (j + 1) * lanes]
        for c in range(blocks):
            rows = rows_of(c)
            wide = tokens[rows, :].astype(f32)
            scale = lax.rsqrt(jnp.sum(wide * wide, axis=1, keepdims=True) / width + epsilon)
            gn = g_norm[rows, :] * norm_gain[...]
            row_dot = jnp.sum(gn * wide, axis=1, keepdims=True)
            grad[rows, :] = (
                cot[rows, :].astype(f32) + gn * scale - wide * (scale * scale * scale * row_dot / width)
            )


def collect_kernel(picks, arrived, up_out, down_out, down_in, up_in):
    dp, tp, rows, _ = arrived.shape
    rank = rows // 4
    for b in range(up_out.shape[0]):
        total = jnp.zeros(arrived.shape[2:], f32)
        for d in range(dp):
            one = arrived[d, 0].astype(f32)
            for t in range(1, tp):
                one = one + arrived[d, t].astype(f32)
            total = total + jnp.where(picks[d] == b, one, 0.0)
        up_out[b] = total[:rank, : up_out.shape[2]]
        down_out[b] = total[rank : 2 * rank].T[: down_out.shape[1]]
        down_in[b] = total[2 * rank : 3 * rank, : down_in.shape[2]]
        up_in[b] = total[3 * rank :].T[: up_in.shape[1]]


def up(x):
    n = lax.axis_size("tensor")
    return lax.ppermute(x, "tensor", [(i, i + 1) for i in range(n - 1)])


def down(x):
    n = lax.axis_size("tensor")
    return lax.ppermute(x, "tensor", [(i + 1, i) for i in range(n - 1)])


def around_tensor(x):
    n = lax.axis_size("tensor")
    return [x] + [lax.ppermute(x, "tensor", [(i, (i + s) % n) for i in range(n)]) for s in range(1, n)]


def swap(x, bit):
    n = lax.axis_size("dp")
    return lax.ppermute(x, "dp", [(i, i ^ (1 << bit)) for i in range(n)])


def all_dp(x):
    count = lax.axis_size("dp").bit_length() - 1
    cur = x.reshape((1,) * count + x.shape)
    for bit in list(range(1, count)) + [0]:
        cur = jnp.concatenate([cur, swap(cur, bit)], axis=count - 1 - bit)
    return cur.reshape((-1,) + x.shape)


def joined_with(x, axis, bit):
    n = lax.axis_size(axis)
    return jnp.concatenate([x, lax.ppermute(x, axis, [(i, i ^ (1 << bit)) for i in range(n)])])


def after(x, *events):
    return lax.optimization_barrier((x, events))[0]


def spread_dp(rotated, events):
    out = []
    curs = [after(jnp.stack(rotated[2 * j : 2 * j + 2]), *events) for j in range(2)]
    firsts = [swap(cur, 1 + j) for j, cur in enumerate(curs)]
    pairs = [jnp.stack([cur, first]) for cur, first in zip(curs, firsts)]
    fars = [swap(pair, 2 - j) for j, pair in enumerate(pairs)]
    for pair, far in zip(pairs, fars):
        out += [pair, far, swap(pair, 0), swap(far, 0)]
    return out, firsts


def gather_plain(x):
    n, tp = lax.axis_size("dp"), lax.axis_size("tensor")
    whole = lax.all_gather(x, ("dp", "tensor")).reshape((n, tp) + x.shape)
    return [whole.transpose(1, 0, 2, 3).reshape(tp, n * x.shape[0], x.shape[1])]


def pad_lanes(x):
    return jnp.pad(x, ((0, 0), (0, lanes - x.shape[1])))


def shards(
    tokens,
    cotangent,
    doc_ids,
    adapter_pick,
    norm_gain,
    gate_x_weight,
    bc_weight,
    dt_weight,
    conv_x_weight,
    conv_bc_weight,
    conv_x_bias,
    conv_bc_bias,
    dt_bias,
    a_log,
    skip_gain,
    inner_gain,
    out_weight,
    in_down,
    in_up,
    out_down,
    out_up,
):
    dp_size, tp_size = lax.axis_size("dp"), lax.axis_size("tensor")
    both = ("dp", "tensor")
    seq_count, own, width = tokens.shape
    assert seq_count == 1 and width == 8 * lanes
    group = gate_x_weight.shape[2]
    inner = group * tp_size
    part = dt_weight.shape[1]
    heads = part * tp_size
    head_size = inner // heads
    assert head_size * 2 == lanes
    state = bc_weight.shape[1] // 2
    rank = in_down.shape[2]
    adapters = in_down.shape[0]
    hops = min(1 + (doc_most - 2) // own, tp_size - 1)
    blocks = own // chunk
    d_rows = gate_x_weight.shape[0]
    p_part = in_up.shape[4]
    hp = part * p_part
    mine, place_at = lax.axis_index("dp"), lax.axis_index("tensor")
    by_exchange = dp_size == 8 and tp_size == 4 and d_rows == lanes
    cot, tok = cotangent[0], tokens[0]

    local_x, local_z, local_out = gate_x_weight[:, 1], gate_x_weight[:, 0], out_weight.T
    if by_exchange:
        ring_x = around_tensor(local_x)

    cuts = [d_rows, d_rows, adapters * 2 * rank, adapters * 2 * rank, 16, 16]
    starts = [sum(cuts[:n]) for n in range(len(cuts))]
    if by_exchange:
        small_in = [
            bc_weight, dt_weight.T, in_down.transpose(0, 2, 1), out_up,
            in_up.transpose(0, 2, 3, 4, 1).reshape(adapters, 2 * hp, rank), out_down.reshape(adapters, hp, rank),
        ]
        vmem = pl.BlockSpec(memory_space=pltpu.VMEM)
        small = pl.pallas_call(
            pack_kernel,
            name="pack_kernel",
            out_shape=jax.ShapeDtypeStruct((sum(cuts), lanes), bf16),
            in_specs=[vmem] * 6 + [pl.BlockSpec(memory_space=pltpu.SMEM)],
            out_specs=vmem,
        )(*small_in, adapter_pick)
    else:
        small = [
            bc_weight[:, :state],
            bc_weight[:, state:],
            jnp.concatenate([in_down.transpose(0, 2, 1), out_up], axis=1).reshape(-1, d_rows),
            jnp.concatenate(
                [in_up.reshape(adapters, rank, 2 * hp),
                 jnp.pad(out_down.reshape(adapters, hp, rank).transpose(0, 2, 1), ((0, 0), (0, 0), (0, hp)))],
                axis=1,
            ).reshape(-1, 2 * hp),
            jnp.pad(dt_weight.T, ((0, 16 - part), (0, 0))),
            jnp.broadcast_to(adapter_pick.astype(bf16)[:, None], (16, lanes)),
        ]
        small = lax.all_gather(jnp.concatenate([pad_lanes(x) for x in small]), "dp")
    if by_exchange:
        natural = jnp.arange(8) ^ mine
    else:
        natural, small_at = jnp.asarray(np.argsort(korder)), jnp.arange(8)

    last = tok[-edge:].astype(f32)
    last_scale = lax.rsqrt(jnp.mean(last * last, axis=1, keepdims=True) + epsilon)
    halo_in = up((last * last_scale * norm_gain).astype(bf16))

    heads_row = jnp.pad(jnp.concatenate([dt_bias, a_log])[None], ((0, 0), (0, group - 2 * part)))
    params = jnp.concatenate(
        [conv_x_weight, conv_x_bias[None], inner_gain[None], jnp.repeat(skip_gain, head_size)[None], heads_row]
    )

    if by_exchange:
        params = jnp.stack(around_tensor(params))
        small = joined_with(joined_with(small[None], "dp", 1), "dp", 2)
        small = jnp.concatenate([small, swap(small, 0)])
        w_x, near_x = spread_dp(ring_x, [])
        ring_z = around_tensor(after(local_z, *ring_x[1:]))
        w_z, near_z = spread_dp(ring_z, near_x)
        small_at = jnp.asarray(np.argsort(korder))[natural]
    else:
        w_x, w_z, w_out = gather_plain(local_x), gather_plain(local_z), gather_plain(local_out)
        params = jnp.stack(around_tensor(params))
    pick = adapter_pick[0]
    taken = [small[:, a : a + c] for a, c in zip(starts, cuts)]
    picks = taken[5][:, 0, 0].astype(jnp.int32)
    inner_t = lax.dynamic_slice_in_dim(taken[3], pick * 2 * rank, 2 * rank, 1)
    dt_own = taken[4][:, :part]
    if by_exchange:
        picks, dt_own = picks[small_at], dt_own[small_at]
    if d_rows != lanes:
        fold = lanes // d_rows

        def rows_first(x):
            return x.reshape(8, fold * d_rows, lanes)

        def lanes_last(x):
            x = x[:, :, :d_rows].reshape(8, fold, x.shape[1], d_rows)
            return x.transpose(0, 2, 1, 3).reshape(8, -1, lanes)

        small = jnp.concatenate([rows_first(taken[0]), rows_first(taken[1]), lanes_last(taken[2])], 1)
        dt_own = lanes_last(dt_own)
    dt_own = dt_own.transpose(1, 0, 2).reshape(part, width)
    inner_rows = inner_t.reshape(-1, lanes)
    dt_rows = dt_own.reshape(-1, lanes)
    ring = jnp.concatenate([inner_rows, dt_rows])
    ring = around_tensor(ring)
    if by_exchange:
        ring_out = around_tensor(after(local_out, *ring[1:], *ring_z[1:]))
        w_out, _ = spread_dp(ring_out, near_z)
    ring = jnp.stack(ring)
    inner_t = ring[:, : inner_rows.shape[0]].reshape(tp_size, dp_size, 2 * rank, lanes)
    dt_t = ring[:, inner_rows.shape[0] :]
    dt_t = dt_t.reshape(heads, width)

    docs = doc_ids[0]
    padded = jnp.concatenate([jnp.full((4,), -1, jnp.int32), docs, jnp.full((4,), -2, jnp.int32)])
    near = lax.dynamic_slice_in_dim(padded, place_at * own, own + 8)
    segs = jnp.stack([near[1 + k : 1 + k + own] for k in range(7)]).astype(f32).reshape(7, blocks, chunk)
    bounds = jnp.stack([near[3 : 3 + own : chunk], near[3 + chunk :: chunk][:blocks]], axis=1).reshape(-1)
    groups = (place_at - jnp.arange(tp_size)) % tp_size
    sel = jnp.concatenate([natural, groups, jnp.arange(tp_size), pick[None], bounds, small_at]).astype(jnp.int32)

    def spread(width_each, copies):
        out = np.zeros((lanes, heads * width_each), np.float32)
        at = np.arange(heads * width_each)
        for n in range(copies):
            out[n * heads + at // width_each, at] = 1.0
        return jnp.asarray(out, bf16)

    ex, exl = spread(head_size, 2), spread(lanes, 3)
    red = jnp.asarray(np.arange(inner)[:, None] // head_size == np.arange(lanes)[None, :], bf16)
    at = np.arange(group)
    place = np.zeros((dp_size, hp, group), np.float32)
    place[at % head_size // p_part, at // head_size * p_part + at % p_part, at] = 1.0
    order = jnp.asarray(place.reshape(group, group).T, bf16)
    place = jnp.asarray(place, bf16)

    def full(*shape):
        return pl.BlockSpec(shape, lambda *s: (0,) * len(shape))

    def cols(rows, size=group, turn=0):
        return pl.BlockSpec((rows, size), lambda g, *s: (0, (g + turn) % tp_size))

    def stacked(*shape, base=0):
        return pl.BlockSpec((1,) + shape, lambda g, *s: (g + base,) + (0,) * len(shape))

    def params_at(base=0):
        return stacked(8, group, base=base)

    def weight_specs(ws, half=None):
        if len(ws) == 1:
            base = (half or 0) * tp_size // 2
            return [pl.BlockSpec((1,) + ws[0].shape[1:], lambda g, s: (s[8 + base + g], 0, 0))]
        shape = (2, 1) + ws[0].shape[2:]
        if half is not None:
            return [pl.BlockSpec(shape, lambda g, *s: (0, g, 0, 0))] * 4
        first = pl.BlockSpec(shape, lambda g, *s: (0, jnp.minimum(g, 1), 0, 0))
        second = pl.BlockSpec(shape, lambda g, *s: (0, jnp.maximum(g - 2, 0), 0, 0))
        return [first] * 4 + [second] * 4

    def call(kernel, out, in_specs, out_specs, scratch, flops, moved, steps=tp_size, fill=(), grant=vmem_bytes):
        kernel, kernel_takes_sel, name = kernel

        def body(sel_ref, *refs):
            refs = refs[: len(in_specs)] + refs[len(in_specs) + len(fill) :]
            return kernel(sel_ref, *refs) if kernel_takes_sel else kernel(*refs)

        return pl.pallas_call(
            body,
            name=name,
            input_output_aliases={1 + len(in_specs) + i: to for i, to in enumerate(fill)},
            out_shape=[jax.ShapeDtypeStruct(s, d) for s, d in out],
            grid_spec=pltpu.PrefetchScalarGridSpec(
                num_scalar_prefetch=1,
                grid=steps if isinstance(steps, tuple) else (steps,),
                in_specs=in_specs + [pl.BlockSpec(memory_space=pl.ANY)] * len(fill),
                out_specs=out_specs,
                scratch_shapes=scratch,
            ),
            compiler_params=pltpu.CompilerParams(
                dimension_semantics=("arbitrary",) * (len(steps) if isinstance(steps, tuple) else 1),
                vmem_limit_bytes=grant,
            ),
            cost_estimate=pl.CostEstimate(flops=flops, bytes_accessed=moved, transcendentals=0),
        )

    def plain(kernel, **static):
        return (lambda *refs: kernel(*refs, **static)), False, kernel.__name__

    def selecting(kernel, **static):
        return (lambda *refs: kernel(*refs, **static)), True, kernel.__name__

    n_w = len(w_x)
    big = (own, inner)
    ext = own + edge
    mat = 2 * own * width * inner
    mega = 1 << 20
    params_bc = jnp.concatenate([conv_bc_weight, conv_bc_bias[None], jnp.zeros((3, 2 * state), f32)])
    prep_out = [
        ((ext, width), bf16), ((own, width), bf16), ((ext, 2 * rank), bf16), ((own, 2 * rank), bf16),
        ((own, 6 * lanes), bf16), ((own, 2 * state), bf16),
        ((2 * state, own), bf16), ((2, blocks, chunk, chunk), f32), ((own, 2 * state + lanes), f32),
        ((tp_size, blocks, part, chunk), f32), ((8, inner), f32), ((5 * rank, inner), bf16),
        ((2 * rank, width), bf16), ((width, 2 * state), bf16), ((6, own, lanes), f32),
    ]
    prep_in = [tok, halo_in, norm_gain[None], small, dt_t, inner_t, place, params, params_bc, segs, ex]
    normed_moved, normed, ranks, ranks_own, tables, bc, bc_t, scores, rows_f32, cums_t, keep, ups, wides, w_bc, masks = call(
        selecting(prep_kernel, rank=rank, state=state, moved_blocks=by_exchange),
        prep_out,
        [full(*x.shape) for x in prep_in],
        [full(*s) for s, _ in prep_out],
        [pltpu.VMEM((ext, width), bf16)],
        mat // 4, 6 * mega, 1, grant=vmem_bytes * 5 // 4,
    )(sel, *prep_in)

    def part_at(row, col, *shape):
        return pl.BlockSpec(shape, lambda *s: (row, col))

    def up_at(row, rows, base=0):
        return pl.BlockSpec((rows, group), lambda g, *s: (row, g + base))

    def first_at(row, *shape):
        return pl.BlockSpec(shape, lambda g, *s: (row,) + (0,) * (len(shape) - 1))

    scores_spec, allowed_spec = (first_at(n, 1, blocks, chunk, chunk) for n in range(2))
    b_t_spec, c_t_spec = part_at(0, 0, state, own), part_at(1, 0, state, own)
    masks_spec, masks_after_spec = first_at(0, 3, own, lanes), first_at(1, 3, own, lanes)
    ad_spec, b_up_spec = part_at(0, 0, rank, width), part_at(1, 0, rank, width)
    chunk_rows = stacked(blocks, part, chunk)
    z_specs = weight_specs(w_z)
    p_spec = params_at()
    order_spec = full(group, group)
    u, scaled, sent_state = call(
        plain(proj_kernel, weights=n_w),
        [(big, f32), (big, bf16), ((state, inner), bf16)],
        [full(ext, width)] + weight_specs(w_x)
        + [full(ext, 2 * rank), up_at(1, 2 * rank), p_spec, masks_spec, part_at(0, 0, own, 2 * lanes), cols(lanes),
           b_t_spec],
        [cols(own), cols(own), cols(state)],
        [pltpu.VMEM((ext, group), f32), pltpu.VMEM((own, group), bf16)],
        mat, 12 * mega, grant=vmem_bytes * 5 // 4,
    )(sel, normed_moved, *w_x, ranks, ups, params, masks, tables, ex, bc_t)

    def chain(x, step, sign, *events):
        out, moved = [step(x)], x
        for hop in range(1, hops):
            kept = jnp.roll(keep[7:8], sign * hop * group, axis=1)
            moved = (after(out[-1], *events).astype(f32) * kept).astype(bf16)
            out.append(step(moved))
        return out, moved

    within_specs = [cols(own), part_at(0, 5, own, lanes), chunk_rows, scores_spec, cols(lanes, part * lanes)]
    (y_within,) = call(
        plain(within_kernel), [(big, f32)], within_specs, [cols(own)], [], mat, 6 * mega
    )(sel, scaled, tables, cums_t, scores, exl)
    states_in, _ = chain(sent_state, up, -1, y_within)

    states_spec = pl.BlockSpec((blocks, state, group), lambda g, *s: (0, 0, g))
    def steps_in(phase, first, then):
        return lambda p, g: jnp.where(p == phase, g, jnp.where(p < phase, first, then))

    def moving(phase, make):
        at = steps_in(phase, 0, tp_size - 1)
        return lambda p, g, s: make(at(p, g), s)

    def cols_in(phase, rows, size=group, turn=0):
        return pl.BlockSpec((rows, size), moving(phase, lambda i, s: (0, (i + turn) % tp_size)))

    def up_in(phase, row, rows):
        return pl.BlockSpec((rows, group), moving(phase, lambda i, s: (row, i)))

    def weights_in(phase, ws):
        if len(ws) == 1:
            return [pl.BlockSpec((1,) + ws[0].shape[1:], moving(phase, lambda i, s: (s[8 + i], 0, 0)))]
        shape = (2, 1) + ws[0].shape[2:]
        first = pl.BlockSpec(shape, moving(phase, lambda i, s: (0, jnp.minimum(i, 1), 0, 0)))
        second = pl.BlockSpec(shape, moving(phase, lambda i, s: (0, jnp.maximum(i - 2, 0), 0, 0)))
        return [first] * 4 + [second] * 4

    def cols_always(rows, size):
        return pl.BlockSpec((rows, size), lambda p, g, s: (0, g))

    sent_shape = (dp_size, tp_size, 2 * rank, max(d_rows, 2 * hp))
    cot = cotangent[0]
    big3 = (tp_size, own, group)
    y, states, mixed, sent_out, g_heads, low_z, sent_grad = call(
        selecting(middle_kernel, weights=n_w, hops=hops, inner=inner),
        [(big, f32), ((blocks, state, inner), bf16), ((own, width), f32), (sent_shape, bf16), (big, f32), (big, bf16),
         ((state, inner), bf16)],
        [full(ext, width)] + weights_in(0, w_z) + weights_in(1, w_out)
        + [cols_in(0, state, group, -h) for h in range(1, hops + 1)]
        + [full(own, 2 * rank), up_in(0, 0, 2 * rank), pl.BlockSpec((1, 8, group), lambda p, g, s: (g, 0, 0)),
           cols_in(0, own), cols_in(0, own), cols_in(0, own), part_at(0, 1, own, 2 * lanes),
           part_at(0, 4, own, lanes), cols_in(0, 8), cols_always(lanes, group), b_t_spec, c_t_spec,
           part_at(0, 1, own, state), full(own, width), full(own, width), b_up_spec, up_in(1, 4, rank), order_spec],
        [cols_in(0, own), pl.BlockSpec((blocks, state, group), moving(0, lambda i, s: (0, 0, i))), full(own, width),
         full(*sent_shape), cols_in(2, own), cols_in(2, own), cols_in(2, state)],
        [pltpu.VMEM(big3, f32), pltpu.VMEM(big3, f32), pltpu.VMEM(big3, f32), pltpu.VMEM(big3, f32),
         pltpu.VMEM((own, lanes), f32), pltpu.VMEM((own, lanes), f32), pltpu.VMEM((own, width), f32),
         pltpu.VMEM((own, width), bf16), pltpu.VMEM((own, rank), f32), pltpu.VMEM((own, rank), f32),
         pltpu.VMEM((own, group), bf16)],
        4 * mat, 40 * mega, (3, tp_size), grant=vmem_bytes * 5 // 4,
    )(sel, normed_moved, *w_z, *w_out, *states_in, ranks_own, ups, params, y_within, u, scaled, tables, tables, keep,
      ex, bc_t, bc_t, bc, cot, tok, wides, ups, order)
    red_spec = pl.BlockSpec((group, lanes), lambda g, *s: (g, 0))
    d_within, d_scores, ahead = call(
        plain(back_within_kernel),
        [(big, f32), ((blocks, chunk, chunk), f32), ((own, lanes), f32)],
        [cols(own), cols(own)] + within_specs + [red_spec],
        [cols(own), full(blocks, chunk, chunk), full(own, lanes)],
        [pltpu.VMEM((chunk, group), f32)],
        2 * mat, 14 * mega, grant=vmem_bytes * 5 // 4,
    )(sel, g_heads, y, scaled, tables, cums_t, scores, exl, red)
    grads_in, moved_grad = chain(sent_grad, down, 1, ahead)
    low_z = after(low_z, moved_grad)

    acc_z, g_rank_z, p_up_z = call(
        plain(in_z_kernel, weights=n_w),
        [((own, width), f32), ((own, rank), f32), ((tp_size, rank, group), f32)],
        [cols(own)] + z_specs + [up_at(0, rank), full(own, 2 * rank)],
        [full(own, width), full(own, rank), stacked(rank, group)],
        [],
        mat, 8 * mega,
    )(sel, low_z, *w_z, ups, ranks_own)

    grads_in = [after(x, acc_z) for x in grads_in]
    edges_shape = (edge, inner + 2 * state)
    g_u, g_u_bc, low_dt, edges = call(
        plain(back_state_kernel, hops=hops),
        [(big, f32), ((own, 2 * state), f32), ((own, heads), bf16), (edges_shape, bf16)],
        [cols(state, group, h) for h in range(1, hops + 1)]
        + [states_spec, cols(own), cols(own), cols(own), cols(own), p_spec, full(own, 2 * state), c_t_spec,
           part_at(0, 0, own, 4 * lanes), cols(8), part_at(0, 0, 8, lanes), cols(lanes), red_spec,
           full(blocks, chunk, chunk), full(own, lanes), allowed_spec, full(own, 2 * state + lanes)],
        [cols(own), full(own, 2 * state), full(own, heads), full(*edges_shape)],
        [pltpu.VMEM((own, state), f32), pltpu.VMEM((own, state), f32), pltpu.VMEM((own, lanes), f32),
         pltpu.VMEM((own, lanes), f32), pltpu.VMEM((8, lanes), f32)],
        mat, 24 * mega,
    )(sel, *grads_in, states, g_heads, scaled, d_within, u, params, bc, bc_t, tables, keep, keep, ex, red, d_scores,
      ahead, scores, rows_f32)

    halo = down(edges)
    low_x, g_rank, sent_in = call(
        selecting(in_x_kernel),
        [(big, bf16), ((own, rank), f32), (sent_shape, bf16)],
        [cols(own), cols(edge, group, 1), up_at(2, rank), full(own, 2 * rank), p_spec, masks_after_spec,
         full(own, rank), stacked(rank, group), order_spec, full(own, width)],
        [cols(own), full(own, rank), full(*sent_shape)],
        [],
        mat // 8, 8 * mega,
    )(sel, g_u, halo, ups, ranks_own, params, masks, g_rank_z, p_up_z, order, normed)

    (tokens_grad,) = call(
        selecting(tokens_kernel, weights=n_w),
        [((own, width), f32)],
        [cols(own)] + weight_specs(w_x)
        + [full(own, width), full(own, rank), full(own, 2 * state),
           pl.BlockSpec((edge, 2 * state), lambda g, *s: (0, inner // (2 * state))),
           full(8, 2 * state), full(width, 2 * state), full(own, heads), full(heads, width), ad_spec,
           masks_after_spec, full(own, width), full(own, width), full(1, width)],
        [full(own, width)],
        [pltpu.VMEM((own, width), f32), pltpu.VMEM((own, 2 * state), bf16), pltpu.VMEM((own, width), f32)],
        mat, 14 * mega, grant=vmem_bytes * 5 // 4,
    )(sel, low_x, *w_x, acc_z, g_rank, g_u_bc, halo, params_bc, w_bc, low_dt, dt_t, wides, masks, tok, cot,
      norm_gain[None])

    sent = jnp.concatenate([sent_out, sent_in], axis=2)
    arrived = lax.all_to_all(sent.reshape((-1,) + sent.shape[2:]), both, 0, 0, tiled=True)
    arrived = arrived.reshape(sent.shape)
    shapes = [(adapters, rank, d_rows), (adapters, hp, rank), (adapters, rank, d_rows), (adapters, 2 * hp, rank)]
    grad_out_up, grad_out_down, grad_in_down, grad_in_up = call(
        selecting(collect_kernel), [(s, f32) for s in shapes], [full(*sent.shape)],
        [full(*s) for s in shapes], [], mega, mega, 1,
    )(picks, arrived)

    grad_out_down = grad_out_down.reshape(out_down.shape)
    grad_in_down = grad_in_down.transpose(0, 2, 1)
    grad_in_up = grad_in_up.reshape(adapters, 2, part, p_part, rank).transpose(0, 4, 1, 2, 3)
    return (mixed[None], tokens_grad[None], grad_in_down, grad_in_up, grad_out_down, grad_out_up)


def solution(mesh):
    placed = (
        P("dp", "tensor", None),
        P("dp", "tensor", None),
        P("dp", None),
        P("dp"),
        P(),
        P("dp", None, "tensor"),
        P("dp", None),
        P("dp", "tensor"),
        P(None, "tensor"),
        P(),
        P("tensor"),
        P(),
        P("tensor"),
        P("tensor"),
        P("tensor"),
        P("tensor"),
        P("tensor", "dp"),
        P(None, "dp", None),
        P(None, None, None, "tensor", "dp"),
        P(None, "tensor", "dp", None),
        P(None, None, "dp"),
    )
    return jax.shard_map(
        shards,
        mesh=mesh,
        in_specs=placed,
        out_specs=(
            P("dp", "tensor", None),
            P("dp", "tensor", None),
            P(None, "dp", None),
            P(None, None, None, "tensor", "dp"),
            P(None, "tensor", "dp", None),
            P(None, None, "dp"),
        ),
        check_vma=False,
    )
```

time: 405 us -> 271 us (0.67); the launches traced: 397 us -> 270 us
  local copies, waits for them, and re-layouts: 92.7 us -> 17.5 us
  other arithmetic: 73.1 us -> 15.4 us
  Pallas kernels: 108 us -> 128 us
  starting transfers between devices: 81.5 us -> 61.8 us
  waiting for transfers between devices: 30.3 us -> 45.5 us
  matrix products: 5.64 us -> 0 us
    concatenate x34 -> x7, other arithmetic: 35.9 us -> 5.03 us  [the longest x2 2.02 us: joined_with(): jnp.concatenate([x, lax.ppermute(x, axis, [(i, i ^ 1 << bit) for i in ran...]
    pallas_call x9 -> x11, Pallas kernels: 108 us -> 128 us  [the longest x1 37 us: shards(): call(selecting(middle_kernel, weights=n_w, hops=hops, inner=inner), [(big...]
    unnamed x275 -> x129, local copies, waits for them, and re-layouts: 25.4 us -> 7.19 us
    all_to_all x3 -> x1, starting transfers between devices: 21.5 us -> 6.64 us  [shards(): lax.all_to_all(sent.reshape((-1,) + sent.shape[2:]), both, 0, 0, tiled=True)]
    convert_element_type x14 -> x5, other arithmetic: 14.7 us -> 2.62 us  [the longest x1 0.95 us: shards(): picks = taken[5][:, 0, 0].astype(jnp.int32)]
    transpose x8 -> x1, local copies, waits for them, and re-layouts: 12 us -> 0.01 us  [shards(): dt_own = dt_own.transpose(1, 0, 2).reshape(part, width)]
    concatenate x10 -> x2, local copies, waits for them, and re-layouts: 12.7 us -> 0.69 us  [the longest x1 0.61 us: shards(): jnp.concatenate([natural, groups, jnp.arange(tp_size), pick[None], bounds...]
    reshape x18 -> x2, local copies, waits for them, and re-layouts: 12.5 us -> 0.75 us  [the longest x1 0.66 us: shards(): dt_t = dt_t.reshape(heads, width)]
  transfers between devices with their start and end apart: 48 -> 49, of which waited for: 9 -> 11; matrix products, arithmetic and copies ran while one was open for 35% -> 9% of each run, Pallas kernels for 17% -> 24%
where the time goes in v2:
time: 271 us; the launch traced here: 270 us
  Pallas kernels  128 us (47%)
  starting transfers between devices  61.8 us (23%)
  waiting for transfers between devices  45.5 us (17%)
  local copies, waits for them, and re-layouts  17.5 us (6%)
  other arithmetic  15.4 us (6%)
    pallas_call x1, Pallas kernels, shards(): call(selecting(middle_kernel, weights=n_w, hops=hops, inner=inner), [(big...  37 us
    ppermute x25, starting transfers between devices, swap(): return lax.ppermute(x, 'dp', [(i, i ^ 1 << bit) for i in range(n)])  22.9 us
    ppermute x15, starting transfers between devices, around_tensor(): lax.ppermute(x, 'tensor', [(i, (i + s) % n) for i in range(n)])  17.5 us
    pallas_call x1, Pallas kernels, shards(): call(plain(back_state_kernel, hops=hops), [(big, f32), ((own, 2 * state),...  15.6 us
    pallas_call x1, Pallas kernels, shards(): call(plain(back_within_kernel), [(big, f32), ((blocks, chunk, chunk), f32...  14.8 us
    pallas_call x1, Pallas kernels, shards(): call(plain(proj_kernel, weights=n_w), [(big, f32), (big, bf16), ((state,...  12.8 us
    pallas_call x1, Pallas kernels, shards(): call(selecting(tokens_kernel, weights=n_w), [((own, width), f32)], [cols(...  12.2 us
    ppermute x3, waiting for transfers between devices, up(): return lax.ppermute(x, 'tensor', [(i, i + 1) for i in range(n - 1)])  11.6 us
  transfers between devices with their start and end apart: 49, of which 11 were waited for; matrix products, arithmetic and copies ran while one was open for 9% of the time, Pallas kernels for 24%

profile of v2, /device:TPU:1, one launch (start us, length us, event | category | flops | bytes accessed | tf_op | source)
XLA Modules:
  0.0 270.1 jit_solution(3711161747000262004)
XLA Ops:
  2.2 3.2 %collective-permute-start.11 = (bf16[128,512]{1,0:T(8,128)(2,1)S(1)}, bf16[128,512]{1,0:T(8,128)(2,1)S(1)}, u32[]{:S(2)}, u32[]{:S(2)}) collective-permute-start(bf16[128,512]{1,0:T(8,128)(2,1)S(1)} %bitcast.117), channel_id=1, source_target_pairs={{0,2},{1,3},{2,0},{3,1},{4,6},{5,7},{6,4},{7,5},{8,10},{9,11},{10,... | collective-permute-start | bytes 393224 | tf_op jit(solution)/shard_map/ppermute | solution.py:699
  6.7 2.0 collective-permute-start.12
  11.7 1.9 pack_kernel.1
  24.2 4.5 %collective-permute-done.2 = bf16[2,800,128]{2,1,0:T(8,128)(2,1)S(1)} collective-permute-done((bf16[2,800,128]{2,1,0:T(8,128)(2,1)S(1)}, bf16[2,800,128]{2,1,0:T(8,128)(2,1)S(1)}, u32[]{:S(2)}, u32[]{:S(2)}) %collective-permute-start.2) | collective-permute-done | bytes 409632 | tf_op jit(solution)/shard_map/ppermute | solution.py:717
  32.0 3.9 %collective-permute-start.3 = (bf16[4,800,128]{2,1,0:T(8,128)(2,1)}, bf16[4,800,128]{2,1,0:T(8,128)(2,1)}, u32[]{:S(2)}, u32[]{:S(2)}) collective-permute-start(bf16[4,800,128]{2,1,0:T(8,128)(2,1)} %pad_maximum_fusion.1), channel_id=1, source_target_pairs={{0,4},{4,0},{8,12},{12,8},{16,20},{20,16},{24,28},{28,24},{1,5},{5... | collective-permute-start | bytes 2457608 | tf_op jit(solution)/shard_map/ppermute | solution.py:704
  37.8 1.8 collective-permute-start.20
  42.6 6.3 %collective-permute-done.20 = bf16[128,512]{1,0:T(8,128)(2,1)S(1)} collective-permute-done((bf16[128,512]{1,0:T(8,128)(2,1)S(1)}, bf16[128,512]{1,0:T(8,128)(2,1)S(1)}, u32[]{:S(2)}, u32[]{:S(2)}) %collective-permute-start.20) | collective-permute-done | bytes 131104 | tf_op jit(solution)/shard_map/ppermute | solution.py:699
  56.2 1.6 collective-permute-start.4
  57.8 1.7 collective-permute-start.6
  59.5 1.9 pad_maximum_fusion.3.refs_5_
  63.7 4.5 %collective-permute-done.37.refs_2_ = bf16[2,2,128,512]{3,2,1,0:T(8,128)(2,1)} collective-permute-done((bf16[2,2,128,512]{3,2,1,0:T(8,128)(2,1)S(1)}, bf16[2,2,128,512]{3,2,1,0:T(8,128)(2,1)}, u32[]{:S(2)}, u32[]{:S(2)}) %collective-permute-start.37) | collective-permute-done | bytes 524320 | tf_op jit(solution)/shard_map/ppermute | solution.py:704
  68.2 1.7 collective-permute-start.41
  72.5 9.1 %prep_kernel.1 = (bf16[528,1024]{1,0:T(8,128)(2,1)}, bf16[512,1024]{1,0:T(8,128)(2,1)}, bf16[528,32]{1,0:T(8,128)(2,1)}, bf16[512,32]{1,0:T(8,128)(2,1)}, bf16[5...) custom-call(s32[33]{0:T(128)} %concatenate.42.sel_ref, ...), custom_call_target="tpu_custom_call" | custom-call | flops 536870912 | bytes 6291456 | tf_op jit(solution)/shard_map/prep_kernel/pallas_call | solution.py:972
  85.0 2.7 collective-permute-start.32
  88.5 12.8 %proj_kernel.1 = (f32[512,2048]{1,0:T(8,128)}, bf16[512,2048]{1,0:T(8,128)(2,1)}, bf16[128,2048]{1,0:T(8,128)(2,1)}) custom-call(s32[33]{0:T(128)} %concatenate.42.sel_ref, bf16[528,1024]{1,0:T(8,128)(2,1)} %get-tuple-element.59.refs_0_, bf16[2,2,128,512]{3,2,1,0:T(8,128)(2,1)} %copy-done.36, bf16[2,2,128,512]{3,2,1,0:T(8,128)(2,1)} %collective-permute-done.37.refs_2_, ...), custom_call_target="tpu_custom_call" | custom-call | flops 2147483648 | bytes 12582912 | tf_op jit(solution)/shard_map/proj_kernel/pallas_call | solution.py:998
  101.3 1.9 collective-permute-start.24
  103.2 2.6 collective-permute-start.43
  109.1 4.3 %collective-permute-done.33 = bf16[2,128,512]{2,1,0:T(8,128)(2,1)S(1)} collective-permute-done((bf16[2,128,512]{2,1,0:T(8,128)(2,1)S(1)}, bf16[2,128,512]{2,1,0:T(8,128)(2,1)S(1)}, u32[]{:S(2)}, u32[]{:S(2)}) %collective-permute-start.33) | collective-permute-done | bytes 262176 | tf_op jit(solution)/shard_map/ppermute | solution.py:704
  115.4 1.7 collective-permute-done.43.refs_17_
  119.6 6.1 %within_kernel.1.refs_22_ = f32[512,2048]{1,0:T(8,128)} custom-call(s32[33]{0:T(128)S(1)} %copy-done.27, bf16[512,2048]{1,0:T(8,128)(2,1)S(1)} %copy-done.1, bf16[512,768]{1,0:T(8,128)(2,1)S(1)} %copy-done.2, f32[4,4,8,128]{3,2,1,0:T(8,128)S(1)} %copy-done.26, f32[2,4,128,128]{3,2,1,0:T(8,128)S(1)} %copy-done.5, bf16[128,4096]{1,0:T(8,128)(2,1)S(1)} %copy-done.10), custom_call_target="tpu_custom_call" | custom-call | flops 2147483648 | bytes 6291456 | tf_op jit(solution)/shard_map/within_kernel/pallas_call | solution.py:1018
  127.9 4.3 %collective-permute-start.44 = (bf16[128,2048]{1,0:T(8,128)(2,1)S(1)}, bf16[128,2048]{1,0:T(8,128)(2,1)S(1)}, u32[]{:S(2)}, u32[]{:S(2)}) collective-permute-start(bf16[128,2048]{1,0:T(8,128)(2,1)S(1)} %multiply_convert_fusion.1), channel_id=1, source_target_pairs={{0,1},{1,2},{2,3},{4,5},{5,6},{6,7},{8,9},{9,10},{10,11},{12,13},{... | collective-permute-start | bytes 1572872 | tf_op jit(solution)/shard_map/ppermute | solution.py:689
  133.2 9.9 %collective-permute-done.44.refs_18_ = bf16[128,2048]{1,0:T(8,128)(2,1)S(1)} collective-permute-done((bf16[128,2048]{1,0:T(8,128)(2,1)S(1)}, bf16[128,2048]{1,0:T(8,128)(2,1)S(1)}, u32[]{:S(2)}, u32[]{:S(2)}) %collective-permute-start.44) | collective-permute-done | bytes 524320 | tf_op jit(solution)/shard_map/ppermute | solution.py:689
  144.7 37.0 %middle_kernel.1 = (f32[512,2048]{1,0:T(8,128)}, bf16[4,128,2048]{2,1,0:T(8,128)(2,1)}, f32[512,1024]{1,0:T(8,128)}, bf16[8,4,32,128]{3,2,1,0:T(8,128)(2,1)}, f3...) custom-call(s32[33]{0:T(128)} %concatenate.42.sel_ref, ...), custom_call_target="tpu_custom_call" | custom-call | flops 8589934592 | bytes 41943040 | tf_op jit(solution)/shard_map/middle_kernel/pallas_call | solution.py:1051
  183.3 14.8 %back_within_kernel.1 = (f32[512,2048]{1,0:T(8,128)}, f32[4,128,128]{2,1,0:T(8,128)}, f32[512,128]{1,0:T(8,128)}) custom-call(s32[33]{0:T(128)} %concatenate.42.sel_ref, f32[512,2048]{1,0:T(8,128)} %get-tuple-element.84.refs_0_.refs_3_, f32[512,2048]{1,0:T(8,128)} %get-tuple-element.85.refs_1_, ...), custom_call_target="tpu_custom_call" | custom-call | flops 4294967296 | bytes 14680064 | tf_op jit(solution)/shard_map/back_within_kernel/pallas_call | solution.py:1071
  199.7 8.3 %in_z_kernel.1 = (f32[512,1024]{1,0:T(8,128)}, f32[512,16]{1,0:T(8,128)S(1)}, f32[4,16,512]{2,1,0:T(8,128)S(1)}) custom-call(s32[33]{0:T(128)S(1)} %copy-done.28, bf16[512,2048]{1,0:T(8,128)(2,1)} %get-tuple-element.88.refs_0_, bf16[2,2,128,512]{3,2,1,0:T(8,128)(2,1)S(1)} %copy-done.17, bf16[2,2,128,512]{3,2,1,0:T(8,128)(2,1)} %collective-permute-done.17.refs_2_, ...), custom_call_target="tpu_custom_call" | custom-call | flops 2147483648 | bytes 8388608 | tf_op jit(solution)/shard_map/in_z_kernel/pallas_call | solution.py:1082
  208.0 5.9 %collective-permute-done.46.refs_1_ = bf16[128,2048]{1,0:T(8,128)(2,1)S(1)} collective-permute-done((bf16[128,2048]{1,0:T(8,128)(2,1)S(1)}, bf16[128,2048]{1,0:T(8,128)(2,1)S(1)}, u32[]{:S(2)}, u32[]{:S(2)}) %collective-permute-start.46) | collective-permute-done | bytes 524320 | tf_op jit(solution)/shard_map/ppermute | solution.py:694
  214.0 15.6 %back_state_kernel.1 = (f32[512,2048]{1,0:T(8,128)}, f32[512,256]{1,0:T(8,128)S(1)}, bf16[512,32]{1,0:T(8,128)(2,1)S(1)}, bf16[16,2304]{1,0:T(8,128)(2,1)S(1)}) custom-call(s32[33]{0:T(128)S(1)} %copy-done.28, bf16[128,2048]{1,0:T(8,128)(2,1)S(1)} %collective-permute-done.45.refs_0_, bf16[128,2048]{1,0:T(8,128)(2,1)S(1)} %collective-permute-done.46.refs_1_, ...), custom_call_target="tpu_custom_call" | custom-call | flops 2147483648 | bytes 25165824 | tf_op jit(solution)/shard_map/back_state_kernel/pallas_call | solution.py:1093
  232.4 4.4 %collective-permute-done.47.refs_1_.refs_12_ = bf16[16,2304]{1,0:T(8,128)(2,1)S(1)} collective-permute-done((bf16[16,2304]{1,0:T(8,128)(2,1)S(1)}, bf16[16,2304]{1,0:T(8,128)(2,1)S(1)}, u32[]{:S(2)}, u32[]{:S(2)}) %collective-permute-start.47) | collective-permute-done | bytes 73760 | tf_op jit(solution)/shard_map/ppermute | solution.py:694
  236.8 7.7 %in_x_kernel.1 = (bf16[512,2048]{1,0:T(8,128)(2,1)}, f32[512,16]{1,0:T(8,128)S(1)}, bf16[8,4,32,128]{3,2,1,0:T(8,128)(2,1)S(1)}) custom-call(s32[33]{0:T(128)S(1)} %copy-done.28, f32[512,2048]{1,0:T(8,128)} %get-tuple-element.96.refs_0_, bf16[16,2304]{1,0:T(8,128)(2,1)S(1)} %collective-permute-done.47.refs_1_.refs_12_, bf16[80,2048]{1,0:T(8,128)(2,1)S(1)} %copy-done.8, ...), custom_call_target="tpu_custom_call" | custom-call | flops 268435456 | bytes 8388608 | tf_op jit(solution)/shard_map/in_x_kernel/pallas_call | solution.py:1108
  246.1 6.6 %all-to-all-start = ((bf16[32,64,128]{2,1,0:T(8,128)(2,1)}), bf16[32,64,128]{2,1,0:T(8,128)(2,1)S(1)}, u32[]{:S(2)}, u32[]{:S(2)}) async-start(bf16[32,64,128]{2,1,0:T(8,128)(2,1)} %bitcast.72), calls=%async_computation | async-start | bytes 1048576 | tf_op jit(solution)/shard_map/all_to_all | solution.py:1133
  254.3 12.2 %tokens_kernel.1 = f32[512,1024]{1,0:T(8,128)} custom-call(s32[33]{0:T(128)} %concatenate.42.sel_ref, bf16[512,2048]{1,0:T(8,128)(2,1)} %get-tuple-element.101.refs_0_, bf16[2,2,128,512]{3,2,1,0:T(8,128)(2,1)} %copy-done.36, bf16[2,2,128,512]{3,2,1,0:T(8,128)(2,1)} %collective-permute-done.37.refs_2_, ...), custom_call_target="tpu_custom_call" | custom-call | flops 2147483648 | bytes 14680064 | tf_op jit(solution)/shard_map/tokens_kernel/pallas_call | solution.py:1118
  268.0 2.1 collect_kernel.1
  (272 shorter events, 62.8 us)
Async XLA Ops:
  2.2 19.1 %collective-permute-start.11 = (bf16[128,512]{1,0:T(8,128)(2,1)S(1)}, bf16[128,512]{1,0:T(8,128)(2,1)S(1)}, u32[]{:S(2)}, u32[]{:S(2)}) collective-permute-start(bf16[128,512]{1,0:T(8,128)(2,1)S(1)} %bitcast.117), channel_id=1, source_target_pairs={{0,2},{1,3},{2,0},{3,1},{4,6},{5,7},{6,4},{7,5},{8,10},{9,11},{10,... | collective-permute-start | bytes 393224 | tf_op jit(solution)/shard_map/ppermute | solution.py:699
  5.5 16.7 %collective-permute-start.10 = (bf16[128,512]{1,0:T(8,128)(2,1)S(1)}, bf16[128,512]{1,0:T(8,128)(2,1)S(1)}, u32[]{:S(2)}, u32[]{:S(2)}) collective-permute-start(bf16[128,512]{1,0:T(8,128)(2,1)S(1)} %bitcast.118), channel_id=1, source_target_pairs={{0,1},{1,2},{2,3},{3,0},{4,5},{5,6},{6,7},{7,4},{8,9},{9,10},{10,1... | collective-permute-start | bytes 393224 | tf_op jit(solution)/shard_map/ppermute | solution.py:699
  6.7 16.2 %collective-permute-start.12 = (bf16[128,512]{1,0:T(8,128)(2,1)S(1)}, bf16[128,512]{1,0:T(8,128)(2,1)S(1)}, u32[]{:S(2)}, u32[]{:S(2)}) collective-permute-start(bf16[128,512]{1,0:T(8,128)(2,1)S(1)} %bitcast.119), channel_id=1, source_target_pairs={{0,3},{1,0},{2,1},{3,2},{4,7},{5,4},{6,5},{7,6},{8,11},{9,8},{10,9... | collective-permute-start | bytes 393224 | tf_op jit(solution)/shard_map/ppermute | solution.py:699
  11.0 19.7 %collective-permute-start.9 = (f32[8,512]{1,0:T(8,128)S(1)}, f32[8,512]{1,0:T(8,128)S(1)}, u32[]{:S(2)}, u32[]{:S(2)}) collective-permute-start(f32[8,512]{1,0:T(8,128)S(1)} %concatenate.48), channel_id=1, source_target_pairs={{0,3},{1,0},{2,1},{3,2},{4,7},{5,4},{6,5},{7,6},{8,11},{9,8},{10,9... | collective-permute-start | bytes 49160 | tf_op jit(solution)/shard_map/ppermute | solution.py:699
  22.1 15.3 %collective-permute-start.7 = (f32[8,512]{1,0:T(8,128)S(1)}, f32[8,512]{1,0:T(8,128)S(1)}, u32[]{:S(2)}, u32[]{:S(2)}) collective-permute-start(f32[8,512]{1,0:T(8,128)S(1)} %concatenate.48), channel_id=1, source_target_pairs={{0,1},{1,2},{2,3},{3,0},{4,5},{5,6},{6,7},{7,4},{8,9},{9,10},{10,1... | collective-permute-start | bytes 49160 | tf_op jit(solution)/shard_map/ppermute | solution.py:699
  23.0 14.9 %collective-permute-start.13 = (bf16[128,512]{1,0:T(8,128)(2,1)S(1)}, bf16[128,512]{1,0:T(8,128)(2,1)S(1)}, u32[]{:S(2)}, u32[]{:S(2)}) collective-permute-start(bf16[128,512]{1,0:T(8,128)(2,1)S(1)} %bitcast.121), channel_id=1, source_target_pairs={{0,1},{1,2},{2,3},{3,0},{4,5},{5,6},{6,7},{7,4},{8,9},{9,10},{10,1... | collective-permute-start | bytes 393224 | tf_op jit(solution)/shard_map/ppermute | solution.py:699
  32.0 20.2 %collective-permute-start.3 = (bf16[4,800,128]{2,1,0:T(8,128)(2,1)}, bf16[4,800,128]{2,1,0:T(8,128)(2,1)}, u32[]{:S(2)}, u32[]{:S(2)}) collective-permute-start(bf16[4,800,128]{2,1,0:T(8,128)(2,1)} %pad_maximum_fusion.1), channel_id=1, source_target_pairs={{0,4},{4,0},{8,12},{12,8},{16,20},{20,16},{24,28},{28,24},{1,5},{5... | collective-permute-start | bytes 2457608 | tf_op jit(solution)/shard_map/ppermute | solution.py:704
  49.9 12.5 %collective-permute-start.40 = (bf16[2,2,128,512]{3,2,1,0:T(8,128)(2,1)S(1)}, bf16[2,2,128,512]{3,2,1,0:T(8,128)(2,1)}, u32[]{:S(2)}, u32[]{:S(2)}) collective-permute-start(bf16[2,2,128,512]{3,2,1,0:T(8,128)(2,1)S(1)} %pad_maximum_fusion.7.refs_5_), channel_id=1, source_target_pairs={{0,8},{4,12},{8,0},{12,4},{16,24},{20,28},{24,16},{28,20},{1,9},{5... | collective-permute-start | bytes 1572872 | tf_op jit(solution)/shard_map/ppermute | solution.py:704
  50.8 17.4 %collective-permute-start.37 = (bf16[2,2,128,512]{3,2,1,0:T(8,128)(2,1)S(1)}, bf16[2,2,128,512]{3,2,1,0:T(8,128)(2,1)}, u32[]{:S(2)}, u32[]{:S(2)}) collective-permute-start(bf16[2,2,128,512]{3,2,1,0:T(8,128)(2,1)S(1)} %pad_maximum_fusion.6.refs_1_), channel_id=1, source_target_pairs={{0,16},{4,20},{8,24},{12,28},{16,0},{20,4},{24,8},{28,12},{1,17},{... | collective-permute-start | bytes 1572872 | tf_op jit(solution)/shard_map/ppermute | solution.py:704
  56.1 13.8 %collective-permute-start.5 = (bf16[320,128]{1,0:T(8,128)(2,1)S(1)}, bf16[320,128]{1,0:T(8,128)(2,1)S(1)}, u32[]{:S(2)}, u32[]{:S(2)}) collective-permute-start(bf16[320,128]{1,0:T(8,128)(2,1)S(1)} %get-tuple-element.117), channel_id=1, source_target_pairs={{0,2},{1,3},{2,0},{3,1},{4,6},{5,7},{6,4},{7,5},{8,10},{9,11},{10,... | collective-permute-start | bytes 245768 | tf_op jit(solution)/shard_map/ppermute | solution.py:699
  56.2 13.8 %collective-permute-start.4 = (bf16[320,128]{1,0:T(8,128)(2,1)S(1)}, bf16[320,128]{1,0:T(8,128)(2,1)S(1)}, u32[]{:S(2)}, u32[]{:S(2)}) collective-permute-start(bf16[320,128]{1,0:T(8,128)(2,1)S(1)} %get-tuple-element.117), channel_id=1, source_target_pairs={{0,1},{1,2},{2,3},{3,0},{4,5},{5,6},{6,7},{7,4},{8,9},{9,10},{10,1... | collective-permute-start | bytes 245768 | tf_op jit(solution)/shard_map/ppermute | solution.py:699
  57.8 12.7 %collective-permute-start.6 = (bf16[320,128]{1,0:T(8,128)(2,1)S(1)}, bf16[320,128]{1,0:T(8,128)(2,1)S(1)}, u32[]{:S(2)}, u32[]{:S(2)}) collective-permute-start(bf16[320,128]{1,0:T(8,128)(2,1)S(1)} %get-tuple-element.117), channel_id=1, source_target_pairs={{0,3},{1,0},{2,1},{3,2},{4,7},{5,4},{6,5},{7,6},{8,11},{9,8},{10,9... | collective-permute-start | bytes 245768 | tf_op jit(solution)/shard_map/ppermute | solution.py:699
  68.2 16.6 %collective-permute-start.41 = (bf16[2,2,128,512]{3,2,1,0:T(8,128)(2,1)S(1)}, bf16[2,2,128,512]{3,2,1,0:T(8,128)(2,1)}, u32[]{:S(2)}, u32[]{:S(2)}) collective-permute-start(bf16[2,2,128,512]{3,2,1,0:T(8,128)(2,1)S(1)} %pad_maximum_fusion.7.refs_5_), channel_id=1, source_target_pairs={{0,4},{4,0},{8,12},{12,8},{16,20},{20,16},{24,28},{28,24},{1,5},{5... | collective-permute-start | bytes 1572872 | tf_op jit(solution)/shard_map/ppermute | solution.py:704
  69.9 15.1 %collective-permute-start.38 = (bf16[2,2,128,512]{3,2,1,0:T(8,128)(2,1)S(1)}, bf16[2,2,128,512]{3,2,1,0:T(8,128)(2,1)}, u32[]{:S(2)}, u32[]{:S(2)}) collective-permute-start(bf16[2,2,128,512]{3,2,1,0:T(8,128)(2,1)S(1)} %pad_maximum_fusion.6.refs_1_), channel_id=1, source_target_pairs={{0,4},{4,0},{8,12},{12,8},{16,20},{20,16},{24,28},{28,24},{1,5},{5... | collective-permute-start | bytes 1572872 | tf_op jit(solution)/shard_map/ppermute | solution.py:704
  70.0 17.7 %collective-permute-start.42 = (bf16[2,2,128,512]{3,2,1,0:T(8,128)(2,1)}, bf16[2,2,128,512]{3,2,1,0:T(8,128)(2,1)}, u32[]{:S(2)}, u32[]{:S(2)}) collective-permute-start(bf16[2,2,128,512]{3,2,1,0:T(8,128)(2,1)} %collective-permute-done.40.refs_6_), channel_id=1, source_target_pairs={{0,4},{4,0},{8,12},{12,8},{16,20},{20,16},{24,28},{28,24},{1,5},{5... | collective-permute-start | bytes 1572872 | tf_op jit(solution)/shard_map/ppermute | solution.py:704
  70.4 17.3 %collective-permute-start.39 = (bf16[2,2,128,512]{3,2,1,0:T(8,128)(2,1)}, bf16[2,2,128,512]{3,2,1,0:T(8,128)(2,1)}, u32[]{:S(2)}, u32[]{:S(2)}) collective-permute-start(bf16[2,2,128,512]{3,2,1,0:T(8,128)(2,1)} %collective-permute-done.37.refs_2_), channel_id=1, source_target_pairs={{0,4},{4,0},{8,12},{12,8},{16,20},{20,16},{24,28},{28,24},{1,5},{5... | collective-permute-start | bytes 1572872 | tf_op jit(solution)/shard_map/ppermute | solution.py:704
  83.3 24.9 %collective-permute-start.23 = (bf16[2,2,128,512]{3,2,1,0:T(8,128)(2,1)}, bf16[2,2,128,512]{3,2,1,0:T(8,128)(2,1)}, u32[]{:S(2)}, u32[]{:S(2)}) collective-permute-start(bf16[2,2,128,512]{3,2,1,0:T(8,128)(2,1)} %pad_maximum_fusion.3.refs_5_), channel_id=1, source_target_pairs={{0,8},{4,12},{8,0},{12,4},{16,24},{20,28},{24,16},{28,20},{1,9},{5... | collective-permute-start | bytes 1572872 | tf_op jit(solution)/shard_map/ppermute | solution.py:704
  84.8 24.2 %collective-permute-start.17 = (bf16[2,2,128,512]{3,2,1,0:T(8,128)(2,1)S(1)}, bf16[2,2,128,512]{3,2,1,0:T(8,128)(2,1)}, u32[]{:S(2)}, u32[]{:S(2)}) collective-permute-start(bf16[2,2,128,512]{3,2,1,0:T(8,128)(2,1)S(1)} %pad_maximum_fusion.2.refs_1_), channel_id=1, source_target_pairs={{0,16},{4,20},{8,24},{12,28},{16,0},{20,4},{24,8},{28,12},{1,17},{... | collective-permute-start | bytes 1572872 | tf_op jit(solution)/shard_map/ppermute | solution.py:704
  85.0 16.3 %collective-permute-start.32 = (bf16[128,512]{1,0:T(8,128)(2,1)S(1)}, bf16[128,512]{1,0:T(8,128)(2,1)S(1)}, u32[]{:S(2)}, u32[]{:S(2)}) collective-permute-start(bf16[128,512]{1,0:T(8,128)(2,1)S(1)} %bitcast.127), channel_id=1, source_target_pairs={{0,3},{1,0},{2,1},{3,2},{4,7},{5,4},{6,5},{7,6},{8,11},{9,8},{10,9... | collective-permute-start | bytes 393224 | tf_op jit(solution)/shard_map/ppermute | solution.py:699
  87.7 15.5 %collective-permute-start.31 = (bf16[128,512]{1,0:T(8,128)(2,1)S(1)}, bf16[128,512]{1,0:T(8,128)(2,1)S(1)}, u32[]{:S(2)}, u32[]{:S(2)}) collective-permute-start(bf16[128,512]{1,0:T(8,128)(2,1)S(1)} %bitcast.128), channel_id=1, source_target_pairs={{0,2},{1,3},{2,0},{3,1},{4,6},{5,7},{6,4},{7,5},{8,10},{9,11},{10,... | collective-permute-start | bytes 393224 | tf_op jit(solution)/shard_map/ppermute | solution.py:699
  87.7 18.1 %collective-permute-start.27 = (bf16[2,128,512]{2,1,0:T(8,128)(2,1)}, bf16[2,128,512]{2,1,0:T(8,128)(2,1)S(1)}, u32[]{:S(2)}, u32[]{:S(2)}) collective-permute-start(bf16[2,128,512]{2,1,0:T(8,128)(2,1)} %pad_maximum_fusion.17), channel_id=1, source_target_pairs={{0,8},{4,12},{8,0},{12,4},{16,24},{20,28},{24,16},{28,20},{1,9},{5... | collective-permute-start | bytes 786440 | tf_op jit(solution)/shard_map/ppermute | solution.py:704
  101.3 13.4 %collective-permute-start.24 = (bf16[2,2,128,512]{3,2,1,0:T(8,128)(2,1)}, bf16[2,2,128,512]{3,2,1,0:T(8,128)(2,1)S(1)}, u32[]{:S(2)}, u32[]{:S(2)}) collective-permute-start(bf16[2,2,128,512]{3,2,1,0:T(8,128)(2,1)} %pad_maximum_fusion.3.refs_5_), channel_id=1, source_target_pairs={{0,4},{4,0},{8,12},{12,8},{16,20},{20,16},{24,28},{28,24},{1,5},{5... | collective-permute-start | bytes 1572872 | tf_op jit(solution)/shard_map/ppermute | solution.py:704
  103.2 13.9 %collective-permute-start.43 = (bf16[128,2048]{1,0:T(8,128)(2,1)}, bf16[128,2048]{1,0:T(8,128)(2,1)S(1)}, u32[]{:S(2)}, u32[]{:S(2)}) collective-permute-start(bf16[128,2048]{1,0:T(8,128)(2,1)} %get-tuple-element.71), channel_id=1, source_target_pairs={{0,1},{1,2},{2,3},{4,5},{5,6},{6,7},{8,9},{9,10},{10,11},{12,13},{... | collective-permute-start | bytes 1572872 | tf_op jit(solution)/shard_map/ppermute | solution.py:689
  108.2 17.6 %collective-permute-start.18 = (bf16[2,2,128,512]{3,2,1,0:T(8,128)(2,1)S(1)}, bf16[2,2,128,512]{3,2,1,0:T(8,128)(2,1)S(1)}, u32[]{:S(2)}, u32[]{:S(2)}) collective-permute-start(bf16[2,2,128,512]{3,2,1,0:T(8,128)(2,1)S(1)} %pad_maximum_fusion.2.refs_1_), channel_id=1, source_target_pairs={{0,4},{4,0},{8,12},{12,8},{16,20},{20,16},{24,28},{28,24},{1,5},{5... | collective-permute-start | bytes 1572872 | tf_op jit(solution)/shard_map/ppermute | solution.py:704
  109.0 18.9 %collective-permute-start.25 = (bf16[2,2,128,512]{3,2,1,0:T(8,128)(2,1)}, bf16[2,2,128,512]{3,2,1,0:T(8,128)(2,1)}, u32[]{:S(2)}, u32[]{:S(2)}) collective-permute-start(bf16[2,2,128,512]{3,2,1,0:T(8,128)(2,1)} %collective-permute-done.23.refs_6_), channel_id=1, source_target_pairs={{0,4},{4,0},{8,12},{12,8},{16,20},{20,16},{24,28},{28,24},{1,5},{5... | collective-permute-start | bytes 1572872 | tf_op jit(solution)/shard_map/ppermute | solution.py:704
  113.4 14.6 %collective-permute-start.19 = (bf16[2,2,128,512]{3,2,1,0:T(8,128)(2,1)}, bf16[2,2,128,512]{3,2,1,0:T(8,128)(2,1)}, u32[]{:S(2)}, u32[]{:S(2)}) collective-permute-start(bf16[2,2,128,512]{3,2,1,0:T(8,128)(2,1)} %collective-permute-done.17.refs_2_), channel_id=1, source_target_pairs={{0,4},{4,0},{8,12},{12,8},{16,20},{20,16},{24,28},{28,24},{1,5},{5... | collective-permute-start | bytes 1572872 | tf_op jit(solution)/shard_map/ppermute | solution.py:704
  114.7 17.5 %collective-permute-start.34 = (bf16[2,2,128,512]{3,2,1,0:T(8,128)(2,1)S(1)}, bf16[2,2,128,512]{3,2,1,0:T(8,128)(2,1)S(1)}, u32[]{:S(2)}, u32[]{:S(2)}) collective-permute-start(bf16[2,2,128,512]{3,2,1,0:T(8,128)(2,1)S(1)} %pad_maximum_fusion.5.refs_13_), channel_id=1, source_target_pairs={{0,8},{4,12},{8,0},{12,4},{16,24},{20,28},{24,16},{28,20},{1,9},{5... | collective-permute-start | bytes 1572872 | tf_op jit(solution)/shard_map/ppermute | solution.py:704
  117.1 16.0 %collective-permute-start.28 = (bf16[2,2,128,512]{3,2,1,0:T(8,128)(2,1)S(1)}, bf16[2,2,128,512]{3,2,1,0:T(8,128)(2,1)S(1)}, u32[]{:S(2)}, u32[]{:S(2)}) collective-permute-start(bf16[2,2,128,512]{3,2,1,0:T(8,128)(2,1)S(1)} %pad_maximum_fusion.4.refs_9_), channel_id=1, source_target_pairs={{0,16},{4,20},{8,24},{12,28},{16,0},{20,4},{24,8},{28,12},{1,17},{... | collective-permute-start | bytes 1572872 | tf_op jit(solution)/shard_map/ppermute | solution.py:704
  127.9 15.1 %collective-permute-start.44 = (bf16[128,2048]{1,0:T(8,128)(2,1)S(1)}, bf16[128,2048]{1,0:T(8,128)(2,1)S(1)}, u32[]{:S(2)}, u32[]{:S(2)}) collective-permute-start(bf16[128,2048]{1,0:T(8,128)(2,1)S(1)} %multiply_convert_fusion.1), channel_id=1, source_target_pairs={{0,1},{1,2},{2,3},{4,5},{5,6},{6,7},{8,9},{9,10},{10,11},{12,13},{... | collective-permute-start | bytes 1572872 | tf_op jit(solution)/shard_map/ppermute | solution.py:689
  181.7 16.4 %collective-permute-start.45 = (bf16[128,2048]{1,0:T(8,128)(2,1)}, bf16[128,2048]{1,0:T(8,128)(2,1)S(1)}, u32[]{:S(2)}, u32[]{:S(2)}) collective-permute-start(bf16[128,2048]{1,0:T(8,128)(2,1)} %get-tuple-element.82), channel_id=1, source_target_pairs={{1,0},{2,1},{3,2},{5,4},{6,5},{7,6},{9,8},{10,9},{11,10},{13,12},{... | collective-permute-start | bytes 1572872 | tf_op jit(solution)/shard_map/ppermute | solution.py:694
  198.2 15.7 %collective-permute-start.46 = (bf16[128,2048]{1,0:T(8,128)(2,1)S(1)}, bf16[128,2048]{1,0:T(8,128)(2,1)S(1)}, u32[]{:S(2)}, u32[]{:S(2)}) collective-permute-start(bf16[128,2048]{1,0:T(8,128)(2,1)S(1)} %multiply_convert_fusion), channel_id=1, source_target_pairs={{1,0},{2,1},{3,2},{5,4},{6,5},{7,6},{9,8},{10,9},{11,10},{13,12},{... | collective-permute-start | bytes 1572872 | tf_op jit(solution)/shard_map/ppermute | solution.py:694
  246.1 21.9 %all-to-all-start = ((bf16[32,64,128]{2,1,0:T(8,128)(2,1)}), bf16[32,64,128]{2,1,0:T(8,128)(2,1)S(1)}, u32[]{:S(2)}, u32[]{:S(2)}) async-start(bf16[32,64,128]{2,1,0:T(8,128)(2,1)} %bitcast.72), calls=%async_computation | async-start | bytes 1048576 | tf_op jit(solution)/shard_map/all_to_all | solution.py:1133
  (77 other events, 998.4 us)

commit v3 on v2

--- a/solution.py
+++ b/solution.py
@@ -82,13 +82,15 @@
 
 def weight_pieces(refs, at=0):
     if len(refs) == 1:
-        return [refs[0][...].reshape(-1, refs[0].shape[-1])]
-    a01, a23, c01, c23 = (refs[4 * at + j] for j in range(4))
-    if at == 0:
-        parts = [a01[0, 0], a01[1, 0], a23[0, 0], a23[1, 0], c01[0, 0], c01[1, 0], c23[0, 0], c23[1, 0]]
-    else:
-        parts = [a01[0, 0], a23[0, 0], a01[1, 0], a23[1, 0], c01[0, 0], c23[0, 0], c01[1, 0], c23[1, 0]]
-    return [jnp.concatenate(parts[j : j + 2], axis=0) for j in range(0, 8, 2)]
+        return [(refs[0][...].reshape(-1, refs[0].shape[-1]), None)]
+    pairs = ((0, 1), (2, 3), (4, 5), (6, 7)) if at == 0 else ((0, 2), (1, 3), (4, 6), (5, 7))
+    return [
+        (ref[...].reshape(2 * lanes, ref.shape[-1]), pair) for ref, pair in zip(refs[4 * at : 4 * at + 4], pairs)
+    ]
+
+
+def block_at(n):
+    return slice(n * lanes, (n + 1) * lanes)
 
 
 def with_weight(refs, body, half):
@@ -109,19 +111,29 @@
 
 
 def times(left, parts):
-    total, k = None, 0
-    for w in parts:
-        term = dot(left[:, k : k + w.shape[0]], w)
+    total = None
+    for w, pair in parts:
+        if pair is None:
+            value = left(slice(None))
+        elif pair[1] == pair[0] + 1:
+            value = left(slice(pair[0] * lanes, (pair[1] + 1) * lanes))
+        else:
+            value = jnp.concatenate([left(block_at(n)) for n in pair], axis=1)
+        term = dot(value, w)
         total = term if total is None else total + term
-        k += w.shape[0]
     return total
 
 
 def add_times_transposed(acc, low, parts):
-    k = 0
-    for w in parts:
-        acc[:, k : k + w.shape[0]] += dot_nt(low, w)
-        k += w.shape[0]
+    for w, pair in parts:
+        term = dot_nt(low, w)
+        if pair is None:
+            acc[...] += term
+        elif pair[1] == pair[0] + 1:
+            acc[:, pair[0] * lanes : (pair[1] + 1) * lanes] += term
+        else:
+            for i, n in enumerate(pair):
+                acc[:, block_at(n)] += term[:, block_at(i)]
 
 
 def rows_of(c):
@@ -293,7 +305,7 @@
     ranks, a_up, params, masks, tables, ex, b_t, u_out, sc_out, f_out, xs, moved = refs
 
     def body(parts):
-        xs[...] = times(left, parts) + dot(ranks[...], a_up[...])
+        xs[...] = times(lambda at: left[:, at], parts) + dot(ranks[...], a_up[...])
 
     with_weight(ws, body, pl.program_id(0) // 2)
     own, width = u_out.shape
@@ -367,18 +379,19 @@
 def middle_kernel(sel, left, *refs, weights, hops, inner):
     zs, outs, refs = refs[:weights], refs[weights : 2 * weights], refs[2 * weights :]
     s_ins, refs = refs[:hops], refs[hops:]
-    (ranks, a_up, params, yw, u, sc, tables, own_in, keep, ex, b_t, c_t, in_c, cot, tokens, b_up, b_down, order,
-     y_out, states, mixed, sent, gh_out, lz_out, g_out,
-     heads, gate_z, gated, gg, sumsq, dots, acc, cots, g_rank, rank, low) = refs
+    (ranks, a_up, params, yw, u, sc, tables, own_in, keep, ex, b_t, c_t, in_c, cot, tokens, b_up, b_down, order, red,
+     states, mixed, sent, gh_out, lz_out, g_out, ahead,
+     ys, heads, gate_z, gated, gg, sumsq, dots, acc, cots, g_rank, rank, low) = refs
     phase, g = pl.program_id(0), pl.program_id(1)
     last = pl.num_programs(1) - 1
     half = g // 2
-    own, width = y_out.shape
+    own, width = gh_out.shape
     step = min(width, 256)
     blocks = own // chunk
 
     @pl.when((phase == 0) & (g == 0))
     def _():
+        ahead[...] = jnp.zeros_like(ahead)
         sumsq[...] = jnp.zeros_like(sumsq)
         acc[...] = jnp.zeros_like(acc)
         rank[...] = jnp.zeros_like(rank)
@@ -392,7 +405,8 @@
     @pl.when(phase == 0)
     def _():
         def body(parts):
-            gate_z[g] = times(left[left.shape[0] - own :, :], parts) + dot(ranks[...], a_up[...])
+            first = left.shape[0] - own
+            gate_z[g] = times(lambda at: left[first:, at], parts) + dot(ranks[...], a_up[...])
 
         with_weight(zs, body, half)
         for n in range(width // step):
@@ -409,7 +423,7 @@
             for c in range(blocks):
                 rows = rows_of(c)
                 y = yw[rows, cols] + dot(tables[rows, :lanes], ex[:, cols]) * dot(in_c[rows, :], states[c, :, cols])
-                y_out[rows, cols] = y
+                ys[g, rows, cols] = y
                 head = y + params[0, 6:7, cols] * silu(u[rows, cols])
                 heads[g, rows, cols] = head
                 gd = head * silu(gate_z[g, rows, cols])
@@ -432,7 +446,7 @@
         put_inner_parts(sent, sel[8 + g], p_down, order, 0)
 
         def body(parts):
-            value = (times(cots, parts) + dot2(g_rank[...], b_down[...])) * params[0, 5:6, :]
+            value = (times(lambda at: cots[:, at], parts) + dot2(g_rank[...], b_down[...])) * params[0, 5:6, :]
             gg[g] = value
             prod = value * gated[g]
             total = dots[...]
@@ -466,16 +480,17 @@
                 gh = g_gated * gate
                 gh_out[rows, cols] = gh
                 low[rows, cols] = (dot(own_in[rows, :], ex[:, cols]) * gh).astype(bf16)
+                ahead[rows, :] += dot2(ys[g, rows, cols] * gh, red[cols, :])
         g_out[...] = dot(c_t[...], low[...]).astype(bf16)
 
 
-def back_within_kernel(gh, y, sc, cums3, cums_t, scores, exl, red, dv_out, ds_out, ahead, prod):
+def back_within_kernel(gh, ahead_in, sc, cums3, cums_t, scores, exl, red, dv_out, ds_out, ahead, prod):
     g = pl.program_id(0)
 
     @pl.when(g == 0)
     def _():
         ds_out[...] = jnp.zeros_like(ds_out)
-        ahead[...] = jnp.zeros_like(ahead)
+        ahead[...] = ahead_in[...]
 
     own, width = dv_out.shape
     for c in range(own // chunk):
@@ -499,15 +514,23 @@
             lane = lax.broadcasted_iota(jnp.int32, (chunk, lanes), 1)
             dv = jnp.where(lane < lanes // 2, dvb[:chunk], dvb[chunk:])
             dv_out[rows, cols] = dv
-            prod[:, cols] = y[rows, cols] * dy - v.astype(f32) * dv
+            prod[:, cols] = v.astype(f32) * dv
         ds_out[c] += ds
-        ahead[rows, :] += dot2(prod[...], red[...])
+        ahead[rows, :] -= dot2(prod[...], red[...])
+
+
+def conv_back(cur, params, masks, rows, width):
+    total = params[3:4, :] * cur[:chunk]
+    for k in range(1, 4):
+        shifted = pltpu.roll(cur, cur.shape[0] - k, 0)[:chunk]
+        total = total + params[3 - k : 4 - k, :] * (shifted * tile_lanes(masks[k - 1, rows, :], width))
+    return total
 
 
 def back_state_kernel(*refs, hops):
     grads_in, refs = refs[:hops], refs[hops:]
-    (states, gh, sc, dv, u, params, bc, c_t, tables, keep, decays, ex, red, ds, ahead, allowed, rows_in, gu_out, gbc_out,
-     ldt_out, edges, db, dc, behind, direct, carry) = refs
+    (states, gh, sc, dv, u, params, bc, c_t, tables, keep, decays, ex, red, ds, ahead, allowed, rows_in, masks, lx_out, gbc_out,
+     ldt_out, edges, tail, db, dc, behind, direct, carry) = refs
     state = c_t.shape[0]
     g = pl.program_id(0)
 
@@ -516,12 +539,13 @@
         for ref in (db, dc, behind, direct, carry):
             ref[...] = jnp.zeros_like(ref)
 
-    own, width = gu_out.shape
+    own, width = lx_out.shape
     step = min(width, 256)
     blocks = own // chunk
     for n in range(width // step):
         cols = slice(n * step, (n + 1) * step)
         gs = sum(r[:, cols].astype(f32) for r in grads_in)
+        following = jnp.zeros((8, step), f32)
         for c in reversed(range(blocks)):
             rows = rows_of(c)
             low_g = gs.astype(bf16)
@@ -542,10 +566,15 @@
             behind[rows, :] += dot2(scaled * dvs, red[cols, :])
             direct[rows, :] += dot2(v * g_sc, red[cols, :])
             g_v = dot(tables[rows, :lanes], ex[:, cols]) * g_sc + params[0, 6:7, cols] * dy
-            gu_out[rows, cols] = g_v * slope
+            g_u = g_v * slope
+            g_x = conv_back(jnp.concatenate([g_u, following], axis=0), params[0, :, cols], masks, rows, step)
+            lx_out[rows, cols] = g_x.astype(bf16)
+            following = g_u[:8]
+            if c == blocks - 1:
+                tail[:, cols] = g_x[-edge:]
             if c == 0:
                 at = pl.ds(pl.multiple_of(g * width + n * step, lanes), step)
-                edges[:, at] = (g_v * slope)[:edge].astype(bf16)
+                edges[:, at] = g_u[:edge].astype(bf16)
 
     @pl.when(g == pl.num_programs(0) - 1)
     def _():
@@ -588,15 +617,8 @@
     with_weight(ws, lambda parts: add_times_transposed(acc, lz[...], parts), pl.program_id(0) // 2)
 
 
-def conv_back(cur, params, masks, rows, width):
-    total = params[3:4, :] * cur[:chunk]
-    for k in range(1, 4):
-        shifted = pltpu.roll(cur, cur.shape[0] - k, 0)[:chunk]
-        total = total + params[3 - k : 4 - k, :] * (shifted * tile_lanes(masks[k - 1, rows, :], width))
-    return total
-
-
-def in_x_kernel(sel, gu, halo, a_up, ranks, params, masks, g_rank_z, p_up_z, order, normed, lx_out, g_rank, sent):
+def in_x_kernel(sel, lx, tail, halo, a_up, ranks, params, masks, g_rank_z, p_up_z, order, normed,
+                fixed, g_rank, sent, low):
     g = pl.program_id(0)
 
     @pl.when(g == 0)
@@ -604,21 +626,20 @@
         g_rank[...] = g_rank_z[...]
         sent[...] = jnp.zeros_like(sent)
 
-    own, width = gu.shape
-    step = min(width, 256)
-    blocks = own // chunk
-    for c in range(blocks):
-        rows = rows_of(c)
-        for n in range(width // step):
-            cols = slice(n * step, (n + 1) * step)
-            if c < blocks - 1:
-                cur = gu[c * chunk : (c + 1) * chunk + 8, cols]
-            else:
-                cur = jnp.concatenate([gu[rows, cols], halo[:, cols].astype(f32)[:8]], axis=0)
-            lx_out[rows, cols] = conv_back(cur, params[0, :, cols], masks, rows, step).astype(bf16)
+    own, width = low.shape
+    beyond = jnp.concatenate([jnp.zeros((edge, width), f32), halo[...].astype(f32)[:8]], axis=0)
+    total = tail[...]
+    for k in range(1, 4):
+        shifted = pltpu.roll(beyond, beyond.shape[0] - k, 0)[:edge]
+        total = total + params[0, 3 - k : 4 - k, :] * (
+            shifted * tile_lanes(masks[k - 1, own - edge :, :], width)
+        )
+    fixed[...] = total.astype(bf16)
+    low[: own - edge, :] = lx[: own - edge, :]
+    low[own - edge :, :] = total.astype(bf16)
     size = g_rank.shape[1]
-    g_rank[...] += dot_nt(lx_out[...], a_up[...])
-    both = dot_tn(ranks[...], lx_out[...])
+    g_rank[...] += dot_nt(low[...], a_up[...])
+    both = dot_tn(ranks[...], low[...])
     to = sel[8 + g]
     put_inner_parts(sent, to, p_up_z[0], order, 0)
     put_inner_parts(sent, to, both[:size] + both[size:], order, width // sent.shape[0])
@@ -835,8 +856,8 @@
     )
 
     if by_exchange:
-        params = jnp.stack(around_tensor(params))
         small = joined_with(joined_with(small[None], "dp", 1), "dp", 2)
+        params = jnp.stack(around_tensor(after(params, small)))
         small = jnp.concatenate([small, swap(small, 0)])
         w_x, near_x = spread_dp(ring_x, [])
         ring_z = around_tensor(after(local_z, *ring_x[1:]))
@@ -923,22 +944,21 @@
         second = pl.BlockSpec(shape, lambda g, *s: (0, jnp.maximum(g - 2, 0), 0, 0))
         return [first] * 4 + [second] * 4
 
-    def call(kernel, out, in_specs, out_specs, scratch, flops, moved, steps=tp_size, fill=(), grant=vmem_bytes):
+    def call(kernel, out, in_specs, out_specs, scratch, flops, moved, steps=tp_size, grant=vmem_bytes, in_place=None):
         kernel, kernel_takes_sel, name = kernel
 
         def body(sel_ref, *refs):
-            refs = refs[: len(in_specs)] + refs[len(in_specs) + len(fill) :]
             return kernel(sel_ref, *refs) if kernel_takes_sel else kernel(*refs)
 
         return pl.pallas_call(
             body,
             name=name,
-            input_output_aliases={1 + len(in_specs) + i: to for i, to in enumerate(fill)},
+            input_output_aliases={1 + i: to for i, to in (in_place or {}).items()},
             out_shape=[jax.ShapeDtypeStruct(s, d) for s, d in out],
             grid_spec=pltpu.PrefetchScalarGridSpec(
                 num_scalar_prefetch=1,
                 grid=steps if isinstance(steps, tuple) else (steps,),
-                in_specs=in_specs + [pl.BlockSpec(memory_space=pl.ANY)] * len(fill),
+                in_specs=in_specs,
                 out_specs=out_specs,
                 scratch_shapes=scratch,
             ),
@@ -1015,10 +1035,10 @@
         return out, moved
 
     within_specs = [cols(own), part_at(0, 5, own, lanes), chunk_rows, scores_spec, cols(lanes, part * lanes)]
+    states_in, moved_state = chain(sent_state, up, -1)
     (y_within,) = call(
         plain(within_kernel), [(big, f32)], within_specs, [cols(own)], [], mat, 6 * mega
-    )(sel, scaled, tables, cums_t, scores, exl)
-    states_in, _ = chain(sent_state, up, -1, y_within)
+    )(sel, after(scaled, moved_state), tables, cums_t, scores, exl)
 
     states_spec = pl.BlockSpec((blocks, state, group), lambda g, *s: (0, 0, g))
     def steps_in(phase, first, then):
@@ -1048,34 +1068,36 @@
     sent_shape = (dp_size, tp_size, 2 * rank, max(d_rows, 2 * hp))
     cot = cotangent[0]
     big3 = (tp_size, own, group)
-    y, states, mixed, sent_out, g_heads, low_z, sent_grad = call(
+    states, mixed, sent_out, g_heads, low_z, sent_grad, ahead_sums = call(
         selecting(middle_kernel, weights=n_w, hops=hops, inner=inner),
-        [(big, f32), ((blocks, state, inner), bf16), ((own, width), f32), (sent_shape, bf16), (big, f32), (big, bf16),
-         ((state, inner), bf16)],
+        [((blocks, state, inner), bf16), ((own, width), f32), (sent_shape, bf16), (big, f32), (big, bf16),
+         ((state, inner), bf16), ((own, lanes), f32)],
         [full(ext, width)] + weights_in(0, w_z) + weights_in(1, w_out)
         + [cols_in(0, state, group, -h) for h in range(1, hops + 1)]
         + [full(own, 2 * rank), up_in(0, 0, 2 * rank), pl.BlockSpec((1, 8, group), lambda p, g, s: (g, 0, 0)),
            cols_in(0, own), cols_in(0, own), cols_in(0, own), part_at(0, 1, own, 2 * lanes),
            part_at(0, 4, own, lanes), cols_in(0, 8), cols_always(lanes, group), b_t_spec, c_t_spec,
-           part_at(0, 1, own, state), full(own, width), full(own, width), b_up_spec, up_in(1, 4, rank), order_spec],
-        [cols_in(0, own), pl.BlockSpec((blocks, state, group), moving(0, lambda i, s: (0, 0, i))), full(own, width),
-         full(*sent_shape), cols_in(2, own), cols_in(2, own), cols_in(2, state)],
+           part_at(0, 1, own, state), full(own, width), full(own, width), b_up_spec, up_in(1, 4, rank), order_spec,
+           pl.BlockSpec((group, lanes), moving(2, lambda i, s: (i, 0)))],
+        [pl.BlockSpec((blocks, state, group), moving(0, lambda i, s: (0, 0, i))), full(own, width),
+         full(*sent_shape), cols_in(2, own), cols_in(2, own), cols_in(2, state), full(own, lanes)],
         [pltpu.VMEM(big3, f32), pltpu.VMEM(big3, f32), pltpu.VMEM(big3, f32), pltpu.VMEM(big3, f32),
+         pltpu.VMEM(big3, f32),
          pltpu.VMEM((own, lanes), f32), pltpu.VMEM((own, lanes), f32), pltpu.VMEM((own, width), f32),
          pltpu.VMEM((own, width), bf16), pltpu.VMEM((own, rank), f32), pltpu.VMEM((own, rank), f32),
          pltpu.VMEM((own, group), bf16)],
         4 * mat, 40 * mega, (3, tp_size), grant=vmem_bytes * 5 // 4,
     )(sel, normed_moved, *w_z, *w_out, *states_in, ranks_own, ups, params, y_within, u, scaled, tables, tables, keep,
-      ex, bc_t, bc_t, bc, cot, tok, wides, ups, order)
+      ex, bc_t, bc_t, bc, cot, tok, wides, ups, order, red)
     red_spec = pl.BlockSpec((group, lanes), lambda g, *s: (g, 0))
     d_within, d_scores, ahead = call(
         plain(back_within_kernel),
         [(big, f32), ((blocks, chunk, chunk), f32), ((own, lanes), f32)],
-        [cols(own), cols(own)] + within_specs + [red_spec],
+        [cols(own), full(own, lanes)] + within_specs + [red_spec],
         [cols(own), full(blocks, chunk, chunk), full(own, lanes)],
         [pltpu.VMEM((chunk, group), f32)],
         2 * mat, 14 * mega, grant=vmem_bytes * 5 // 4,
-    )(sel, g_heads, y, scaled, tables, cums_t, scores, exl, red)
+    )(sel, g_heads, ahead_sums, scaled, tables, cums_t, scores, exl, red)
     grads_in, moved_grad = chain(sent_grad, down, 1, ahead)
     low_z = after(low_z, moved_grad)
 
@@ -1090,30 +1112,31 @@
 
     grads_in = [after(x, acc_z) for x in grads_in]
     edges_shape = (edge, inner + 2 * state)
-    g_u, g_u_bc, low_dt, edges = call(
+    low_x, g_u_bc, low_dt, edges, tail = call(
         plain(back_state_kernel, hops=hops),
-        [(big, f32), ((own, 2 * state), f32), ((own, heads), bf16), (edges_shape, bf16)],
+        [(big, bf16), ((own, 2 * state), f32), ((own, heads), bf16), (edges_shape, bf16), ((edge, inner), f32)],
         [cols(state, group, h) for h in range(1, hops + 1)]
         + [states_spec, cols(own), cols(own), cols(own), cols(own), p_spec, full(own, 2 * state), c_t_spec,
            part_at(0, 0, own, 4 * lanes), cols(8), part_at(0, 0, 8, lanes), cols(lanes), red_spec,
-           full(blocks, chunk, chunk), full(own, lanes), allowed_spec, full(own, 2 * state + lanes)],
-        [cols(own), full(own, 2 * state), full(own, heads), full(*edges_shape)],
+           full(blocks, chunk, chunk), full(own, lanes), allowed_spec, full(own, 2 * state + lanes),
+           masks_after_spec],
+        [cols(own), full(own, 2 * state), full(own, heads), full(*edges_shape), cols(edge)],
         [pltpu.VMEM((own, state), f32), pltpu.VMEM((own, state), f32), pltpu.VMEM((own, lanes), f32),
          pltpu.VMEM((own, lanes), f32), pltpu.VMEM((8, lanes), f32)],
         mat, 24 * mega,
     )(sel, *grads_in, states, g_heads, scaled, d_within, u, params, bc, bc_t, tables, keep, keep, ex, red, d_scores,
-      ahead, scores, rows_f32)
+      ahead, scores, rows_f32, masks)
 
     halo = down(edges)
     low_x, g_rank, sent_in = call(
         selecting(in_x_kernel),
         [(big, bf16), ((own, rank), f32), (sent_shape, bf16)],
-        [cols(own), cols(edge, group, 1), up_at(2, rank), full(own, 2 * rank), p_spec, masks_after_spec,
+        [cols(own), cols(edge), cols(edge, group, 1), up_at(2, rank), full(own, 2 * rank), p_spec, masks_after_spec,
          full(own, rank), stacked(rank, group), order_spec, full(own, width)],
-        [cols(own), full(own, rank), full(*sent_shape)],
-        [],
-        mat // 8, 8 * mega,
-    )(sel, g_u, halo, ups, ranks_own, params, masks, g_rank_z, p_up_z, order, normed)
+        [pl.BlockSpec((edge, group), lambda g, *s: (own // edge - 1, g)), full(own, rank), full(*sent_shape)],
+        [pltpu.VMEM((own, group), bf16)],
+        mat // 8, 8 * mega, in_place={0: 0},
+    )(sel, low_x, tail, halo, ups, ranks_own, params, masks, g_rank_z, p_up_z, order, normed)
 
     (tokens_grad,) = call(
         selecting(tokens_kernel, weights=n_w),

time: 271 us -> 256 us (0.945)
  waiting for transfers between devices: 45.5 us -> 31.5 us
  local copies, waits for them, and re-layouts: 17.5 us -> 13.9 us
  starting transfers between devices: 61.8 us -> 64.6 us
    ppermute x3, waiting for transfers between devices: 11.6 us -> 2.08 us  [up(): return lax.ppermute(x, 'tensor', [(i, i + 1) for i in range(n - 1)])]
    ppermute x15, waiting for transfers between devices: 7.78 us -> 2.21 us  [around_tensor(): lax.ppermute(x, 'tensor', [(i, (i + s) % n) for i in range(n)])]
    unnamed x129 -> x143, local copies, waits for them, and re-layouts: 7.19 us -> 4.94 us
  transfers between devices with their start and end apart: 49 -> 49, of which waited for: 11 -> 12; matrix products, arithmetic and copies ran while one was open for 9% -> 9% of each run, Pallas kernels for 24% -> 25%
where the time goes in v3:
time: 256 us; the launch traced here: 254 us
  Pallas kernels  127 us (50%)
  starting transfers between devices  64.6 us (25%)
  waiting for transfers between devices  31.5 us (12%)
  other arithmetic  14.7 us (6%)
  local copies, waits for them, and re-layouts  13.9 us (5%)
    pallas_call x1, Pallas kernels, shards(): call(selecting(middle_kernel, weights=n_w, hops=hops, inner=inner), [((bl...  37.3 us
    ppermute x25, starting transfers between devices, swap(): return lax.ppermute(x, 'dp', [(i, i ^ 1 << bit) for i in range(n)])  24.4 us
    ppermute x15, starting transfers between devices, around_tensor(): lax.ppermute(x, 'tensor', [(i, (i + s) % n) for i in range(n)])  19.8 us
    pallas_call x1, Pallas kernels, shards(): call(plain(back_state_kernel, hops=hops), [(big, bf16), ((own, 2 * state)...  18 us
    pallas_call x1, Pallas kernels, shards(): call(plain(back_within_kernel), [(big, f32), ((blocks, chunk, chunk), f32...  14.2 us
    pallas_call x1, Pallas kernels, shards(): call(plain(proj_kernel, weights=n_w), [(big, f32), (big, bf16), ((state,...  12.6 us
    pallas_call x1, Pallas kernels, shards(): call(selecting(tokens_kernel, weights=n_w), [((own, width), f32)], [cols(...  12.2 us
    ppermute x3, waiting for transfers between devices, down(): return lax.ppermute(x, 'tensor', [(i + 1, i) for i in range(n - 1)])  11.2 us
  transfers between devices with their start and end apart: 49, of which 12 were waited for; matrix products, arithmetic and copies ran while one was open for 9% of the time, Pallas kernels for 25%

profile of v3, /device:TPU:1, one launch (start us, length us, event | category | flops | bytes accessed | tf_op | source)
XLA Modules:
  0.0 254.5 jit_solution(6006552891074013506)
XLA Ops:
  2.2 3.2 %collective-permute-start.11 = (bf16[128,512]{1,0:T(8,128)(2,1)S(1)}, bf16[128,512]{1,0:T(8,128)(2,1)S(1)}, u32[]{:S(2)}, u32[]{:S(2)}) collective-permute-start(bf16[128,512]{1,0:T(8,128)(2,1)S(1)} %bitcast.117), channel_id=1, source_target_pairs={{0,2},{1,3},{2,0},{3,1},{4,6},{5,7},{6,4},{7,5},{8,10},{9,11},{10,... | collective-permute-start | bytes 393224 | tf_op jit(solution)/shard_map/ppermute | solution.py:720
  6.7 2.0 collective-permute-start.12
  9.4 1.9 pack_kernel.1
  23.0 3.5 %collective-permute-done.2 = bf16[2,800,128]{2,1,0:T(8,128)(2,1)S(1)} collective-permute-done((bf16[2,800,128]{2,1,0:T(8,128)(2,1)S(1)}, bf16[2,800,128]{2,1,0:T(8,128)(2,1)S(1)}, u32[]{:S(2)}, u32[]{:S(2)}) %collective-permute-start.2) | collective-permute-done | bytes 409632 | tf_op jit(solution)/shard_map/ppermute | solution.py:738
  28.9 3.3 %collective-permute-start.3 = (bf16[4,800,128]{2,1,0:T(8,128)(2,1)}, bf16[4,800,128]{2,1,0:T(8,128)(2,1)}, u32[]{:S(2)}, u32[]{:S(2)}) collective-permute-start(bf16[4,800,128]{2,1,0:T(8,128)(2,1)} %pad_maximum_fusion.1), channel_id=1, source_target_pairs={{0,4},{4,0},{8,12},{12,8},{16,20},{20,16},{24,28},{28,24},{1,5},{5... | collective-permute-start | bytes 2457608 | tf_op jit(solution)/shard_map/ppermute | solution.py:725
  36.4 2.3 collective-permute-start.8
  41.2 2.0 collective-permute-done.7
  49.4 3.1 %collective-permute-start.6 = (bf16[320,128]{1,0:T(8,128)(2,1)S(1)}, bf16[320,128]{1,0:T(8,128)(2,1)S(1)}, u32[]{:S(2)}, u32[]{:S(2)}) collective-permute-start(bf16[320,128]{1,0:T(8,128)(2,1)S(1)} %get-tuple-element.121), channel_id=1, source_target_pairs={{0,3},{1,0},{2,1},{3,2},{4,7},{5,4},{6,5},{7,6},{8,11},{9,8},{10,9... | collective-permute-start | bytes 245768 | tf_op jit(solution)/shard_map/ppermute | solution.py:720
  52.6 1.9 pad_maximum_fusion.3.refs_5_
  55.7 2.5 collective-permute-done.37.refs_2_
  58.3 2.2 collective-permute-start.41
  63.1 9.2 %prep_kernel.1 = (bf16[528,1024]{1,0:T(8,128)(2,1)}, bf16[512,1024]{1,0:T(8,128)(2,1)}, bf16[528,32]{1,0:T(8,128)(2,1)}, bf16[512,32]{1,0:T(8,128)(2,1)}, bf16[5...) custom-call(s32[33]{0:T(128)} %concatenate.42.sel_ref, ...), custom_call_target="tpu_custom_call" | custom-call | flops 536870912 | bytes 6291456 | tf_op jit(solution)/shard_map/prep_kernel/pallas_call | solution.py:992
  74.9 2.7 %collective-permute-start.32 = (bf16[128,512]{1,0:T(8,128)(2,1)S(1)}, bf16[128,512]{1,0:T(8,128)(2,1)S(1)}, u32[]{:S(2)}, u32[]{:S(2)}) collective-permute-start(bf16[128,512]{1,0:T(8,128)(2,1)S(1)} %bitcast.127), channel_id=1, source_target_pairs={{0,3},{1,0},{2,1},{3,2},{4,7},{5,4},{6,5},{7,6},{8,11},{9,8},{10,9... | collective-permute-start | bytes 393224 | tf_op jit(solution)/shard_map/ppermute | solution.py:720
  78.9 12.6 %proj_kernel.1 = (f32[512,2048]{1,0:T(8,128)}, bf16[512,2048]{1,0:T(8,128)(2,1)}, bf16[128,2048]{1,0:T(8,128)(2,1)}) custom-call(s32[33]{0:T(128)} %concatenate.42.sel_ref, bf16[528,1024]{1,0:T(8,128)(2,1)} %get-tuple-element.62.refs_0_, bf16[2,2,128,512]{3,2,1,0:T(8,128)(2,1)} %copy-done.36, bf16[2,2,128,512]{3,2,1,0:T(8,128)(2,1)} %collective-permute-done.37.refs_2_, ...), custom_call_target="tpu_custom_call" | custom-call | flops 2147483648 | bytes 12582912 | tf_op jit(solution)/shard_map/proj_kernel/pallas_call | solution.py:1018
  91.5 1.9 collective-permute-start.24
  93.5 2.5 collective-permute-start.43
  99.6 3.8 %collective-permute-done.33 = bf16[2,128,512]{2,1,0:T(8,128)(2,1)S(1)} collective-permute-done((bf16[2,128,512]{2,1,0:T(8,128)(2,1)S(1)}, bf16[2,128,512]{2,1,0:T(8,128)(2,1)S(1)}, u32[]{:S(2)}, u32[]{:S(2)}) %collective-permute-start.33) | collective-permute-done | bytes 262176 | tf_op jit(solution)/shard_map/ppermute | solution.py:725
  105.2 2.1 collective-permute-done.43.refs_17_
  109.7 4.4 %collective-permute-start.44 = (bf16[128,2048]{1,0:T(8,128)(2,1)S(1)}, bf16[128,2048]{1,0:T(8,128)(2,1)S(1)}, u32[]{:S(2)}, u32[]{:S(2)}) collective-permute-start(bf16[128,2048]{1,0:T(8,128)(2,1)S(1)} %multiply_convert_fusion.1), channel_id=1, source_target_pairs={{0,1},{1,2},{2,3},{4,5},{5,6},{6,7},{8,9},{9,10},{10,11},{12,13},{... | collective-permute-start | bytes 1572872 | tf_op jit(solution)/shard_map/ppermute | solution.py:710
  114.1 4.4 %collective-permute-done.34.refs_14_ = bf16[2,2,128,512]{3,2,1,0:T(8,128)(2,1)S(1)} collective-permute-done((bf16[2,2,128,512]{3,2,1,0:T(8,128)(2,1)S(1)}, bf16[2,2,128,512]{3,2,1,0:T(8,128)(2,1)S(1)}, u32[]{:S(2)}, u32[]{:S(2)}) %collective-permute-start.34) | collective-permute-done | bytes 524320 | tf_op jit(solution)/shard_map/ppermute | solution.py:725
  119.6 2.0 collective-permute-start.30
  122.9 6.1 %within_kernel.1.refs_22_ = f32[512,2048]{1,0:T(8,128)} custom-call(s32[33]{0:T(128)S(1)} %copy-done.26, bf16[512,2048]{1,0:T(8,128)(2,1)S(1)} %copy-done.1, bf16[512,768]{1,0:T(8,128)(2,1)S(1)} %copy-done.2, f32[4,4,8,128]{3,2,1,0:T(8,128)S(1)} %copy-done.25, f32[2,4,128,128]{3,2,1,0:T(8,128)S(1)} %copy-done.5, bf16[128,4096]{1,0:T(8,128)(2,1)S(1)} %copy-done.10), custom_call_target="tpu_custom_call" | custom-call | flops 2147483648 | bytes 6291456 | tf_op jit(solution)/shard_map/within_kernel/pallas_call | solution.py:1039
  130.7 37.3 %middle_kernel.1 = (bf16[4,128,2048]{2,1,0:T(8,128)(2,1)}, f32[512,1024]{1,0:T(8,128)}, bf16[8,4,32,128]{3,2,1,0:T(8,128)(2,1)}, f32[512,2048]{1,0:T(8,128)}, bf...) custom-call(s32[33]{0:T(128)} %concatenate.42.sel_ref, ...), custom_call_target="tpu_custom_call" | custom-call | flops 8589934592 | bytes 41943040 | tf_op jit(solution)/shard_map/middle_kernel/pallas_call | solution.py:1071
  169.4 14.2 %back_within_kernel.1 = (f32[512,2048]{1,0:T(8,128)}, f32[4,128,128]{2,1,0:T(8,128)}, f32[512,128]{1,0:T(8,128)}) custom-call(s32[33]{0:T(128)} %concatenate.42.sel_ref, f32[512,2048]{1,0:T(8,128)} %get-tuple-element.87.refs_0_.refs_3_, f32[512,128]{1,0:T(8,128)} %get-tuple-element.88.refs_1_, ...), custom_call_target="tpu_custom_call" | custom-call | flops 4294967296 | bytes 14680064 | tf_op jit(solution)/shard_map/back_within_kernel/pallas_call | solution.py:1093
  186.4 8.2 %in_z_kernel.1 = (f32[512,1024]{1,0:T(8,128)}, f32[512,16]{1,0:T(8,128)S(1)}, f32[4,16,512]{2,1,0:T(8,128)S(1)}) custom-call(s32[33]{0:T(128)S(1)} %copy-done.27, bf16[512,2048]{1,0:T(8,128)(2,1)} %get-tuple-element.91.refs_0_, bf16[2,2,128,512]{3,2,1,0:T(8,128)(2,1)S(1)} %copy-done.16, bf16[2,2,128,512]{3,2,1,0:T(8,128)(2,1)} %collective-permute-done.17.refs_2_, ...), custom_call_target="tpu_custom_call" | custom-call | flops 2147483648 | bytes 8388608 | tf_op jit(solution)/shard_map/in_z_kernel/pallas_call | solution.py:1104
  194.7 5.7 %collective-permute-done.46.refs_1_ = bf16[128,2048]{1,0:T(8,128)(2,1)S(1)} collective-permute-done((bf16[128,2048]{1,0:T(8,128)(2,1)S(1)}, bf16[128,2048]{1,0:T(8,128)(2,1)S(1)}, u32[]{:S(2)}, u32[]{:S(2)}) %collective-permute-start.46) | collective-permute-done | bytes 524320 | tf_op jit(solution)/shard_map/ppermute | solution.py:715
  200.5 18.0 %back_state_kernel.1 = (bf16[512,2048]{1,0:T(8,128)(2,1)}, f32[512,256]{1,0:T(8,128)S(1)}, bf16[512,32]{1,0:T(8,128)(2,1)S(1)}, bf16[16,2304]{1,0:T(8,128)(2,1)S(1)}, f32[16,2048]{1,0:T(8,128)S(1)}) custom-call(s32[33]{0:T(128)S(1)} %copy-done.27, bf16[128,2048]{1,0:T(8,128)(2,1)S(1)} %collective-permute-done.45.refs_0_, ...), custom_call_target="tpu_custom_call" | custom-call | flops 2147483648 | bytes 25165824 | tf_op jit(solution)/shard_map/back_state_kernel/pallas_call | solution.py:1115
  219.8 4.5 %collective-permute-done.47.refs_2_.refs_12_ = bf16[16,2304]{1,0:T(8,128)(2,1)S(1)} collective-permute-done((bf16[16,2304]{1,0:T(8,128)(2,1)S(1)}, bf16[16,2304]{1,0:T(8,128)(2,1)S(1)}, u32[]{:S(2)}, u32[]{:S(2)}) %collective-permute-start.47) | collective-permute-done | bytes 73760 | tf_op jit(solution)/shard_map/ppermute | solution.py:715
  224.3 5.5 %in_x_kernel.1 = (bf16[512,2048]{1,0:T(8,128)(2,1)}, f32[512,16]{1,0:T(8,128)S(1)}, bf16[8,4,32,128]{3,2,1,0:T(8,128)(2,1)S(1)}) custom-call(s32[33]{0:T(128)S(1)} %copy-done.27, bf16[512,2048]{1,0:T(8,128)(2,1)} %get-tuple-element.99.refs_0_, f32[16,2048]{1,0:T(8,128)S(1)} %get-tuple-element.100.refs_1_, ...), custom_call_target="tpu_custom_call", output_to_operand_aliasing={{0}: (1, {})} | custom-call | flops 268435456 | bytes 8388608 | tf_op jit(solution)/shard_map/in_x_kernel/pallas_call | solution.py:1131
  231.4 5.7 %all-to-all-start = ((bf16[32,64,128]{2,1,0:T(8,128)(2,1)}), bf16[32,64,128]{2,1,0:T(8,128)(2,1)S(1)}, u32[]{:S(2)}, u32[]{:S(2)}) async-start(bf16[32,64,128]{2,1,0:T(8,128)(2,1)} %bitcast.72), calls=%async_computation | async-start | bytes 1048576 | tf_op jit(solution)/shard_map/all_to_all | solution.py:1156
  238.7 12.2 %tokens_kernel.1 = f32[512,1024]{1,0:T(8,128)} custom-call(s32[33]{0:T(128)} %concatenate.42.sel_ref, bf16[512,2048]{1,0:T(8,128)(2,1)} %get-tuple-element.105.refs_0_, bf16[2,2,128,512]{3,2,1,0:T(8,128)(2,1)} %copy-done.36, bf16[2,2,128,512]{3,2,1,0:T(8,128)(2,1)} %collective-permute-done.37.refs_2_, ...), custom_call_target="tpu_custom_call" | custom-call | flops 2147483648 | bytes 14680064 | tf_op jit(solution)/shard_map/tokens_kernel/pallas_call | solution.py:1141
  252.4 2.1 collect_kernel.1
  (286 shorter events, 59.1 us)
Async XLA Ops:
  2.2 16.9 %collective-permute-start.11 = (bf16[128,512]{1,0:T(8,128)(2,1)S(1)}, bf16[128,512]{1,0:T(8,128)(2,1)S(1)}, u32[]{:S(2)}, u32[]{:S(2)}) collective-permute-start(bf16[128,512]{1,0:T(8,128)(2,1)S(1)} %bitcast.117), channel_id=1, source_target_pairs={{0,2},{1,3},{2,0},{3,1},{4,6},{5,7},{6,4},{7,5},{8,10},{9,11},{10,... | collective-permute-start | bytes 393224 | tf_op jit(solution)/shard_map/ppermute | solution.py:720
  5.4 13.7 %collective-permute-start.10 = (bf16[128,512]{1,0:T(8,128)(2,1)S(1)}, bf16[128,512]{1,0:T(8,128)(2,1)S(1)}, u32[]{:S(2)}, u32[]{:S(2)}) collective-permute-start(bf16[128,512]{1,0:T(8,128)(2,1)S(1)} %bitcast.118), channel_id=1, source_target_pairs={{0,1},{1,2},{2,3},{3,0},{4,5},{5,6},{6,7},{7,4},{8,9},{9,10},{10,1... | collective-permute-start | bytes 393224 | tf_op jit(solution)/shard_map/ppermute | solution.py:720
  6.7 12.4 %collective-permute-start.12 = (bf16[128,512]{1,0:T(8,128)(2,1)S(1)}, bf16[128,512]{1,0:T(8,128)(2,1)S(1)}, u32[]{:S(2)}, u32[]{:S(2)}) collective-permute-start(bf16[128,512]{1,0:T(8,128)(2,1)S(1)} %bitcast.119), channel_id=1, source_target_pairs={{0,3},{1,0},{2,1},{3,2},{4,7},{5,4},{6,5},{7,6},{8,11},{9,8},{10,9... | collective-permute-start | bytes 393224 | tf_op jit(solution)/shard_map/ppermute | solution.py:720
  19.1 15.0 %collective-permute-start.21 = (bf16[128,512]{1,0:T(8,128)(2,1)S(1)}, bf16[128,512]{1,0:T(8,128)(2,1)S(1)}, u32[]{:S(2)}, u32[]{:S(2)}) collective-permute-start(bf16[128,512]{1,0:T(8,128)(2,1)S(1)} %bitcast.121), channel_id=1, source_target_pairs={{0,3},{1,0},{2,1},{3,2},{4,7},{5,4},{6,5},{7,6},{8,11},{9,8},{10,9... | collective-permute-start | bytes 393224 | tf_op jit(solution)/shard_map/ppermute | solution.py:720
  19.3 14.9 %collective-permute-start.20 = (bf16[128,512]{1,0:T(8,128)(2,1)S(1)}, bf16[128,512]{1,0:T(8,128)(2,1)S(1)}, u32[]{:S(2)}, u32[]{:S(2)}) collective-permute-start(bf16[128,512]{1,0:T(8,128)(2,1)S(1)} %bitcast.122), channel_id=1, source_target_pairs={{0,2},{1,3},{2,0},{3,1},{4,6},{5,7},{6,4},{7,5},{8,10},{9,11},{10,... | collective-permute-start | bytes 393224 | tf_op jit(solution)/shard_map/ppermute | solution.py:720
  21.7 13.2 %collective-permute-start.14 = (bf16[2,128,512]{2,1,0:T(8,128)(2,1)S(1)}, bf16[2,128,512]{2,1,0:T(8,128)(2,1)S(1)}, u32[]{:S(2)}, u32[]{:S(2)}) collective-permute-start(bf16[2,128,512]{2,1,0:T(8,128)(2,1)S(1)} %pad_maximum_fusion.14), channel_id=1, source_target_pairs={{0,8},{4,12},{8,0},{12,4},{16,24},{20,28},{24,16},{28,20},{1,9},{5... | collective-permute-start | bytes 786440 | tf_op jit(solution)/shard_map/ppermute | solution.py:725
  28.9 15.5 %collective-permute-start.3 = (bf16[4,800,128]{2,1,0:T(8,128)(2,1)}, bf16[4,800,128]{2,1,0:T(8,128)(2,1)}, u32[]{:S(2)}, u32[]{:S(2)}) collective-permute-start(bf16[4,800,128]{2,1,0:T(8,128)(2,1)} %pad_maximum_fusion.1), channel_id=1, source_target_pairs={{0,4},{4,0},{8,12},{12,8},{16,20},{20,16},{24,28},{28,24},{1,5},{5... | collective-permute-start | bytes 2457608 | tf_op jit(solution)/shard_map/ppermute | solution.py:725
  40.9 13.5 %collective-permute-start.40 = (bf16[2,2,128,512]{3,2,1,0:T(8,128)(2,1)S(1)}, bf16[2,2,128,512]{3,2,1,0:T(8,128)(2,1)}, u32[]{:S(2)}, u32[]{:S(2)}) collective-permute-start(bf16[2,2,128,512]{3,2,1,0:T(8,128)(2,1)S(1)} %pad_maximum_fusion.7.refs_5_), channel_id=1, source_target_pairs={{0,8},{4,12},{8,0},{12,4},{16,24},{20,28},{24,16},{28,20},{1,9},{5... | collective-permute-start | bytes 1572872 | tf_op jit(solution)/shard_map/ppermute | solution.py:725
  43.1 15.1 %collective-permute-start.37 = (bf16[2,2,128,512]{3,2,1,0:T(8,128)(2,1)S(1)}, bf16[2,2,128,512]{3,2,1,0:T(8,128)(2,1)}, u32[]{:S(2)}, u32[]{:S(2)}) collective-permute-start(bf16[2,2,128,512]{3,2,1,0:T(8,128)(2,1)S(1)} %pad_maximum_fusion.6.refs_1_), channel_id=1, source_target_pairs={{0,16},{4,20},{8,24},{12,28},{16,0},{20,4},{24,8},{28,12},{1,17},{... | collective-permute-start | bytes 1572872 | tf_op jit(solution)/shard_map/ppermute | solution.py:725
  48.4 12.1 %collective-permute-start.5 = (bf16[320,128]{1,0:T(8,128)(2,1)S(1)}, bf16[320,128]{1,0:T(8,128)(2,1)S(1)}, u32[]{:S(2)}, u32[]{:S(2)}) collective-permute-start(bf16[320,128]{1,0:T(8,128)(2,1)S(1)} %get-tuple-element.121), channel_id=1, source_target_pairs={{0,2},{1,3},{2,0},{3,1},{4,6},{5,7},{6,4},{7,5},{8,10},{9,11},{10,... | collective-permute-start | bytes 245768 | tf_op jit(solution)/shard_map/ppermute | solution.py:720
  49.3 11.3 %collective-permute-start.4 = (bf16[320,128]{1,0:T(8,128)(2,1)S(1)}, bf16[320,128]{1,0:T(8,128)(2,1)S(1)}, u32[]{:S(2)}, u32[]{:S(2)}) collective-permute-start(bf16[320,128]{1,0:T(8,128)(2,1)S(1)} %get-tuple-element.121), channel_id=1, source_target_pairs={{0,1},{1,2},{2,3},{3,0},{4,5},{5,6},{6,7},{7,4},{8,9},{9,10},{10,1... | collective-permute-start | bytes 245768 | tf_op jit(solution)/shard_map/ppermute | solution.py:720
  49.4 11.5 %collective-permute-start.6 = (bf16[320,128]{1,0:T(8,128)(2,1)S(1)}, bf16[320,128]{1,0:T(8,128)(2,1)S(1)}, u32[]{:S(2)}, u32[]{:S(2)}) collective-permute-start(bf16[320,128]{1,0:T(8,128)(2,1)S(1)} %get-tuple-element.121), channel_id=1, source_target_pairs={{0,3},{1,0},{2,1},{3,2},{4,7},{5,4},{6,5},{7,6},{8,11},{9,8},{10,9... | collective-permute-start | bytes 245768 | tf_op jit(solution)/shard_map/ppermute | solution.py:720
  58.3 16.0 %collective-permute-start.41 = (bf16[2,2,128,512]{3,2,1,0:T(8,128)(2,1)S(1)}, bf16[2,2,128,512]{3,2,1,0:T(8,128)(2,1)}, u32[]{:S(2)}, u32[]{:S(2)}) collective-permute-start(bf16[2,2,128,512]{3,2,1,0:T(8,128)(2,1)S(1)} %pad_maximum_fusion.7.refs_5_), channel_id=1, source_target_pairs={{0,4},{4,0},{8,12},{12,8},{16,20},{20,16},{24,28},{28,24},{1,5},{5... | collective-permute-start | bytes 1572872 | tf_op jit(solution)/shard_map/ppermute | solution.py:725
  60.5 14.5 %collective-permute-start.38 = (bf16[2,2,128,512]{3,2,1,0:T(8,128)(2,1)S(1)}, bf16[2,2,128,512]{3,2,1,0:T(8,128)(2,1)}, u32[]{:S(2)}, u32[]{:S(2)}) collective-permute-start(bf16[2,2,128,512]{3,2,1,0:T(8,128)(2,1)S(1)} %pad_maximum_fusion.6.refs_1_), channel_id=1, source_target_pairs={{0,4},{4,0},{8,12},{12,8},{16,20},{20,16},{24,28},{28,24},{1,5},{5... | collective-permute-start | bytes 1572872 | tf_op jit(solution)/shard_map/ppermute | solution.py:725
  60.5 17.1 %collective-permute-start.42 = (bf16[2,2,128,512]{3,2,1,0:T(8,128)(2,1)}, bf16[2,2,128,512]{3,2,1,0:T(8,128)(2,1)}, u32[]{:S(2)}, u32[]{:S(2)}) collective-permute-start(bf16[2,2,128,512]{3,2,1,0:T(8,128)(2,1)} %collective-permute-done.40.refs_6_), channel_id=1, source_target_pairs={{0,4},{4,0},{8,12},{12,8},{16,20},{20,16},{24,28},{28,24},{1,5},{5... | collective-permute-start | bytes 1572872 | tf_op jit(solution)/shard_map/ppermute | solution.py:725
  61.0 16.6 %collective-permute-start.39 = (bf16[2,2,128,512]{3,2,1,0:T(8,128)(2,1)}, bf16[2,2,128,512]{3,2,1,0:T(8,128)(2,1)}, u32[]{:S(2)}, u32[]{:S(2)}) collective-permute-start(bf16[2,2,128,512]{3,2,1,0:T(8,128)(2,1)} %collective-permute-done.37.refs_2_), channel_id=1, source_target_pairs={{0,4},{4,0},{8,12},{12,8},{16,20},{20,16},{24,28},{28,24},{1,5},{5... | collective-permute-start | bytes 1572872 | tf_op jit(solution)/shard_map/ppermute | solution.py:725
  62.5 10.7 %collective-permute-start.26 = (bf16[128,512]{1,0:T(8,128)(2,1)S(1)}, bf16[128,512]{1,0:T(8,128)(2,1)S(1)}, u32[]{:S(2)}, u32[]{:S(2)}) collective-permute-start(bf16[128,512]{1,0:T(8,128)(2,1)S(1)} %bitcast.125), channel_id=1, source_target_pairs={{0,1},{1,2},{2,3},{3,0},{4,5},{5,6},{6,7},{7,4},{8,9},{9,10},{10,1... | collective-permute-start | bytes 393224 | tf_op jit(solution)/shard_map/ppermute | solution.py:720
  73.1 25.4 %collective-permute-start.23 = (bf16[2,2,128,512]{3,2,1,0:T(8,128)(2,1)}, bf16[2,2,128,512]{3,2,1,0:T(8,128)(2,1)}, u32[]{:S(2)}, u32[]{:S(2)}) collective-permute-start(bf16[2,2,128,512]{3,2,1,0:T(8,128)(2,1)} %pad_maximum_fusion.3.refs_5_), channel_id=1, source_target_pairs={{0,8},{4,12},{8,0},{12,4},{16,24},{20,28},{24,16},{28,20},{1,9},{5... | collective-permute-start | bytes 1572872 | tf_op jit(solution)/shard_map/ppermute | solution.py:725
  74.3 25.2 %collective-permute-start.17 = (bf16[2,2,128,512]{3,2,1,0:T(8,128)(2,1)S(1)}, bf16[2,2,128,512]{3,2,1,0:T(8,128)(2,1)}, u32[]{:S(2)}, u32[]{:S(2)}) collective-permute-start(bf16[2,2,128,512]{3,2,1,0:T(8,128)(2,1)S(1)} %pad_maximum_fusion.2.refs_1_), channel_id=1, source_target_pairs={{0,16},{4,20},{8,24},{12,28},{16,0},{20,4},{24,8},{28,12},{1,17},{... | collective-permute-start | bytes 1572872 | tf_op jit(solution)/shard_map/ppermute | solution.py:725
  74.9 16.6 %collective-permute-start.32 = (bf16[128,512]{1,0:T(8,128)(2,1)S(1)}, bf16[128,512]{1,0:T(8,128)(2,1)S(1)}, u32[]{:S(2)}, u32[]{:S(2)}) collective-permute-start(bf16[128,512]{1,0:T(8,128)(2,1)S(1)} %bitcast.127), channel_id=1, source_target_pairs={{0,3},{1,0},{2,1},{3,2},{4,7},{5,4},{6,5},{7,6},{8,11},{9,8},{10,9... | collective-permute-start | bytes 393224 | tf_op jit(solution)/shard_map/ppermute | solution.py:720
  77.6 15.9 %collective-permute-start.31 = (bf16[128,512]{1,0:T(8,128)(2,1)S(1)}, bf16[128,512]{1,0:T(8,128)(2,1)S(1)}, u32[]{:S(2)}, u32[]{:S(2)}) collective-permute-start(bf16[128,512]{1,0:T(8,128)(2,1)S(1)} %bitcast.128), channel_id=1, source_target_pairs={{0,2},{1,3},{2,0},{3,1},{4,6},{5,7},{6,4},{7,5},{8,10},{9,11},{10,... | collective-permute-start | bytes 393224 | tf_op jit(solution)/shard_map/ppermute | solution.py:720
  77.6 18.4 %collective-permute-start.27 = (bf16[2,128,512]{2,1,0:T(8,128)(2,1)}, bf16[2,128,512]{2,1,0:T(8,128)(2,1)S(1)}, u32[]{:S(2)}, u32[]{:S(2)}) collective-permute-start(bf16[2,128,512]{2,1,0:T(8,128)(2,1)} %pad_maximum_fusion.17), channel_id=1, source_target_pairs={{0,8},{4,12},{8,0},{12,4},{16,24},{20,28},{24,16},{28,20},{1,9},{5... | collective-permute-start | bytes 786440 | tf_op jit(solution)/shard_map/ppermute | solution.py:725
  91.5 13.3 %collective-permute-start.24 = (bf16[2,2,128,512]{3,2,1,0:T(8,128)(2,1)}, bf16[2,2,128,512]{3,2,1,0:T(8,128)(2,1)}, u32[]{:S(2)}, u32[]{:S(2)}) collective-permute-start(bf16[2,2,128,512]{3,2,1,0:T(8,128)(2,1)} %pad_maximum_fusion.3.refs_5_), channel_id=1, source_target_pairs={{0,4},{4,0},{8,12},{12,8},{16,20},{20,16},{24,28},{28,24},{1,5},{5... | collective-permute-start | bytes 1572872 | tf_op jit(solution)/shard_map/ppermute | solution.py:725
  93.5 13.8 %collective-permute-start.43 = (bf16[128,2048]{1,0:T(8,128)(2,1)}, bf16[128,2048]{1,0:T(8,128)(2,1)S(1)}, u32[]{:S(2)}, u32[]{:S(2)}) collective-permute-start(bf16[128,2048]{1,0:T(8,128)(2,1)} %get-tuple-element.74), channel_id=1, source_target_pairs={{0,1},{1,2},{2,3},{4,5},{5,6},{6,7},{8,9},{9,10},{10,11},{12,13},{... | collective-permute-start | bytes 1572872 | tf_op jit(solution)/shard_map/ppermute | solution.py:710
  104.9 13.6 %collective-permute-start.34 = (bf16[2,2,128,512]{3,2,1,0:T(8,128)(2,1)S(1)}, bf16[2,2,128,512]{3,2,1,0:T(8,128)(2,1)S(1)}, u32[]{:S(2)}, u32[]{:S(2)}) collective-permute-start(bf16[2,2,128,512]{3,2,1,0:T(8,128)(2,1)S(1)} %pad_maximum_fusion.5.refs_13_), channel_id=1, source_target_pairs={{0,8},{4,12},{8,0},{12,4},{16,24},{20,28},{24,16},{28,20},{1,9},{5... | collective-permute-start | bytes 1572872 | tf_op jit(solution)/shard_map/ppermute | solution.py:725
  107.3 12.3 %collective-permute-start.28 = (bf16[2,2,128,512]{3,2,1,0:T(8,128)(2,1)S(1)}, bf16[2,2,128,512]{3,2,1,0:T(8,128)(2,1)S(1)}, u32[]{:S(2)}, u32[]{:S(2)}) collective-permute-start(bf16[2,2,128,512]{3,2,1,0:T(8,128)(2,1)S(1)} %pad_maximum_fusion.4.refs_9_), channel_id=1, source_target_pairs={{0,16},{4,20},{8,24},{12,28},{16,0},{20,4},{24,8},{28,12},{1,17},{... | collective-permute-start | bytes 1572872 | tf_op jit(solution)/shard_map/ppermute | solution.py:725
  108.1 20.9 %collective-permute-start.35 = (bf16[2,2,128,512]{3,2,1,0:T(8,128)(2,1)S(1)}, bf16[2,2,128,512]{3,2,1,0:T(8,128)(2,1)S(1)}, u32[]{:S(2)}, u32[]{:S(2)}) collective-permute-start(bf16[2,2,128,512]{3,2,1,0:T(8,128)(2,1)S(1)} %pad_maximum_fusion.5.refs_13_), channel_id=1, source_target_pairs={{0,4},{4,0},{8,12},{12,8},{16,20},{20,16},{24,28},{28,24},{1,5},{5... | collective-permute-start | bytes 1572872 | tf_op jit(solution)/shard_map/ppermute | solution.py:725
  109.6 19.5 %collective-permute-start.29 = (bf16[2,2,128,512]{3,2,1,0:T(8,128)(2,1)S(1)}, bf16[2,2,128,512]{3,2,1,0:T(8,128)(2,1)S(1)}, u32[]{:S(2)}, u32[]{:S(2)}) collective-permute-start(bf16[2,2,128,512]{3,2,1,0:T(8,128)(2,1)S(1)} %pad_maximum_fusion.4.refs_9_), channel_id=1, source_target_pairs={{0,4},{4,0},{8,12},{12,8},{16,20},{20,16},{24,28},{28,24},{1,5},{5... | collective-permute-start | bytes 1572872 | tf_op jit(solution)/shard_map/ppermute | solution.py:725
  109.7 19.4 %collective-permute-start.44 = (bf16[128,2048]{1,0:T(8,128)(2,1)S(1)}, bf16[128,2048]{1,0:T(8,128)(2,1)S(1)}, u32[]{:S(2)}, u32[]{:S(2)}) collective-permute-start(bf16[128,2048]{1,0:T(8,128)(2,1)S(1)} %multiply_convert_fusion.1), channel_id=1, source_target_pairs={{0,1},{1,2},{2,3},{4,5},{5,6},{6,7},{8,9},{9,10},{10,11},{12,13},{... | collective-permute-start | bytes 1572872 | tf_op jit(solution)/shard_map/ppermute | solution.py:710
  168.0 16.6 %collective-permute-start.45 = (bf16[128,2048]{1,0:T(8,128)(2,1)}, bf16[128,2048]{1,0:T(8,128)(2,1)S(1)}, u32[]{:S(2)}, u32[]{:S(2)}) collective-permute-start(bf16[128,2048]{1,0:T(8,128)(2,1)} %get-tuple-element.85), channel_id=1, source_target_pairs={{1,0},{2,1},{3,2},{5,4},{6,5},{7,6},{9,8},{10,9},{11,10},{13,12},{... | collective-permute-start | bytes 1572872 | tf_op jit(solution)/shard_map/ppermute | solution.py:715
  184.7 15.7 %collective-permute-start.46 = (bf16[128,2048]{1,0:T(8,128)(2,1)S(1)}, bf16[128,2048]{1,0:T(8,128)(2,1)S(1)}, u32[]{:S(2)}, u32[]{:S(2)}) collective-permute-start(bf16[128,2048]{1,0:T(8,128)(2,1)S(1)} %multiply_convert_fusion), channel_id=1, source_target_pairs={{1,0},{2,1},{3,2},{5,4},{6,5},{7,6},{9,8},{10,9},{11,10},{13,12},{... | collective-permute-start | bytes 1572872 | tf_op jit(solution)/shard_map/ppermute | solution.py:715
  231.4 21.0 %all-to-all-start = ((bf16[32,64,128]{2,1,0:T(8,128)(2,1)}), bf16[32,64,128]{2,1,0:T(8,128)(2,1)S(1)}, u32[]{:S(2)}, u32[]{:S(2)}) async-start(bf16[32,64,128]{2,1,0:T(8,128)(2,1)} %bitcast.72), calls=%async_computation | async-start | bytes 1048576 | tf_op jit(solution)/shard_map/all_to_all | solution.py:1156
  (84 other events, 1159.8 us)

commit v4 on v3

--- a/solution.py
+++ b/solution.py
@@ -310,6 +310,7 @@
     with_weight(ws, body, pl.program_id(0) // 2)
     own, width = u_out.shape
     step = min(width, 256)
+    dt_wide, out_wide = dot(tables[:, :lanes], ex[...]), dot(tables[:, lanes:], ex[...])
     for c in range(own // chunk):
         rows = rows_of(c)
         for n in range(width // step):
@@ -323,9 +324,9 @@
                 )
             u_out[rows, cols] = total
             value = silu(total)
-            scaled = (dot(tables[rows, :lanes], ex[:, cols]) * value).astype(bf16)
+            scaled = (dt_wide[rows, cols] * value).astype(bf16)
             sc_out[rows, cols] = scaled
-            moved[rows, cols] = (dot(tables[rows, lanes:], ex[:, cols]) * scaled.astype(f32)).astype(bf16)
+            moved[rows, cols] = (out_wide[rows, cols] * scaled.astype(f32)).astype(bf16)
     f_out[...] = dot(b_t[...], moved[...]).astype(bf16)
 
 def pair_parts(lcol, cums_t, p):
@@ -342,9 +343,10 @@
 
 def within_kernel(sc, cums3, cums_t, scores, exl, y_out):
     own, width = y_out.shape
+    wide = dot(cums3[...], exl[...])
     for c in range(own // chunk):
         rows = rows_of(c)
-        lcol = dot(cums3[rows, :], exl[...])
+        lcol = wide[rows]
         allowed = tile_lanes(scores[0, c], 2 * lanes)
         for p in range(width // lanes):
             e = pair_parts(lcol, cums_t[0, c], p)
@@ -400,7 +402,7 @@
         for j in range(8):
             at = pl.ds(pl.multiple_of(sel[korder[j]] * lanes, lanes), lanes)
             cots[:, j * lanes : (j + 1) * lanes] = cot[:, at]
-        g_rank[...] = dot_nt(cot[...], b_up[...])
+        g_rank[...] = parts_of(dot_nt(cot[...], b_up[...]), 2)
 
     @pl.when(phase == 0)
     def _():
@@ -409,12 +411,13 @@
             gate_z[g] = times(lambda at: left[first:, at], parts) + dot(ranks[...], a_up[...])
 
         with_weight(zs, body, half)
+        in_wide, out_wide = dot(tables[:, :lanes], ex[...]), dot(tables[:, lanes:], ex[...])
         for n in range(width // step):
             cols = slice(n * step, (n + 1) * step)
             new = []
             for c in range(blocks):
                 rows = rows_of(c)
-                moved = (dot(tables[rows, lanes:], ex[:, cols]) * sc[rows, cols].astype(f32)).astype(bf16)
+                moved = (out_wide[rows, cols] * sc[rows, cols].astype(f32)).astype(bf16)
                 new.append(dot(b_t[:, rows], moved))
             s = sum(r[:, cols].astype(f32) for r in s_ins)
             for c in range(blocks):
@@ -422,7 +425,7 @@
                 s = s * keep[c : c + 1, cols] + new[c]
             for c in range(blocks):
                 rows = rows_of(c)
-                y = yw[rows, cols] + dot(tables[rows, :lanes], ex[:, cols]) * dot(in_c[rows, :], states[c, :, cols])
+                y = yw[rows, cols] + in_wide[rows, cols] * dot(in_c[rows, :], states[c, :, cols])
                 ys[g, rows, cols] = y
                 head = y + params[0, 6:7, cols] * silu(u[rows, cols])
                 heads[g, rows, cols] = head
@@ -441,12 +444,13 @@
         high, rest = halves(normed_inner)
         low[...] = high
         rank[...] += dot_nt(high, b_down[...]) + dot_nt(rest, b_down[...])
-        r_high, r_low = halves(g_rank[...])
-        p_down = dot_tn(r_high, high) + dot_tn(r_low, high) + dot_tn(r_high, rest)
-        put_inner_parts(sent, sel[8 + g], p_down, order, 0)
+        size = rank.shape[1]
+        both = dot_tn(g_rank[...], high)
+        put_inner_parts(sent, sel[8 + g], both[:size] + both[size:], order, 0)
 
         def body(parts):
-            value = (times(lambda at: cots[:, at], parts) + dot2(g_rank[...], b_down[...])) * params[0, 5:6, :]
+            twice = jnp.concatenate([b_down[...], b_down[...]], axis=0)
+            value = (times(lambda at: cots[:, at], parts) + dot(g_rank[...], twice)) * params[0, 5:6, :]
             gg[g] = value
             prod = value * gated[g]
             total = dots[...]
@@ -469,6 +473,7 @@
     def _():
         scale = row_scale_of(sumsq[...], inner)
         coef = scale * scale * scale * (jnp.sum(dots[...], axis=1, keepdims=True) / inner)
+        own_wide = dot(own_in[...], ex[...])
         for c in range(blocks):
             rows = rows_of(c)
             sc_rows, co_rows = scale[rows], coef[rows]
@@ -479,8 +484,9 @@
                 lz_out[rows, cols] = (g_gated * heads[g, rows, cols] * slope).astype(bf16)
                 gh = g_gated * gate
                 gh_out[rows, cols] = gh
-                low[rows, cols] = (dot(own_in[rows, :], ex[:, cols]) * gh).astype(bf16)
-                ahead[rows, :] += dot2(ys[g, rows, cols] * gh, red[cols, :])
+                low[rows, cols] = (own_wide[rows, cols] * gh).astype(bf16)
+                ys[g, rows, cols] = ys[g, rows, cols] * gh
+        ahead[...] += dot2(ys[g], red[...])
         g_out[...] = dot(c_t[...], low[...]).astype(bf16)
 
 
@@ -493,9 +499,10 @@
         ahead[...] = ahead_in[...]
 
     own, width = dv_out.shape
+    wide = dot(cums3[...], exl[...])
     for c in range(own // chunk):
         rows = rows_of(c)
-        lcol = dot(cums3[rows, :], exl[...])
+        lcol = wide[rows]
         allowed = tile_lanes(scores[0, c], 2 * lanes)
         ds = jnp.zeros((chunk, lanes), f32)
         for p in range(width // lanes):
@@ -514,9 +521,9 @@
             lane = lax.broadcasted_iota(jnp.int32, (chunk, lanes), 1)
             dv = jnp.where(lane < lanes // 2, dvb[:chunk], dvb[chunk:])
             dv_out[rows, cols] = dv
-            prod[:, cols] = v.astype(f32) * dv
+            prod[rows, cols] = v.astype(f32) * dv
         ds_out[c] += ds
-        ahead[rows, :] -= dot2(prod[...], red[...])
+    ahead[...] -= dot2(prod[...], red[...])
 
 
 def conv_back(cur, params, masks, rows, width):
@@ -530,18 +537,20 @@
 def back_state_kernel(*refs, hops):
     grads_in, refs = refs[:hops], refs[hops:]
     (states, gh, sc, dv, u, params, bc, c_t, tables, keep, decays, ex, red, ds, ahead, allowed, rows_in, masks, lx_out, gbc_out,
-     ldt_out, edges, tail, db, dc, behind, direct, carry) = refs
+     ldt_out, edges, tail, db, dc, behind, direct, carry, prods, carries) = refs
     state = c_t.shape[0]
     g = pl.program_id(0)
 
     @pl.when(g == 0)
     def _():
-        for ref in (db, dc, behind, direct, carry):
+        for ref in (db, dc, behind, direct, carry, carries):
             ref[...] = jnp.zeros_like(ref)
 
     own, width = lx_out.shape
     step = min(width, 256)
     blocks = own // chunk
+    dt_wide, in_wide = dot(tables[:, :lanes], ex[...]), dot(tables[:, 2 * lanes : 3 * lanes], ex[...])
+    out_wide = dot(tables[:, 3 * lanes :], ex[...])
     for n in range(width // step):
         cols = slice(n * step, (n + 1) * step)
         gs = sum(r[:, cols].astype(f32) for r in grads_in)
@@ -552,20 +561,20 @@
             kept = keep[c : c + 1, cols]
             low_s = states[c, :, cols]
             scaled = sc[rows, cols].astype(f32)
-            eo = dot(tables[rows, 3 * lanes :], ex[:, cols])
+            eo = out_wide[rows, cols]
             dvs = eo * dot(bc[rows, :state], low_g)
             db[rows, :] += dot_nt((eo * scaled).astype(bf16), low_g)
             dy = gh[rows, cols]
-            moved = (dot(tables[rows, 2 * lanes : 3 * lanes], ex[:, cols]) * dy).astype(bf16)
+            moved = (in_wide[rows, cols] * dy).astype(bf16)
             dc[rows, :] += dot_nt(moved, low_s)
             carried = jnp.sum(low_s.astype(f32) * gs, axis=0, keepdims=True) * kept
-            carry[c : c + 1, :] += dot2(jnp.broadcast_to(carried, (8, step)), red[cols, :])[:1]
+            carries[c : c + 1, cols] = carried
             gs = gs * kept + dot(c_t[:, rows], moved)
             g_sc = dv[rows, cols] + dvs
             v, slope = silu_parts(u[rows, cols])
-            behind[rows, :] += dot2(scaled * dvs, red[cols, :])
-            direct[rows, :] += dot2(v * g_sc, red[cols, :])
-            g_v = dot(tables[rows, :lanes], ex[:, cols]) * g_sc + params[0, 6:7, cols] * dy
+            prods[0, rows, cols] = scaled * dvs
+            prods[1, rows, cols] = v * g_sc
+            g_v = dt_wide[rows, cols] * g_sc + params[0, 6:7, cols] * dy
             g_u = g_v * slope
             g_x = conv_back(jnp.concatenate([g_u, following], axis=0), params[0, :, cols], masks, rows, step)
             lx_out[rows, cols] = g_x.astype(bf16)
@@ -575,6 +584,9 @@
             if c == 0:
                 at = pl.ds(pl.multiple_of(g * width + n * step, lanes), step)
                 edges[:, at] = g_u[:edge].astype(bf16)
+    behind[...] += dot2(prods[0], red[...])
+    direct[...] += dot2(prods[1], red[...])
+    carry[...] += dot2(carries[...], red[...])
 
     @pl.when(g == pl.num_programs(0) - 1)
     def _():
@@ -689,16 +701,18 @@
             )
 
 
-def collect_kernel(picks, arrived, up_out, down_out, down_in, up_in):
+def collect_kernel(picks, arrived, up_out, down_out, down_in, up_in, sums):
     dp, tp, rows, _ = arrived.shape
     rank = rows // 4
+    for d in range(dp):
+        one = arrived[d, 0].astype(f32)
+        for t in range(1, tp):
+            one = one + arrived[d, t].astype(f32)
+        sums[d] = one
     for b in range(up_out.shape[0]):
         total = jnp.zeros(arrived.shape[2:], f32)
         for d in range(dp):
-            one = arrived[d, 0].astype(f32)
-            for t in range(1, tp):
-                one = one + arrived[d, t].astype(f32)
-            total = total + jnp.where(picks[d] == b, one, 0.0)
+            total = total + jnp.where(picks[d] == b, sums[d], 0.0)
         up_out[b] = total[:rank, : up_out.shape[2]]
         down_out[b] = total[rank : 2 * rank].T[: down_out.shape[1]]
         down_in[b] = total[2 * rank : 3 * rank, : down_in.shape[2]]
@@ -1084,7 +1098,7 @@
         [pltpu.VMEM(big3, f32), pltpu.VMEM(big3, f32), pltpu.VMEM(big3, f32), pltpu.VMEM(big3, f32),
          pltpu.VMEM(big3, f32),
          pltpu.VMEM((own, lanes), f32), pltpu.VMEM((own, lanes), f32), pltpu.VMEM((own, width), f32),
-         pltpu.VMEM((own, width), bf16), pltpu.VMEM((own, rank), f32), pltpu.VMEM((own, rank), f32),
+         pltpu.VMEM((own, width), bf16), pltpu.VMEM((own, 2 * rank), bf16), pltpu.VMEM((own, rank), f32),
          pltpu.VMEM((own, group), bf16)],
         4 * mat, 40 * mega, (3, tp_size), grant=vmem_bytes * 5 // 4,
     )(sel, normed_moved, *w_z, *w_out, *states_in, ranks_own, ups, params, y_within, u, scaled, tables, tables, keep,
@@ -1095,7 +1109,7 @@
         [(big, f32), ((blocks, chunk, chunk), f32), ((own, lanes), f32)],
         [cols(own), full(own, lanes)] + within_specs + [red_spec],
         [cols(own), full(blocks, chunk, chunk), full(own, lanes)],
-        [pltpu.VMEM((chunk, group), f32)],
+        [pltpu.VMEM((own, group), f32)],
         2 * mat, 14 * mega, grant=vmem_bytes * 5 // 4,
     )(sel, g_heads, ahead_sums, scaled, tables, cums_t, scores, exl, red)
     grads_in, moved_grad = chain(sent_grad, down, 1, ahead)
@@ -1122,7 +1136,8 @@
            masks_after_spec],
         [cols(own), full(own, 2 * state), full(own, heads), full(*edges_shape), cols(edge)],
         [pltpu.VMEM((own, state), f32), pltpu.VMEM((own, state), f32), pltpu.VMEM((own, lanes), f32),
-         pltpu.VMEM((own, lanes), f32), pltpu.VMEM((8, lanes), f32)],
+         pltpu.VMEM((own, lanes), f32), pltpu.VMEM((8, lanes), f32), pltpu.VMEM((2, own, group), f32),
+         pltpu.VMEM((8, group), f32)],
         mat, 24 * mega,
     )(sel, *grads_in, states, g_heads, scaled, d_within, u, params, bc, bc_t, tables, keep, keep, ex, red, d_scores,
       ahead, scores, rows_f32, masks)
@@ -1158,7 +1173,7 @@
     shapes = [(adapters, rank, d_rows), (adapters, hp, rank), (adapters, rank, d_rows), (adapters, 2 * hp, rank)]
     grad_out_up, grad_out_down, grad_in_down, grad_in_up = call(
         selecting(collect_kernel), [(s, f32) for s in shapes], [full(*sent.shape)],
-        [full(*s) for s in shapes], [], mega, mega, 1,
+        [full(*s) for s in shapes], [pltpu.VMEM((dp_size,) + sent.shape[2:], f32)], mega, mega, 1,
     )(picks, arrived)
 
     grad_out_down = grad_out_down.reshape(out_down.shape)

time: 256 us -> 253 us (0.988)
  Pallas kernels: 127 us -> 123 us
  transfers between devices with their start and end apart: 49 -> 49, of which waited for: 12 -> 12; matrix products, arithmetic and copies ran while one was open for 9% -> 9% of each run, Pallas kernels for 25% -> 24%
where the time goes in v4:
time: 253 us; the launch traced here: 252 us
  Pallas kernels  123 us (49%)
  starting transfers between devices  64.7 us (26%)
  waiting for transfers between devices  32.9 us (13%)
  other arithmetic  14.7 us (6%)
  local copies, waits for them, and re-layouts  13.9 us (5%)
    pallas_call x1, Pallas kernels, shards(): call(selecting(middle_kernel, weights=n_w, hops=hops, inner=inner), [((bl...  36.8 us
    ppermute x25, starting transfers between devices, swap(): return lax.ppermute(x, 'dp', [(i, i ^ 1 << bit) for i in range(n)])  24.3 us
    ppermute x15, starting transfers between devices, around_tensor(): lax.ppermute(x, 'tensor', [(i, (i + s) % n) for i in range(n)])  19.8 us
    pallas_call x1, Pallas kernels, shards(): call(plain(back_state_kernel, hops=hops), [(big, bf16), ((own, 2 * state)...  18 us
    ppermute x3, waiting for transfers between devices, down(): return lax.ppermute(x, 'tensor', [(i + 1, i) for i in range(n - 1)])  12.6 us
    pallas_call x1, Pallas kernels, shards(): call(plain(proj_kernel, weights=n_w), [(big, f32), (big, bf16), ((state,...  12.6 us
    pallas_call x1, Pallas kernels, shards(): call(selecting(tokens_kernel, weights=n_w), [((own, width), f32)], [cols(...  12.2 us
    pallas_call x1, Pallas kernels, shards(): call(plain(back_within_kernel), [(big, f32), ((blocks, chunk, chunk), f32...  12 us
  transfers between devices with their start and end apart: 49, of which 12 were waited for; matrix products, arithmetic and copies ran while one was open for 9% of the time, Pallas kernels for 24%

profile of v4, /device:TPU:1, one launch (start us, length us, event | category | flops | bytes accessed | tf_op | source)
XLA Modules:
  0.0 252.0 jit_solution(11061138626236827988)
XLA Ops:
  2.2 3.2 %collective-permute-start.11 = (bf16[128,512]{1,0:T(8,128)(2,1)S(1)}, bf16[128,512]{1,0:T(8,128)(2,1)S(1)}, u32[]{:S(2)}, u32[]{:S(2)}) collective-permute-start(bf16[128,512]{1,0:T(8,128)(2,1)S(1)} %bitcast.117), channel_id=1, source_target_pairs={{0,2},{1,3},{2,0},{3,1},{4,6},{5,7},{6,4},{7,5},{8,10},{9,11},{10,... | collective-permute-start | bytes 393224 | tf_op jit(solution)/shard_map/ppermute | solution.py:734
  6.7 2.0 collective-permute-start.12
  9.4 1.9 pack_kernel.1
  23.0 3.5 %collective-permute-done.2 = bf16[2,800,128]{2,1,0:T(8,128)(2,1)S(1)} collective-permute-done((bf16[2,800,128]{2,1,0:T(8,128)(2,1)S(1)}, bf16[2,800,128]{2,1,0:T(8,128)(2,1)S(1)}, u32[]{:S(2)}, u32[]{:S(2)}) %collective-permute-start.2) | collective-permute-done | bytes 409632 | tf_op jit(solution)/shard_map/ppermute | solution.py:752
  28.9 3.3 %collective-permute-start.3 = (bf16[4,800,128]{2,1,0:T(8,128)(2,1)}, bf16[4,800,128]{2,1,0:T(8,128)(2,1)}, u32[]{:S(2)}, u32[]{:S(2)}) collective-permute-start(bf16[4,800,128]{2,1,0:T(8,128)(2,1)} %pad_maximum_fusion.1), channel_id=1, source_target_pairs={{0,4},{4,0},{8,12},{12,8},{16,20},{20,16},{24,28},{28,24},{1,5},{5... | collective-permute-start | bytes 2457608 | tf_op jit(solution)/shard_map/ppermute | solution.py:739
  36.4 2.3 collective-permute-start.8
  41.2 2.0 collective-permute-done.7
  49.4 3.1 %collective-permute-start.6 = (bf16[320,128]{1,0:T(8,128)(2,1)S(1)}, bf16[320,128]{1,0:T(8,128)(2,1)S(1)}, u32[]{:S(2)}, u32[]{:S(2)}) collective-permute-start(bf16[320,128]{1,0:T(8,128)(2,1)S(1)} %get-tuple-element.121), channel_id=1, source_target_pairs={{0,3},{1,0},{2,1},{3,2},{4,7},{5,4},{6,5},{7,6},{8,11},{9,8},{10,9... | collective-permute-start | bytes 245768 | tf_op jit(solution)/shard_map/ppermute | solution.py:734
  52.6 1.9 pad_maximum_fusion.3.refs_5_
  55.7 2.5 %collective-permute-done.37.refs_2_ = bf16[2,2,128,512]{3,2,1,0:T(8,128)(2,1)} collective-permute-done((bf16[2,2,128,512]{3,2,1,0:T(8,128)(2,1)S(1)}, bf16[2,2,128,512]{3,2,1,0:T(8,128)(2,1)}, u32[]{:S(2)}, u32[]{:S(2)}) %collective-permute-start.37) | collective-permute-done | bytes 524320 | tf_op jit(solution)/shard_map/ppermute | solution.py:739
  58.3 2.2 collective-permute-start.41
  63.1 9.2 %prep_kernel.1 = (bf16[528,1024]{1,0:T(8,128)(2,1)}, bf16[512,1024]{1,0:T(8,128)(2,1)}, bf16[528,32]{1,0:T(8,128)(2,1)}, bf16[512,32]{1,0:T(8,128)(2,1)}, bf16[5...) custom-call(s32[33]{0:T(128)} %concatenate.42.sel_ref, ...), custom_call_target="tpu_custom_call" | custom-call | flops 536870912 | bytes 6291456 | tf_op jit(solution)/shard_map/prep_kernel/pallas_call | solution.py:1006
  74.9 2.7 %collective-permute-start.32 = (bf16[128,512]{1,0:T(8,128)(2,1)S(1)}, bf16[128,512]{1,0:T(8,128)(2,1)S(1)}, u32[]{:S(2)}, u32[]{:S(2)}) collective-permute-start(bf16[128,512]{1,0:T(8,128)(2,1)S(1)} %bitcast.127), channel_id=1, source_target_pairs={{0,3},{1,0},{2,1},{3,2},{4,7},{5,4},{6,5},{7,6},{8,11},{9,8},{10,9... | collective-permute-start | bytes 393224 | tf_op jit(solution)/shard_map/ppermute | solution.py:734
  78.9 12.6 %proj_kernel.1 = (f32[512,2048]{1,0:T(8,128)}, bf16[512,2048]{1,0:T(8,128)(2,1)}, bf16[128,2048]{1,0:T(8,128)(2,1)}) custom-call(s32[33]{0:T(128)} %concatenate.42.sel_ref, bf16[528,1024]{1,0:T(8,128)(2,1)} %get-tuple-element.62.refs_0_, bf16[2,2,128,512]{3,2,1,0:T(8,128)(2,1)} %copy-done.36, bf16[2,2,128,512]{3,2,1,0:T(8,128)(2,1)} %collective-permute-done.37.refs_2_, ...), custom_call_target="tpu_custom_call" | custom-call | flops 2147483648 | bytes 12582912 | tf_op jit(solution)/shard_map/proj_kernel/pallas_call | solution.py:1032
  91.5 1.9 collective-permute-start.24
  93.4 2.5 collective-permute-start.43
  99.5 3.8 %collective-permute-done.33 = bf16[2,128,512]{2,1,0:T(8,128)(2,1)S(1)} collective-permute-done((bf16[2,128,512]{2,1,0:T(8,128)(2,1)S(1)}, bf16[2,128,512]{2,1,0:T(8,128)(2,1)S(1)}, u32[]{:S(2)}, u32[]{:S(2)}) %collective-permute-start.33) | collective-permute-done | bytes 262176 | tf_op jit(solution)/shard_map/ppermute | solution.py:739
  105.1 2.1 collective-permute-done.43.refs_17_
  109.7 4.4 %collective-permute-start.44 = (bf16[128,2048]{1,0:T(8,128)(2,1)S(1)}, bf16[128,2048]{1,0:T(8,128)(2,1)S(1)}, u32[]{:S(2)}, u32[]{:S(2)}) collective-permute-start(bf16[128,2048]{1,0:T(8,128)(2,1)S(1)} %multiply_convert_fusion.1), channel_id=1, source_target_pairs={{0,1},{1,2},{2,3},{4,5},{5,6},{6,7},{8,9},{9,10},{10,11},{12,13},{... | collective-permute-start | bytes 1572872 | tf_op jit(solution)/shard_map/ppermute | solution.py:724
  114.1 4.4 %collective-permute-done.34.refs_14_ = bf16[2,2,128,512]{3,2,1,0:T(8,128)(2,1)S(1)} collective-permute-done((bf16[2,2,128,512]{3,2,1,0:T(8,128)(2,1)S(1)}, bf16[2,2,128,512]{3,2,1,0:T(8,128)(2,1)S(1)}, u32[]{:S(2)}, u32[]{:S(2)}) %collective-permute-start.34) | collective-permute-done | bytes 524320 | tf_op jit(solution)/shard_map/ppermute | solution.py:739
  119.5 2.0 collective-permute-start.30
  122.8 5.1 %within_kernel.1.refs_22_ = f32[512,2048]{1,0:T(8,128)} custom-call(s32[33]{0:T(128)S(1)} %copy-done.26, bf16[512,2048]{1,0:T(8,128)(2,1)S(1)} %copy-done.1, bf16[512,768]{1,0:T(8,128)(2,1)S(1)} %copy-done.2, f32[4,4,8,128]{3,2,1,0:T(8,128)S(1)} %copy-done.25, f32[2,4,128,128]{3,2,1,0:T(8,128)S(1)} %copy-done.5, bf16[128,4096]{1,0:T(8,128)(2,1)S(1)} %copy-done.10), custom_call_target="tpu_custom_call" | custom-call | flops 2147483648 | bytes 6291456 | tf_op jit(solution)/shard_map/within_kernel/pallas_call | solution.py:1053
  129.7 36.8 %middle_kernel.1 = (bf16[4,128,2048]{2,1,0:T(8,128)(2,1)}, f32[512,1024]{1,0:T(8,128)}, bf16[8,4,32,128]{3,2,1,0:T(8,128)(2,1)}, f32[512,2048]{1,0:T(8,128)}, bf...) custom-call(s32[33]{0:T(128)} %concatenate.42.sel_ref, ...), custom_call_target="tpu_custom_call" | custom-call | flops 8589934592 | bytes 41943040 | tf_op jit(solution)/shard_map/middle_kernel/pallas_call | solution.py:1085
  167.9 12.0 %back_within_kernel.1 = (f32[512,2048]{1,0:T(8,128)}, f32[4,128,128]{2,1,0:T(8,128)}, f32[512,128]{1,0:T(8,128)}) custom-call(s32[33]{0:T(128)} %concatenate.42.sel_ref, f32[512,2048]{1,0:T(8,128)} %get-tuple-element.87.refs_0_.refs_3_, f32[512,128]{1,0:T(8,128)} %get-tuple-element.88.refs_1_, ...), custom_call_target="tpu_custom_call" | custom-call | flops 4294967296 | bytes 14680064 | tf_op jit(solution)/shard_map/back_within_kernel/pallas_call | solution.py:1107
  179.9 3.2 %collective-permute-done.45.refs_0_ = bf16[128,2048]{1,0:T(8,128)(2,1)S(1)} collective-permute-done((bf16[128,2048]{1,0:T(8,128)(2,1)}, bf16[128,2048]{1,0:T(8,128)(2,1)S(1)}, u32[]{:S(2)}, u32[]{:S(2)}) %collective-permute-start.45) | collective-permute-done | bytes 524320 | tf_op jit(solution)/shard_map/ppermute | solution.py:729
  184.9 8.2 %in_z_kernel.1 = (f32[512,1024]{1,0:T(8,128)}, f32[512,16]{1,0:T(8,128)S(1)}, f32[4,16,512]{2,1,0:T(8,128)S(1)}) custom-call(s32[33]{0:T(128)S(1)} %copy-done.27, bf16[512,2048]{1,0:T(8,128)(2,1)} %get-tuple-element.91.refs_0_, bf16[2,2,128,512]{3,2,1,0:T(8,128)(2,1)S(1)} %copy-done.16, bf16[2,2,128,512]{3,2,1,0:T(8,128)(2,1)} %collective-permute-done.17.refs_2_, ...), custom_call_target="tpu_custom_call" | custom-call | flops 2147483648 | bytes 8388608 | tf_op jit(solution)/shard_map/in_z_kernel/pallas_call | solution.py:1118
  193.2 5.6 %collective-permute-done.46.refs_1_ = bf16[128,2048]{1,0:T(8,128)(2,1)S(1)} collective-permute-done((bf16[128,2048]{1,0:T(8,128)(2,1)S(1)}, bf16[128,2048]{1,0:T(8,128)(2,1)S(1)}, u32[]{:S(2)}, u32[]{:S(2)}) %collective-permute-start.46) | collective-permute-done | bytes 524320 | tf_op jit(solution)/shard_map/ppermute | solution.py:729
  198.9 18.0 %back_state_kernel.1 = (bf16[512,2048]{1,0:T(8,128)(2,1)}, f32[512,256]{1,0:T(8,128)S(1)}, bf16[512,32]{1,0:T(8,128)(2,1)S(1)}, bf16[16,2304]{1,0:T(8,128)(2,1)S(1)}, f32[16,2048]{1,0:T(8,128)S(1)}) custom-call(s32[33]{0:T(128)S(1)} %copy-done.27, bf16[128,2048]{1,0:T(8,128)(2,1)S(1)} %collective-permute-done.45.refs_0_, ...), custom_call_target="tpu_custom_call" | custom-call | flops 2147483648 | bytes 25165824 | tf_op jit(solution)/shard_map/back_state_kernel/pallas_call | solution.py:1129
  218.2 3.8 %collective-permute-done.47.refs_2_.refs_12_ = bf16[16,2304]{1,0:T(8,128)(2,1)S(1)} collective-permute-done((bf16[16,2304]{1,0:T(8,128)(2,1)S(1)}, bf16[16,2304]{1,0:T(8,128)(2,1)S(1)}, u32[]{:S(2)}, u32[]{:S(2)}) %collective-permute-start.47) | collective-permute-done | bytes 73760 | tf_op jit(solution)/shard_map/ppermute | solution.py:729
  222.0 5.5 %in_x_kernel.1 = (bf16[512,2048]{1,0:T(8,128)(2,1)}, f32[512,16]{1,0:T(8,128)S(1)}, bf16[8,4,32,128]{3,2,1,0:T(8,128)(2,1)S(1)}) custom-call(s32[33]{0:T(128)S(1)} %copy-done.27, bf16[512,2048]{1,0:T(8,128)(2,1)} %get-tuple-element.99.refs_0_, f32[16,2048]{1,0:T(8,128)S(1)} %get-tuple-element.100.refs_1_, ...), custom_call_target="tpu_custom_call", output_to_operand_aliasing={{0}: (1, {})} | custom-call | flops 268435456 | bytes 8388608 | tf_op jit(solution)/shard_map/in_x_kernel/pallas_call | solution.py:1146
  229.1 5.8 %all-to-all-start = ((bf16[32,64,128]{2,1,0:T(8,128)(2,1)}), bf16[32,64,128]{2,1,0:T(8,128)(2,1)S(1)}, u32[]{:S(2)}, u32[]{:S(2)}) async-start(bf16[32,64,128]{2,1,0:T(8,128)(2,1)} %bitcast.72), calls=%async_computation | async-start | bytes 1048576 | tf_op jit(solution)/shard_map/all_to_all | solution.py:1171
  236.5 12.2 %tokens_kernel.1 = f32[512,1024]{1,0:T(8,128)} custom-call(s32[33]{0:T(128)} %concatenate.42.sel_ref, bf16[512,2048]{1,0:T(8,128)(2,1)} %get-tuple-element.105.refs_0_, bf16[2,2,128,512]{3,2,1,0:T(8,128)(2,1)} %copy-done.36, bf16[2,2,128,512]{3,2,1,0:T(8,128)(2,1)} %collective-permute-done.37.refs_2_, ...), custom_call_target="tpu_custom_call" | custom-call | flops 2147483648 | bytes 14680064 | tf_op jit(solution)/shard_map/tokens_kernel/pallas_call | solution.py:1156
  (286 shorter events, 59.9 us)
Async XLA Ops:
  2.2 16.9 %collective-permute-start.11 = (bf16[128,512]{1,0:T(8,128)(2,1)S(1)}, bf16[128,512]{1,0:T(8,128)(2,1)S(1)}, u32[]{:S(2)}, u32[]{:S(2)}) collective-permute-start(bf16[128,512]{1,0:T(8,128)(2,1)S(1)} %bitcast.117), channel_id=1, source_target_pairs={{0,2},{1,3},{2,0},{3,1},{4,6},{5,7},{6,4},{7,5},{8,10},{9,11},{10,... | collective-permute-start | bytes 393224 | tf_op jit(solution)/shard_map/ppermute | solution.py:734
  5.4 13.7 %collective-permute-start.10 = (bf16[128,512]{1,0:T(8,128)(2,1)S(1)}, bf16[128,512]{1,0:T(8,128)(2,1)S(1)}, u32[]{:S(2)}, u32[]{:S(2)}) collective-permute-start(bf16[128,512]{1,0:T(8,128)(2,1)S(1)} %bitcast.118), channel_id=1, source_target_pairs={{0,1},{1,2},{2,3},{3,0},{4,5},{5,6},{6,7},{7,4},{8,9},{9,10},{10,1... | collective-permute-start | bytes 393224 | tf_op jit(solution)/shard_map/ppermute | solution.py:734
  6.7 12.4 %collective-permute-start.12 = (bf16[128,512]{1,0:T(8,128)(2,1)S(1)}, bf16[128,512]{1,0:T(8,128)(2,1)S(1)}, u32[]{:S(2)}, u32[]{:S(2)}) collective-permute-start(bf16[128,512]{1,0:T(8,128)(2,1)S(1)} %bitcast.119), channel_id=1, source_target_pairs={{0,3},{1,0},{2,1},{3,2},{4,7},{5,4},{6,5},{7,6},{8,11},{9,8},{10,9... | collective-permute-start | bytes 393224 | tf_op jit(solution)/shard_map/ppermute | solution.py:734
  19.1 15.0 %collective-permute-start.21 = (bf16[128,512]{1,0:T(8,128)(2,1)S(1)}, bf16[128,512]{1,0:T(8,128)(2,1)S(1)}, u32[]{:S(2)}, u32[]{:S(2)}) collective-permute-start(bf16[128,512]{1,0:T(8,128)(2,1)S(1)} %bitcast.121), channel_id=1, source_target_pairs={{0,3},{1,0},{2,1},{3,2},{4,7},{5,4},{6,5},{7,6},{8,11},{9,8},{10,9... | collective-permute-start | bytes 393224 | tf_op jit(solution)/shard_map/ppermute | solution.py:734
  19.3 14.9 %collective-permute-start.20 = (bf16[128,512]{1,0:T(8,128)(2,1)S(1)}, bf16[128,512]{1,0:T(8,128)(2,1)S(1)}, u32[]{:S(2)}, u32[]{:S(2)}) collective-permute-start(bf16[128,512]{1,0:T(8,128)(2,1)S(1)} %bitcast.122), channel_id=1, source_target_pairs={{0,2},{1,3},{2,0},{3,1},{4,6},{5,7},{6,4},{7,5},{8,10},{9,11},{10,... | collective-permute-start | bytes 393224 | tf_op jit(solution)/shard_map/ppermute | solution.py:734
  21.7 13.2 %collective-permute-start.14 = (bf16[2,128,512]{2,1,0:T(8,128)(2,1)S(1)}, bf16[2,128,512]{2,1,0:T(8,128)(2,1)S(1)}, u32[]{:S(2)}, u32[]{:S(2)}) collective-permute-start(bf16[2,128,512]{2,1,0:T(8,128)(2,1)S(1)} %pad_maximum_fusion.14), channel_id=1, source_target_pairs={{0,8},{4,12},{8,0},{12,4},{16,24},{20,28},{24,16},{28,20},{1,9},{5... | collective-permute-start | bytes 786440 | tf_op jit(solution)/shard_map/ppermute | solution.py:739
  28.9 15.5 %collective-permute-start.3 = (bf16[4,800,128]{2,1,0:T(8,128)(2,1)}, bf16[4,800,128]{2,1,0:T(8,128)(2,1)}, u32[]{:S(2)}, u32[]{:S(2)}) collective-permute-start(bf16[4,800,128]{2,1,0:T(8,128)(2,1)} %pad_maximum_fusion.1), channel_id=1, source_target_pairs={{0,4},{4,0},{8,12},{12,8},{16,20},{20,16},{24,28},{28,24},{1,5},{5... | collective-permute-start | bytes 2457608 | tf_op jit(solution)/shard_map/ppermute | solution.py:739
  40.9 13.5 %collective-permute-start.40 = (bf16[2,2,128,512]{3,2,1,0:T(8,128)(2,1)S(1)}, bf16[2,2,128,512]{3,2,1,0:T(8,128)(2,1)}, u32[]{:S(2)}, u32[]{:S(2)}) collective-permute-start(bf16[2,2,128,512]{3,2,1,0:T(8,128)(2,1)S(1)} %pad_maximum_fusion.7.refs_5_), channel_id=1, source_target_pairs={{0,8},{4,12},{8,0},{12,4},{16,24},{20,28},{24,16},{28,20},{1,9},{5... | collective-permute-start | bytes 1572872 | tf_op jit(solution)/shard_map/ppermute | solution.py:739
  43.1 15.1 %collective-permute-start.37 = (bf16[2,2,128,512]{3,2,1,0:T(8,128)(2,1)S(1)}, bf16[2,2,128,512]{3,2,1,0:T(8,128)(2,1)}, u32[]{:S(2)}, u32[]{:S(2)}) collective-permute-start(bf16[2,2,128,512]{3,2,1,0:T(8,128)(2,1)S(1)} %pad_maximum_fusion.6.refs_1_), channel_id=1, source_target_pairs={{0,16},{4,20},{8,24},{12,28},{16,0},{20,4},{24,8},{28,12},{1,17},{... | collective-permute-start | bytes 1572872 | tf_op jit(solution)/shard_map/ppermute | solution.py:739
  48.4 12.1 %collective-permute-start.5 = (bf16[320,128]{1,0:T(8,128)(2,1)S(1)}, bf16[320,128]{1,0:T(8,128)(2,1)S(1)}, u32[]{:S(2)}, u32[]{:S(2)}) collective-permute-start(bf16[320,128]{1,0:T(8,128)(2,1)S(1)} %get-tuple-element.121), channel_id=1, source_target_pairs={{0,2},{1,3},{2,0},{3,1},{4,6},{5,7},{6,4},{7,5},{8,10},{9,11},{10,... | collective-permute-start | bytes 245768 | tf_op jit(solution)/shard_map/ppermute | solution.py:734
  49.3 11.3 %collective-permute-start.4 = (bf16[320,128]{1,0:T(8,128)(2,1)S(1)}, bf16[320,128]{1,0:T(8,128)(2,1)S(1)}, u32[]{:S(2)}, u32[]{:S(2)}) collective-permute-start(bf16[320,128]{1,0:T(8,128)(2,1)S(1)} %get-tuple-element.121), channel_id=1, source_target_pairs={{0,1},{1,2},{2,3},{3,0},{4,5},{5,6},{6,7},{7,4},{8,9},{9,10},{10,1... | collective-permute-start | bytes 245768 | tf_op jit(solution)/shard_map/ppermute | solution.py:734
  49.4 11.5 %collective-permute-start.6 = (bf16[320,128]{1,0:T(8,128)(2,1)S(1)}, bf16[320,128]{1,0:T(8,128)(2,1)S(1)}, u32[]{:S(2)}, u32[]{:S(2)}) collective-permute-start(bf16[320,128]{1,0:T(8,128)(2,1)S(1)} %get-tuple-element.121), channel_id=1, source_target_pairs={{0,3},{1,0},{2,1},{3,2},{4,7},{5,4},{6,5},{7,6},{8,11},{9,8},{10,9... | collective-permute-start | bytes 245768 | tf_op jit(solution)/shard_map/ppermute | solution.py:734
  58.3 16.0 %collective-permute-start.41 = (bf16[2,2,128,512]{3,2,1,0:T(8,128)(2,1)S(1)}, bf16[2,2,128,512]{3,2,1,0:T(8,128)(2,1)}, u32[]{:S(2)}, u32[]{:S(2)}) collective-permute-start(bf16[2,2,128,512]{3,2,1,0:T(8,128)(2,1)S(1)} %pad_maximum_fusion.7.refs_5_), channel_id=1, source_target_pairs={{0,4},{4,0},{8,12},{12,8},{16,20},{20,16},{24,28},{28,24},{1,5},{5... | collective-permute-start | bytes 1572872 | tf_op jit(solution)/shard_map/ppermute | solution.py:739
  60.5 14.5 %collective-permute-start.38 = (bf16[2,2,128,512]{3,2,1,0:T(8,128)(2,1)S(1)}, bf16[2,2,128,512]{3,2,1,0:T(8,128)(2,1)}, u32[]{:S(2)}, u32[]{:S(2)}) collective-permute-start(bf16[2,2,128,512]{3,2,1,0:T(8,128)(2,1)S(1)} %pad_maximum_fusion.6.refs_1_), channel_id=1, source_target_pairs={{0,4},{4,0},{8,12},{12,8},{16,20},{20,16},{24,28},{28,24},{1,5},{5... | collective-permute-start | bytes 1572872 | tf_op jit(solution)/shard_map/ppermute | solution.py:739
  60.5 17.1 %collective-permute-start.42 = (bf16[2,2,128,512]{3,2,1,0:T(8,128)(2,1)}, bf16[2,2,128,512]{3,2,1,0:T(8,128)(2,1)}, u32[]{:S(2)}, u32[]{:S(2)}) collective-permute-start(bf16[2,2,128,512]{3,2,1,0:T(8,128)(2,1)} %collective-permute-done.40.refs_6_), channel_id=1, source_target_pairs={{0,4},{4,0},{8,12},{12,8},{16,20},{20,16},{24,28},{28,24},{1,5},{5... | collective-permute-start | bytes 1572872 | tf_op jit(solution)/shard_map/ppermute | solution.py:739
  61.0 16.6 %collective-permute-start.39 = (bf16[2,2,128,512]{3,2,1,0:T(8,128)(2,1)}, bf16[2,2,128,512]{3,2,1,0:T(8,128)(2,1)}, u32[]{:S(2)}, u32[]{:S(2)}) collective-permute-start(bf16[2,2,128,512]{3,2,1,0:T(8,128)(2,1)} %collective-permute-done.37.refs_2_), channel_id=1, source_target_pairs={{0,4},{4,0},{8,12},{12,8},{16,20},{20,16},{24,28},{28,24},{1,5},{5... | collective-permute-start | bytes 1572872 | tf_op jit(solution)/shard_map/ppermute | solution.py:739
  62.5 10.7 %collective-permute-start.26 = (bf16[128,512]{1,0:T(8,128)(2,1)S(1)}, bf16[128,512]{1,0:T(8,128)(2,1)S(1)}, u32[]{:S(2)}, u32[]{:S(2)}) collective-permute-start(bf16[128,512]{1,0:T(8,128)(2,1)S(1)} %bitcast.125), channel_id=1, source_target_pairs={{0,1},{1,2},{2,3},{3,0},{4,5},{5,6},{6,7},{7,4},{8,9},{9,10},{10,1... | collective-permute-start | bytes 393224 | tf_op jit(solution)/shard_map/ppermute | solution.py:734
  73.1 25.4 %collective-permute-start.23 = (bf16[2,2,128,512]{3,2,1,0:T(8,128)(2,1)}, bf16[2,2,128,512]{3,2,1,0:T(8,128)(2,1)}, u32[]{:S(2)}, u32[]{:S(2)}) collective-permute-start(bf16[2,2,128,512]{3,2,1,0:T(8,128)(2,1)} %pad_maximum_fusion.3.refs_5_), channel_id=1, source_target_pairs={{0,8},{4,12},{8,0},{12,4},{16,24},{20,28},{24,16},{28,20},{1,9},{5... | collective-permute-start | bytes 1572872 | tf_op jit(solution)/shard_map/ppermute | solution.py:739
  74.3 25.2 %collective-permute-start.17 = (bf16[2,2,128,512]{3,2,1,0:T(8,128)(2,1)S(1)}, bf16[2,2,128,512]{3,2,1,0:T(8,128)(2,1)}, u32[]{:S(2)}, u32[]{:S(2)}) collective-permute-start(bf16[2,2,128,512]{3,2,1,0:T(8,128)(2,1)S(1)} %pad_maximum_fusion.2.refs_1_), channel_id=1, source_target_pairs={{0,16},{4,20},{8,24},{12,28},{16,0},{20,4},{24,8},{28,12},{1,17},{... | collective-permute-start | bytes 1572872 | tf_op jit(solution)/shard_map/ppermute | solution.py:739
  74.9 16.6 %collective-permute-start.32 = (bf16[128,512]{1,0:T(8,128)(2,1)S(1)}, bf16[128,512]{1,0:T(8,128)(2,1)S(1)}, u32[]{:S(2)}, u32[]{:S(2)}) collective-permute-start(bf16[128,512]{1,0:T(8,128)(2,1)S(1)} %bitcast.127), channel_id=1, source_target_pairs={{0,3},{1,0},{2,1},{3,2},{4,7},{5,4},{6,5},{7,6},{8,11},{9,8},{10,9... | collective-permute-start | bytes 393224 | tf_op jit(solution)/shard_map/ppermute | solution.py:734
  77.6 15.8 %collective-permute-start.31 = (bf16[128,512]{1,0:T(8,128)(2,1)S(1)}, bf16[128,512]{1,0:T(8,128)(2,1)S(1)}, u32[]{:S(2)}, u32[]{:S(2)}) collective-permute-start(bf16[128,512]{1,0:T(8,128)(2,1)S(1)} %bitcast.128), channel_id=1, source_target_pairs={{0,2},{1,3},{2,0},{3,1},{4,6},{5,7},{6,4},{7,5},{8,10},{9,11},{10,... | collective-permute-start | bytes 393224 | tf_op jit(solution)/shard_map/ppermute | solution.py:734
  77.6 18.4 %collective-permute-start.27 = (bf16[2,128,512]{2,1,0:T(8,128)(2,1)}, bf16[2,128,512]{2,1,0:T(8,128)(2,1)S(1)}, u32[]{:S(2)}, u32[]{:S(2)}) collective-permute-start(bf16[2,128,512]{2,1,0:T(8,128)(2,1)} %pad_maximum_fusion.17), channel_id=1, source_target_pairs={{0,8},{4,12},{8,0},{12,4},{16,24},{20,28},{24,16},{28,20},{1,9},{5... | collective-permute-start | bytes 786440 | tf_op jit(solution)/shard_map/ppermute | solution.py:739
  91.5 13.3 %collective-permute-start.24 = (bf16[2,2,128,512]{3,2,1,0:T(8,128)(2,1)}, bf16[2,2,128,512]{3,2,1,0:T(8,128)(2,1)}, u32[]{:S(2)}, u32[]{:S(2)}) collective-permute-start(bf16[2,2,128,512]{3,2,1,0:T(8,128)(2,1)} %pad_maximum_fusion.3.refs_5_), channel_id=1, source_target_pairs={{0,4},{4,0},{8,12},{12,8},{16,20},{20,16},{24,28},{28,24},{1,5},{5... | collective-permute-start | bytes 1572872 | tf_op jit(solution)/shard_map/ppermute | solution.py:739
  93.4 13.8 %collective-permute-start.43 = (bf16[128,2048]{1,0:T(8,128)(2,1)}, bf16[128,2048]{1,0:T(8,128)(2,1)S(1)}, u32[]{:S(2)}, u32[]{:S(2)}) collective-permute-start(bf16[128,2048]{1,0:T(8,128)(2,1)} %get-tuple-element.74), channel_id=1, source_target_pairs={{0,1},{1,2},{2,3},{4,5},{5,6},{6,7},{8,9},{9,10},{10,11},{12,13},{... | collective-permute-start | bytes 1572872 | tf_op jit(solution)/shard_map/ppermute | solution.py:724
  104.8 13.6 %collective-permute-start.34 = (bf16[2,2,128,512]{3,2,1,0:T(8,128)(2,1)S(1)}, bf16[2,2,128,512]{3,2,1,0:T(8,128)(2,1)S(1)}, u32[]{:S(2)}, u32[]{:S(2)}) collective-permute-start(bf16[2,2,128,512]{3,2,1,0:T(8,128)(2,1)S(1)} %pad_maximum_fusion.5.refs_13_), channel_id=1, source_target_pairs={{0,8},{4,12},{8,0},{12,4},{16,24},{20,28},{24,16},{28,20},{1,9},{5... | collective-permute-start | bytes 1572872 | tf_op jit(solution)/shard_map/ppermute | solution.py:739
  107.2 12.3 %collective-permute-start.28 = (bf16[2,2,128,512]{3,2,1,0:T(8,128)(2,1)S(1)}, bf16[2,2,128,512]{3,2,1,0:T(8,128)(2,1)S(1)}, u32[]{:S(2)}, u32[]{:S(2)}) collective-permute-start(bf16[2,2,128,512]{3,2,1,0:T(8,128)(2,1)S(1)} %pad_maximum_fusion.4.refs_9_), channel_id=1, source_target_pairs={{0,16},{4,20},{8,24},{12,28},{16,0},{20,4},{24,8},{28,12},{1,17},{... | collective-permute-start | bytes 1572872 | tf_op jit(solution)/shard_map/ppermute | solution.py:739
  108.1 19.9 %collective-permute-start.35 = (bf16[2,2,128,512]{3,2,1,0:T(8,128)(2,1)S(1)}, bf16[2,2,128,512]{3,2,1,0:T(8,128)(2,1)S(1)}, u32[]{:S(2)}, u32[]{:S(2)}) collective-permute-start(bf16[2,2,128,512]{3,2,1,0:T(8,128)(2,1)S(1)} %pad_maximum_fusion.5.refs_13_), channel_id=1, source_target_pairs={{0,4},{4,0},{8,12},{12,8},{16,20},{20,16},{24,28},{28,24},{1,5},{5... | collective-permute-start | bytes 1572872 | tf_op jit(solution)/shard_map/ppermute | solution.py:739
  109.6 18.5 %collective-permute-start.29 = (bf16[2,2,128,512]{3,2,1,0:T(8,128)(2,1)S(1)}, bf16[2,2,128,512]{3,2,1,0:T(8,128)(2,1)S(1)}, u32[]{:S(2)}, u32[]{:S(2)}) collective-permute-start(bf16[2,2,128,512]{3,2,1,0:T(8,128)(2,1)S(1)} %pad_maximum_fusion.4.refs_9_), channel_id=1, source_target_pairs={{0,4},{4,0},{8,12},{12,8},{16,20},{20,16},{24,28},{28,24},{1,5},{5... | collective-permute-start | bytes 1572872 | tf_op jit(solution)/shard_map/ppermute | solution.py:739
  109.7 18.4 %collective-permute-start.44 = (bf16[128,2048]{1,0:T(8,128)(2,1)S(1)}, bf16[128,2048]{1,0:T(8,128)(2,1)S(1)}, u32[]{:S(2)}, u32[]{:S(2)}) collective-permute-start(bf16[128,2048]{1,0:T(8,128)(2,1)S(1)} %multiply_convert_fusion.1), channel_id=1, source_target_pairs={{0,1},{1,2},{2,3},{4,5},{5,6},{6,7},{8,9},{9,10},{10,11},{12,13},{... | collective-permute-start | bytes 1572872 | tf_op jit(solution)/shard_map/ppermute | solution.py:724
  166.5 16.6 %collective-permute-start.45 = (bf16[128,2048]{1,0:T(8,128)(2,1)}, bf16[128,2048]{1,0:T(8,128)(2,1)S(1)}, u32[]{:S(2)}, u32[]{:S(2)}) collective-permute-start(bf16[128,2048]{1,0:T(8,128)(2,1)} %get-tuple-element.85), channel_id=1, source_target_pairs={{1,0},{2,1},{3,2},{5,4},{6,5},{7,6},{9,8},{10,9},{11,10},{13,12},{... | collective-permute-start | bytes 1572872 | tf_op jit(solution)/shard_map/ppermute | solution.py:729
  183.2 15.6 %collective-permute-start.46 = (bf16[128,2048]{1,0:T(8,128)(2,1)S(1)}, bf16[128,2048]{1,0:T(8,128)(2,1)S(1)}, u32[]{:S(2)}, u32[]{:S(2)}) collective-permute-start(bf16[128,2048]{1,0:T(8,128)(2,1)S(1)} %multiply_convert_fusion), channel_id=1, source_target_pairs={{1,0},{2,1},{3,2},{5,4},{6,5},{7,6},{9,8},{10,9},{11,10},{13,12},{... | collective-permute-start | bytes 1572872 | tf_op jit(solution)/shard_map/ppermute | solution.py:729
  229.1 21.1 %all-to-all-start = ((bf16[32,64,128]{2,1,0:T(8,128)(2,1)}), bf16[32,64,128]{2,1,0:T(8,128)(2,1)S(1)}, u32[]{:S(2)}, u32[]{:S(2)}) async-start(bf16[32,64,128]{2,1,0:T(8,128)(2,1)} %bitcast.72), calls=%async_computation | async-start | bytes 1048576 | tf_op jit(solution)/shard_map/all_to_all | solution.py:1171
  (84 other events, 1147.8 us)

commit v5 on v4

--- a/solution.py
+++ b/solution.py
@@ -164,7 +164,7 @@
     return jnp.broadcast_to(row, (lanes, lanes)).T
 
 
-def prep_kernel(sel, tokens, halo, norm_gain, small, dt_t, inner_t, place, params, params_bc, segs, ex, no_out,
+def prep_kernel(sel, tokens, halo, norm_gain, small, picked, dt_t, inner_t, place, params, params_bc, segs, ex, no_out,
                 normed, ranks, ranks_own, tables, bc_out, bct_out, scores, rows_out, cums_t, keep, ups, wides, w_bc,
                 masks, ext, *, rank, state, moved_blocks):
     own, width = tokens.shape
@@ -172,7 +172,6 @@
     tp, _, group = params.shape
     heads = dt_t.shape[0]
     part = heads // tp
-    bc_rows = 2 * lanes
     turn, pick, bound, small_at = 8 + tp, sel[8 + 2 * tp], 9 + 2 * tp, 9 + 2 * tp + 2 * blocks
 
     for c in range(blocks):
@@ -186,7 +185,7 @@
         cols = slice(j * lanes, (j + 1) * lanes)
         no_out[:, cols] = ext[:, at]
         at = sel[small_at + j]
-        wides[:, cols] = small[at, pl.ds(pl.multiple_of(bc_rows + pick * 2 * rank, 2 * rank), 2 * rank), :]
+        wides[:, cols] = picked[at]
         w_bc[j * lanes : (j + 1) * lanes, :state] = small[at, :lanes, :]
         w_bc[j * lanes : (j + 1) * lanes, state:] = small[at, lanes : 2 * lanes, :]
     normed[...] = ext[edge:, :]
@@ -572,8 +571,8 @@
             gs = gs * kept + dot(c_t[:, rows], moved)
             g_sc = dv[rows, cols] + dvs
             v, slope = silu_parts(u[rows, cols])
-            prods[0, rows, cols] = scaled * dvs
-            prods[1, rows, cols] = v * g_sc
+            prods[0, rows, cols] = (scaled * dvs).astype(bf16)
+            prods[1, rows, cols] = (v * g_sc).astype(bf16)
             g_v = dt_wide[rows, cols] * g_sc + params[0, 6:7, cols] * dy
             g_u = g_v * slope
             g_x = conv_back(jnp.concatenate([g_u, following], axis=0), params[0, :, cols], masks, rows, step)
@@ -584,8 +583,8 @@
             if c == 0:
                 at = pl.ds(pl.multiple_of(g * width + n * step, lanes), step)
                 edges[:, at] = g_u[:edge].astype(bf16)
-    behind[...] += dot2(prods[0], red[...])
-    direct[...] += dot2(prods[1], red[...])
+    behind[...] += dot(prods[0], red[...])
+    direct[...] += dot(prods[1], red[...])
     carry[...] += dot2(carries[...], red[...])
 
     @pl.when(g == pl.num_programs(0) - 1)
@@ -685,7 +684,8 @@
                 cur = jnp.concatenate([gbc[rows, :], halo_bc[...].astype(f32)[:8]], axis=0)
             lbc[rows, :] = conv_back(cur, params_bc[...], masks, rows, gbc.shape[1]).astype(bf16)
         g_norm[...] = (
-            dot_nt(lbc[...], w_bc[...]) + dot(ldt[...], dt_t[...]) + dot2(g_rank[...], ad[...])
+            dot_nt(lbc[...], w_bc[...]) + dot(ldt[...], dt_t[...])
+            + dot(parts_of(g_rank[...], 2), jnp.concatenate([ad[...], ad[...]], axis=0))
         )
         for j in range(8):
             at = pl.ds(pl.multiple_of(sel[korder[j]] * lanes, lanes), lanes)
@@ -1002,11 +1002,15 @@
         ((tp_size, blocks, part, chunk), f32), ((8, inner), f32), ((5 * rank, inner), bf16),
         ((2 * rank, width), bf16), ((width, 2 * state), bf16), ((6, own, lanes), f32),
     ]
-    prep_in = [tok, halo_in, norm_gain[None], small, dt_t, inner_t, place, params, params_bc, segs, ex]
+    at_pick = 8 + 2 * tp_size
+    prep_in = [tok, halo_in, norm_gain[None], small, small, dt_t, inner_t, place, params, params_bc, segs, ex]
+    prep_specs = [full(*x.shape) for x in prep_in]
+    prep_specs[3] = full(8, 2 * lanes, lanes)
+    prep_specs[4] = pl.BlockSpec((8, 2 * rank, lanes), lambda g, s: (0, lanes // rank + s[at_pick], 0))
     normed_moved, normed, ranks, ranks_own, tables, bc, bc_t, scores, rows_f32, cums_t, keep, ups, wides, w_bc, masks = call(
         selecting(prep_kernel, rank=rank, state=state, moved_blocks=by_exchange),
         prep_out,
-        [full(*x.shape) for x in prep_in],
+        prep_specs,
         [full(*s) for s, _ in prep_out],
         [pltpu.VMEM((ext, width), bf16)],
         mat // 4, 6 * mega, 1, grant=vmem_bytes * 5 // 4,
@@ -1136,7 +1140,7 @@
            masks_after_spec],
         [cols(own), full(own, 2 * state), full(own, heads), full(*edges_shape), cols(edge)],
         [pltpu.VMEM((own, state), f32), pltpu.VMEM((own, state), f32), pltpu.VMEM((own, lanes), f32),
-         pltpu.VMEM((own, lanes), f32), pltpu.VMEM((8, lanes), f32), pltpu.VMEM((2, own, group), f32),
+         pltpu.VMEM((own, lanes), f32), pltpu.VMEM((8, lanes), f32), pltpu.VMEM((2, own, group), bf16),
          pltpu.VMEM((8, group), f32)],
         mat, 24 * mega,
     )(sel, *grads_in, states, g_heads, scaled, d_within, u, params, bc, bc_t, tables, keep, keep, ex, red, d_scores,

time: 253 us -> 250 us (0.988)
  Pallas kernels: 123 us -> 120 us
    pallas_call x1, Pallas kernels: 18 us -> 15.4 us  [shards(): call(plain(back_state_kernel, hops=hops), [(big, bf16), ((own, 2 * state)...]
where the time goes in v5:
time: 250 us; the launch traced here: 249 us
  Pallas kernels  120 us (48%)
  starting transfers between devices  64.7 us (26%)
  waiting for transfers between devices  33.2 us (13%)
  other arithmetic  14.7 us (6%)
  local copies, waits for them, and re-layouts  13.9 us (6%)
    pallas_call x1, Pallas kernels, shards(): call(selecting(middle_kernel, weights=n_w, hops=hops, inner=inner), [((bl...  36.8 us
    ppermute x25, starting transfers between devices, swap(): return lax.ppermute(x, 'dp', [(i, i ^ 1 << bit) for i in range(n)])  24.4 us
    ppermute x15, starting transfers between devices, around_tensor(): lax.ppermute(x, 'tensor', [(i, (i + s) % n) for i in range(n)])  19.8 us
    pallas_call x1, Pallas kernels, shards(): call(plain(back_state_kernel, hops=hops), [(big, bf16), ((own, 2 * state)...  15.4 us
    ppermute x3, waiting for transfers between devices, down(): return lax.ppermute(x, 'tensor', [(i + 1, i) for i in range(n - 1)])  12.6 us
    pallas_call x1, Pallas kernels, shards(): call(plain(proj_kernel, weights=n_w), [(big, f32), (big, bf16), ((state,...  12.6 us
    pallas_call x1, Pallas kernels, shards(): call(plain(back_within_kernel), [(big, f32), ((blocks, chunk, chunk), f32...  12 us
    pallas_call x1, Pallas kernels, shards(): call(selecting(tokens_kernel, weights=n_w), [((own, width), f32)], [cols(...  12 us
  transfers between devices with their start and end apart: 49, of which 12 were waited for; matrix products, arithmetic and copies ran while one was open for 9% of the time, Pallas kernels for 24%

profile of v5, /device:TPU:1, one launch (start us, length us, event | category | flops | bytes accessed | tf_op | source)
XLA Modules:
  0.0 248.7 jit_solution(772742448587529046)
XLA Ops:
  2.2 3.2 %collective-permute-start.11 = (bf16[128,512]{1,0:T(8,128)(2,1)S(1)}, bf16[128,512]{1,0:T(8,128)(2,1)S(1)}, u32[]{:S(2)}, u32[]{:S(2)}) collective-permute-start(bf16[128,512]{1,0:T(8,128)(2,1)S(1)} %bitcast.117), channel_id=1, source_target_pairs={{0,2},{1,3},{2,0},{3,1},{4,6},{5,7},{6,4},{7,5},{8,10},{9,11},{10,... | collective-permute-start | bytes 393224 | tf_op jit(solution)/shard_map/ppermute | solution.py:734
  6.7 2.0 collective-permute-start.12
  9.4 1.9 pack_kernel.1
  23.0 3.5 %collective-permute-done.2 = bf16[2,800,128]{2,1,0:T(8,128)(2,1)S(1)} collective-permute-done((bf16[2,800,128]{2,1,0:T(8,128)(2,1)S(1)}, bf16[2,800,128]{2,1,0:T(8,128)(2,1)S(1)}, u32[]{:S(2)}, u32[]{:S(2)}) %collective-permute-start.2) | collective-permute-done | bytes 409632 | tf_op jit(solution)/shard_map/ppermute | solution.py:752
  28.9 3.3 %collective-permute-start.3 = (bf16[4,800,128]{2,1,0:T(8,128)(2,1)}, bf16[4,800,128]{2,1,0:T(8,128)(2,1)}, u32[]{:S(2)}, u32[]{:S(2)}) collective-permute-start(bf16[4,800,128]{2,1,0:T(8,128)(2,1)} %pad_maximum_fusion.1), channel_id=1, source_target_pairs={{0,4},{4,0},{8,12},{12,8},{16,20},{20,16},{24,28},{28,24},{1,5},{5... | collective-permute-start | bytes 2457608 | tf_op jit(solution)/shard_map/ppermute | solution.py:739
  36.4 2.3 collective-permute-start.8
  41.2 2.0 collective-permute-done.7
  49.4 3.1 %collective-permute-start.6 = (bf16[320,128]{1,0:T(8,128)(2,1)S(1)}, bf16[320,128]{1,0:T(8,128)(2,1)S(1)}, u32[]{:S(2)}, u32[]{:S(2)}) collective-permute-start(bf16[320,128]{1,0:T(8,128)(2,1)S(1)} %get-tuple-element.121), channel_id=1, source_target_pairs={{0,3},{1,0},{2,1},{3,2},{4,7},{5,4},{6,5},{7,6},{8,11},{9,8},{10,9... | collective-permute-start | bytes 245768 | tf_op jit(solution)/shard_map/ppermute | solution.py:734
  52.6 1.9 pad_maximum_fusion.3.refs_5_
  55.7 2.5 %collective-permute-done.37.refs_2_ = bf16[2,2,128,512]{3,2,1,0:T(8,128)(2,1)} collective-permute-done((bf16[2,2,128,512]{3,2,1,0:T(8,128)(2,1)S(1)}, bf16[2,2,128,512]{3,2,1,0:T(8,128)(2,1)}, u32[]{:S(2)}, u32[]{:S(2)}) %collective-permute-start.37) | collective-permute-done | bytes 524320 | tf_op jit(solution)/shard_map/ppermute | solution.py:739
  58.3 2.2 collective-permute-start.41
  63.1 8.5 %prep_kernel.1 = (bf16[528,1024]{1,0:T(8,128)(2,1)}, bf16[512,1024]{1,0:T(8,128)(2,1)}, bf16[528,32]{1,0:T(8,128)(2,1)}, bf16[512,32]{1,0:T(8,128)(2,1)}, bf16[5...) custom-call(s32[33]{0:T(128)} %concatenate.42.sel_ref, ...), custom_call_target="tpu_custom_call" | custom-call | flops 536870912 | bytes 6291456 | tf_op jit(solution)/shard_map/prep_kernel/pallas_call | solution.py:1010
  74.2 2.7 %collective-permute-start.32 = (bf16[128,512]{1,0:T(8,128)(2,1)S(1)}, bf16[128,512]{1,0:T(8,128)(2,1)S(1)}, u32[]{:S(2)}, u32[]{:S(2)}) collective-permute-start(bf16[128,512]{1,0:T(8,128)(2,1)S(1)} %bitcast.127), channel_id=1, source_target_pairs={{0,3},{1,0},{2,1},{3,2},{4,7},{5,4},{6,5},{7,6},{8,11},{9,8},{10,9... | collective-permute-start | bytes 393224 | tf_op jit(solution)/shard_map/ppermute | solution.py:734
  78.2 12.6 %proj_kernel.1 = (f32[512,2048]{1,0:T(8,128)}, bf16[512,2048]{1,0:T(8,128)(2,1)}, bf16[128,2048]{1,0:T(8,128)(2,1)}) custom-call(s32[33]{0:T(128)} %concatenate.42.sel_ref, bf16[528,1024]{1,0:T(8,128)(2,1)} %get-tuple-element.62.refs_0_, bf16[2,2,128,512]{3,2,1,0:T(8,128)(2,1)} %copy-done.36, bf16[2,2,128,512]{3,2,1,0:T(8,128)(2,1)} %collective-permute-done.37.refs_2_, ...), custom_call_target="tpu_custom_call" | custom-call | flops 2147483648 | bytes 12582912 | tf_op jit(solution)/shard_map/proj_kernel/pallas_call | solution.py:1036
  90.8 1.9 collective-permute-start.24
  92.7 2.5 collective-permute-start.43
  98.9 3.8 %collective-permute-done.33 = bf16[2,128,512]{2,1,0:T(8,128)(2,1)S(1)} collective-permute-done((bf16[2,128,512]{2,1,0:T(8,128)(2,1)S(1)}, bf16[2,128,512]{2,1,0:T(8,128)(2,1)S(1)}, u32[]{:S(2)}, u32[]{:S(2)}) %collective-permute-start.33) | collective-permute-done | bytes 262176 | tf_op jit(solution)/shard_map/ppermute | solution.py:739
  104.5 2.0 collective-permute-done.43.refs_17_
  109.0 4.4 %collective-permute-start.44 = (bf16[128,2048]{1,0:T(8,128)(2,1)S(1)}, bf16[128,2048]{1,0:T(8,128)(2,1)S(1)}, u32[]{:S(2)}, u32[]{:S(2)}) collective-permute-start(bf16[128,2048]{1,0:T(8,128)(2,1)S(1)} %multiply_convert_fusion.1), channel_id=1, source_target_pairs={{0,1},{1,2},{2,3},{4,5},{5,6},{6,7},{8,9},{9,10},{10,11},{12,13},{... | collective-permute-start | bytes 1572872 | tf_op jit(solution)/shard_map/ppermute | solution.py:724
  113.4 4.4 %collective-permute-done.34.refs_14_ = bf16[2,2,128,512]{3,2,1,0:T(8,128)(2,1)S(1)} collective-permute-done((bf16[2,2,128,512]{3,2,1,0:T(8,128)(2,1)S(1)}, bf16[2,2,128,512]{3,2,1,0:T(8,128)(2,1)S(1)}, u32[]{:S(2)}, u32[]{:S(2)}) %collective-permute-start.34) | collective-permute-done | bytes 524320 | tf_op jit(solution)/shard_map/ppermute | solution.py:739
  118.8 2.0 collective-permute-start.30
  122.1 5.1 %within_kernel.1.refs_22_ = f32[512,2048]{1,0:T(8,128)} custom-call(s32[33]{0:T(128)S(1)} %copy-done.26, bf16[512,2048]{1,0:T(8,128)(2,1)S(1)} %copy-done.1, bf16[512,768]{1,0:T(8,128)(2,1)S(1)} %copy-done.2, f32[4,4,8,128]{3,2,1,0:T(8,128)S(1)} %copy-done.25, f32[2,4,128,128]{3,2,1,0:T(8,128)S(1)} %copy-done.5, bf16[128,4096]{1,0:T(8,128)(2,1)S(1)} %copy-done.10), custom_call_target="tpu_custom_call" | custom-call | flops 2147483648 | bytes 6291456 | tf_op jit(solution)/shard_map/within_kernel/pallas_call | solution.py:1057
  129.0 36.8 %middle_kernel.1 = (bf16[4,128,2048]{2,1,0:T(8,128)(2,1)}, f32[512,1024]{1,0:T(8,128)}, bf16[8,4,32,128]{3,2,1,0:T(8,128)(2,1)}, f32[512,2048]{1,0:T(8,128)}, bf...) custom-call(s32[33]{0:T(128)} %concatenate.42.sel_ref, ...), custom_call_target="tpu_custom_call" | custom-call | flops 8589934592 | bytes 41943040 | tf_op jit(solution)/shard_map/middle_kernel/pallas_call | solution.py:1089
  167.2 12.0 %back_within_kernel.1 = (f32[512,2048]{1,0:T(8,128)}, f32[4,128,128]{2,1,0:T(8,128)}, f32[512,128]{1,0:T(8,128)}) custom-call(s32[33]{0:T(128)} %concatenate.42.sel_ref, f32[512,2048]{1,0:T(8,128)} %get-tuple-element.87.refs_0_.refs_3_, f32[512,128]{1,0:T(8,128)} %get-tuple-element.88.refs_1_, ...), custom_call_target="tpu_custom_call" | custom-call | flops 4294967296 | bytes 14680064 | tf_op jit(solution)/shard_map/back_within_kernel/pallas_call | solution.py:1111
  179.2 3.2 %collective-permute-done.45.refs_0_ = bf16[128,2048]{1,0:T(8,128)(2,1)S(1)} collective-permute-done((bf16[128,2048]{1,0:T(8,128)(2,1)}, bf16[128,2048]{1,0:T(8,128)(2,1)S(1)}, u32[]{:S(2)}, u32[]{:S(2)}) %collective-permute-start.45) | collective-permute-done | bytes 524320 | tf_op jit(solution)/shard_map/ppermute | solution.py:729
  184.2 8.2 %in_z_kernel.1 = (f32[512,1024]{1,0:T(8,128)}, f32[512,16]{1,0:T(8,128)S(1)}, f32[4,16,512]{2,1,0:T(8,128)S(1)}) custom-call(s32[33]{0:T(128)S(1)} %copy-done.27, bf16[512,2048]{1,0:T(8,128)(2,1)} %get-tuple-element.91.refs_0_, bf16[2,2,128,512]{3,2,1,0:T(8,128)(2,1)S(1)} %copy-done.16, bf16[2,2,128,512]{3,2,1,0:T(8,128)(2,1)} %collective-permute-done.17.refs_2_, ...), custom_call_target="tpu_custom_call" | custom-call | flops 2147483648 | bytes 8388608 | tf_op jit(solution)/shard_map/in_z_kernel/pallas_call | solution.py:1122
  192.5 5.6 %collective-permute-done.46.refs_1_ = bf16[128,2048]{1,0:T(8,128)(2,1)S(1)} collective-permute-done((bf16[128,2048]{1,0:T(8,128)(2,1)S(1)}, bf16[128,2048]{1,0:T(8,128)(2,1)S(1)}, u32[]{:S(2)}, u32[]{:S(2)}) %collective-permute-start.46) | collective-permute-done | bytes 524320 | tf_op jit(solution)/shard_map/ppermute | solution.py:729
  198.2 15.4 %back_state_kernel.1 = (bf16[512,2048]{1,0:T(8,128)(2,1)}, f32[512,256]{1,0:T(8,128)S(1)}, bf16[512,32]{1,0:T(8,128)(2,1)S(1)}, bf16[16,2304]{1,0:T(8,128)(2,1)S(1)}, f32[16,2048]{1,0:T(8,128)S(1)}) custom-call(s32[33]{0:T(128)S(1)} %copy-done.27, bf16[128,2048]{1,0:T(8,128)(2,1)S(1)} %collective-permute-done.45.refs_0_, ...), custom_call_target="tpu_custom_call" | custom-call | flops 2147483648 | bytes 25165824 | tf_op jit(solution)/shard_map/back_state_kernel/pallas_call | solution.py:1133
  215.0 3.8 %collective-permute-done.47.refs_2_.refs_12_ = bf16[16,2304]{1,0:T(8,128)(2,1)S(1)} collective-permute-done((bf16[16,2304]{1,0:T(8,128)(2,1)S(1)}, bf16[16,2304]{1,0:T(8,128)(2,1)S(1)}, u32[]{:S(2)}, u32[]{:S(2)}) %collective-permute-start.47) | collective-permute-done | bytes 73760 | tf_op jit(solution)/shard_map/ppermute | solution.py:729
  218.8 5.5 %in_x_kernel.1 = (bf16[512,2048]{1,0:T(8,128)(2,1)}, f32[512,16]{1,0:T(8,128)S(1)}, bf16[8,4,32,128]{3,2,1,0:T(8,128)(2,1)S(1)}) custom-call(s32[33]{0:T(128)S(1)} %copy-done.27, bf16[512,2048]{1,0:T(8,128)(2,1)} %get-tuple-element.99.refs_0_, f32[16,2048]{1,0:T(8,128)S(1)} %get-tuple-element.100.refs_1_, ...), custom_call_target="tpu_custom_call", output_to_operand_aliasing={{0}: (1, {})} | custom-call | flops 268435456 | bytes 8388608 | tf_op jit(solution)/shard_map/in_x_kernel/pallas_call | solution.py:1150
  225.8 5.8 %all-to-all-start = ((bf16[32,64,128]{2,1,0:T(8,128)(2,1)}), bf16[32,64,128]{2,1,0:T(8,128)(2,1)S(1)}, u32[]{:S(2)}, u32[]{:S(2)}) async-start(bf16[32,64,128]{2,1,0:T(8,128)(2,1)} %bitcast.72), calls=%async_computation | async-start | bytes 1048576 | tf_op jit(solution)/shard_map/all_to_all | solution.py:1175
  233.2 12.0 %tokens_kernel.1 = f32[512,1024]{1,0:T(8,128)} custom-call(s32[33]{0:T(128)} %concatenate.42.sel_ref, bf16[512,2048]{1,0:T(8,128)(2,1)} %get-tuple-element.105.refs_0_, bf16[2,2,128,512]{3,2,1,0:T(8,128)(2,1)} %copy-done.36, bf16[2,2,128,512]{3,2,1,0:T(8,128)(2,1)} %collective-permute-done.37.refs_2_, ...), custom_call_target="tpu_custom_call" | custom-call | flops 2147483648 | bytes 14680064 | tf_op jit(solution)/shard_map/tokens_kernel/pallas_call | solution.py:1160
  (286 shorter events, 60.2 us)
Async XLA Ops:
  2.2 16.9 %collective-permute-start.11 = (bf16[128,512]{1,0:T(8,128)(2,1)S(1)}, bf16[128,512]{1,0:T(8,128)(2,1)S(1)}, u32[]{:S(2)}, u32[]{:S(2)}) collective-permute-start(bf16[128,512]{1,0:T(8,128)(2,1)S(1)} %bitcast.117), channel_id=1, source_target_pairs={{0,2},{1,3},{2,0},{3,1},{4,6},{5,7},{6,4},{7,5},{8,10},{9,11},{10,... | collective-permute-start | bytes 393224 | tf_op jit(solution)/shard_map/ppermute | solution.py:734
  5.4 13.7 %collective-permute-start.10 = (bf16[128,512]{1,0:T(8,128)(2,1)S(1)}, bf16[128,512]{1,0:T(8,128)(2,1)S(1)}, u32[]{:S(2)}, u32[]{:S(2)}) collective-permute-start(bf16[128,512]{1,0:T(8,128)(2,1)S(1)} %bitcast.118), channel_id=1, source_target_pairs={{0,1},{1,2},{2,3},{3,0},{4,5},{5,6},{6,7},{7,4},{8,9},{9,10},{10,1... | collective-permute-start | bytes 393224 | tf_op jit(solution)/shard_map/ppermute | solution.py:734
  6.7 12.4 %collective-permute-start.12 = (bf16[128,512]{1,0:T(8,128)(2,1)S(1)}, bf16[128,512]{1,0:T(8,128)(2,1)S(1)}, u32[]{:S(2)}, u32[]{:S(2)}) collective-permute-start(bf16[128,512]{1,0:T(8,128)(2,1)S(1)} %bitcast.119), channel_id=1, source_target_pairs={{0,3},{1,0},{2,1},{3,2},{4,7},{5,4},{6,5},{7,6},{8,11},{9,8},{10,9... | collective-permute-start | bytes 393224 | tf_op jit(solution)/shard_map/ppermute | solution.py:734
  19.1 15.0 %collective-permute-start.21 = (bf16[128,512]{1,0:T(8,128)(2,1)S(1)}, bf16[128,512]{1,0:T(8,128)(2,1)S(1)}, u32[]{:S(2)}, u32[]{:S(2)}) collective-permute-start(bf16[128,512]{1,0:T(8,128)(2,1)S(1)} %bitcast.121), channel_id=1, source_target_pairs={{0,3},{1,0},{2,1},{3,2},{4,7},{5,4},{6,5},{7,6},{8,11},{9,8},{10,9... | collective-permute-start | bytes 393224 | tf_op jit(solution)/shard_map/ppermute | solution.py:734
  19.3 14.9 %collective-permute-start.20 = (bf16[128,512]{1,0:T(8,128)(2,1)S(1)}, bf16[128,512]{1,0:T(8,128)(2,1)S(1)}, u32[]{:S(2)}, u32[]{:S(2)}) collective-permute-start(bf16[128,512]{1,0:T(8,128)(2,1)S(1)} %bitcast.122), channel_id=1, source_target_pairs={{0,2},{1,3},{2,0},{3,1},{4,6},{5,7},{6,4},{7,5},{8,10},{9,11},{10,... | collective-permute-start | bytes 393224 | tf_op jit(solution)/shard_map/ppermute | solution.py:734
  21.7 13.2 %collective-permute-start.14 = (bf16[2,128,512]{2,1,0:T(8,128)(2,1)S(1)}, bf16[2,128,512]{2,1,0:T(8,128)(2,1)S(1)}, u32[]{:S(2)}, u32[]{:S(2)}) collective-permute-start(bf16[2,128,512]{2,1,0:T(8,128)(2,1)S(1)} %pad_maximum_fusion.14), channel_id=1, source_target_pairs={{0,8},{4,12},{8,0},{12,4},{16,24},{20,28},{24,16},{28,20},{1,9},{5... | collective-permute-start | bytes 786440 | tf_op jit(solution)/shard_map/ppermute | solution.py:739
  28.9 15.5 %collective-permute-start.3 = (bf16[4,800,128]{2,1,0:T(8,128)(2,1)}, bf16[4,800,128]{2,1,0:T(8,128)(2,1)}, u32[]{:S(2)}, u32[]{:S(2)}) collective-permute-start(bf16[4,800,128]{2,1,0:T(8,128)(2,1)} %pad_maximum_fusion.1), channel_id=1, source_target_pairs={{0,4},{4,0},{8,12},{12,8},{16,20},{20,16},{24,28},{28,24},{1,5},{5... | collective-permute-start | bytes 2457608 | tf_op jit(solution)/shard_map/ppermute | solution.py:739
  40.9 13.5 %collective-permute-start.40 = (bf16[2,2,128,512]{3,2,1,0:T(8,128)(2,1)S(1)}, bf16[2,2,128,512]{3,2,1,0:T(8,128)(2,1)}, u32[]{:S(2)}, u32[]{:S(2)}) collective-permute-start(bf16[2,2,128,512]{3,2,1,0:T(8,128)(2,1)S(1)} %pad_maximum_fusion.7.refs_5_), channel_id=1, source_target_pairs={{0,8},{4,12},{8,0},{12,4},{16,24},{20,28},{24,16},{28,20},{1,9},{5... | collective-permute-start | bytes 1572872 | tf_op jit(solution)/shard_map/ppermute | solution.py:739
  43.1 15.1 %collective-permute-start.37 = (bf16[2,2,128,512]{3,2,1,0:T(8,128)(2,1)S(1)}, bf16[2,2,128,512]{3,2,1,0:T(8,128)(2,1)}, u32[]{:S(2)}, u32[]{:S(2)}) collective-permute-start(bf16[2,2,128,512]{3,2,1,0:T(8,128)(2,1)S(1)} %pad_maximum_fusion.6.refs_1_), channel_id=1, source_target_pairs={{0,16},{4,20},{8,24},{12,28},{16,0},{20,4},{24,8},{28,12},{1,17},{... | collective-permute-start | bytes 1572872 | tf_op jit(solution)/shard_map/ppermute | solution.py:739
  48.4 12.1 %collective-permute-start.5 = (bf16[320,128]{1,0:T(8,128)(2,1)S(1)}, bf16[320,128]{1,0:T(8,128)(2,1)S(1)}, u32[]{:S(2)}, u32[]{:S(2)}) collective-permute-start(bf16[320,128]{1,0:T(8,128)(2,1)S(1)} %get-tuple-element.121), channel_id=1, source_target_pairs={{0,2},{1,3},{2,0},{3,1},{4,6},{5,7},{6,4},{7,5},{8,10},{9,11},{10,... | collective-permute-start | bytes 245768 | tf_op jit(solution)/shard_map/ppermute | solution.py:734
  49.3 11.3 %collective-permute-start.4 = (bf16[320,128]{1,0:T(8,128)(2,1)S(1)}, bf16[320,128]{1,0:T(8,128)(2,1)S(1)}, u32[]{:S(2)}, u32[]{:S(2)}) collective-permute-start(bf16[320,128]{1,0:T(8,128)(2,1)S(1)} %get-tuple-element.121), channel_id=1, source_target_pairs={{0,1},{1,2},{2,3},{3,0},{4,5},{5,6},{6,7},{7,4},{8,9},{9,10},{10,1... | collective-permute-start | bytes 245768 | tf_op jit(solution)/shard_map/ppermute | solution.py:734
  49.4 11.5 %collective-permute-start.6 = (bf16[320,128]{1,0:T(8,128)(2,1)S(1)}, bf16[320,128]{1,0:T(8,128)(2,1)S(1)}, u32[]{:S(2)}, u32[]{:S(2)}) collective-permute-start(bf16[320,128]{1,0:T(8,128)(2,1)S(1)} %get-tuple-element.121), channel_id=1, source_target_pairs={{0,3},{1,0},{2,1},{3,2},{4,7},{5,4},{6,5},{7,6},{8,11},{9,8},{10,9... | collective-permute-start | bytes 245768 | tf_op jit(solution)/shard_map/ppermute | solution.py:734
  58.3 15.3 %collective-permute-start.41 = (bf16[2,2,128,512]{3,2,1,0:T(8,128)(2,1)S(1)}, bf16[2,2,128,512]{3,2,1,0:T(8,128)(2,1)}, u32[]{:S(2)}, u32[]{:S(2)}) collective-permute-start(bf16[2,2,128,512]{3,2,1,0:T(8,128)(2,1)S(1)} %pad_maximum_fusion.7.refs_5_), channel_id=1, source_target_pairs={{0,4},{4,0},{8,12},{12,8},{16,20},{20,16},{24,28},{28,24},{1,5},{5... | collective-permute-start | bytes 1572872 | tf_op jit(solution)/shard_map/ppermute | solution.py:739
  60.5 13.8 %collective-permute-start.38 = (bf16[2,2,128,512]{3,2,1,0:T(8,128)(2,1)S(1)}, bf16[2,2,128,512]{3,2,1,0:T(8,128)(2,1)}, u32[]{:S(2)}, u32[]{:S(2)}) collective-permute-start(bf16[2,2,128,512]{3,2,1,0:T(8,128)(2,1)S(1)} %pad_maximum_fusion.6.refs_1_), channel_id=1, source_target_pairs={{0,4},{4,0},{8,12},{12,8},{16,20},{20,16},{24,28},{28,24},{1,5},{5... | collective-permute-start | bytes 1572872 | tf_op jit(solution)/shard_map/ppermute | solution.py:739
  60.5 16.4 %collective-permute-start.42 = (bf16[2,2,128,512]{3,2,1,0:T(8,128)(2,1)}, bf16[2,2,128,512]{3,2,1,0:T(8,128)(2,1)}, u32[]{:S(2)}, u32[]{:S(2)}) collective-permute-start(bf16[2,2,128,512]{3,2,1,0:T(8,128)(2,1)} %collective-permute-done.40.refs_6_), channel_id=1, source_target_pairs={{0,4},{4,0},{8,12},{12,8},{16,20},{20,16},{24,28},{28,24},{1,5},{5... | collective-permute-start | bytes 1572872 | tf_op jit(solution)/shard_map/ppermute | solution.py:739
  61.0 15.9 %collective-permute-start.39 = (bf16[2,2,128,512]{3,2,1,0:T(8,128)(2,1)}, bf16[2,2,128,512]{3,2,1,0:T(8,128)(2,1)}, u32[]{:S(2)}, u32[]{:S(2)}) collective-permute-start(bf16[2,2,128,512]{3,2,1,0:T(8,128)(2,1)} %collective-permute-done.37.refs_2_), channel_id=1, source_target_pairs={{0,4},{4,0},{8,12},{12,8},{16,20},{20,16},{24,28},{28,24},{1,5},{5... | collective-permute-start | bytes 1572872 | tf_op jit(solution)/shard_map/ppermute | solution.py:739
  72.5 25.4 %collective-permute-start.23 = (bf16[2,2,128,512]{3,2,1,0:T(8,128)(2,1)}, bf16[2,2,128,512]{3,2,1,0:T(8,128)(2,1)}, u32[]{:S(2)}, u32[]{:S(2)}) collective-permute-start(bf16[2,2,128,512]{3,2,1,0:T(8,128)(2,1)} %pad_maximum_fusion.3.refs_5_), channel_id=1, source_target_pairs={{0,8},{4,12},{8,0},{12,4},{16,24},{20,28},{24,16},{28,20},{1,9},{5... | collective-permute-start | bytes 1572872 | tf_op jit(solution)/shard_map/ppermute | solution.py:739
  73.6 25.2 %collective-permute-start.17 = (bf16[2,2,128,512]{3,2,1,0:T(8,128)(2,1)S(1)}, bf16[2,2,128,512]{3,2,1,0:T(8,128)(2,1)}, u32[]{:S(2)}, u32[]{:S(2)}) collective-permute-start(bf16[2,2,128,512]{3,2,1,0:T(8,128)(2,1)S(1)} %pad_maximum_fusion.2.refs_1_), channel_id=1, source_target_pairs={{0,16},{4,20},{8,24},{12,28},{16,0},{20,4},{24,8},{28,12},{1,17},{... | collective-permute-start | bytes 1572872 | tf_op jit(solution)/shard_map/ppermute | solution.py:739
  74.2 16.6 %collective-permute-start.32 = (bf16[128,512]{1,0:T(8,128)(2,1)S(1)}, bf16[128,512]{1,0:T(8,128)(2,1)S(1)}, u32[]{:S(2)}, u32[]{:S(2)}) collective-permute-start(bf16[128,512]{1,0:T(8,128)(2,1)S(1)} %bitcast.127), channel_id=1, source_target_pairs={{0,3},{1,0},{2,1},{3,2},{4,7},{5,4},{6,5},{7,6},{8,11},{9,8},{10,9... | collective-permute-start | bytes 393224 | tf_op jit(solution)/shard_map/ppermute | solution.py:734
  76.9 15.8 %collective-permute-start.31 = (bf16[128,512]{1,0:T(8,128)(2,1)S(1)}, bf16[128,512]{1,0:T(8,128)(2,1)S(1)}, u32[]{:S(2)}, u32[]{:S(2)}) collective-permute-start(bf16[128,512]{1,0:T(8,128)(2,1)S(1)} %bitcast.128), channel_id=1, source_target_pairs={{0,2},{1,3},{2,0},{3,1},{4,6},{5,7},{6,4},{7,5},{8,10},{9,11},{10,... | collective-permute-start | bytes 393224 | tf_op jit(solution)/shard_map/ppermute | solution.py:734
  76.9 18.4 %collective-permute-start.27 = (bf16[2,128,512]{2,1,0:T(8,128)(2,1)}, bf16[2,128,512]{2,1,0:T(8,128)(2,1)S(1)}, u32[]{:S(2)}, u32[]{:S(2)}) collective-permute-start(bf16[2,128,512]{2,1,0:T(8,128)(2,1)} %pad_maximum_fusion.17), channel_id=1, source_target_pairs={{0,8},{4,12},{8,0},{12,4},{16,24},{20,28},{24,16},{28,20},{1,9},{5... | collective-permute-start | bytes 786440 | tf_op jit(solution)/shard_map/ppermute | solution.py:739
  90.8 13.3 %collective-permute-start.24 = (bf16[2,2,128,512]{3,2,1,0:T(8,128)(2,1)}, bf16[2,2,128,512]{3,2,1,0:T(8,128)(2,1)}, u32[]{:S(2)}, u32[]{:S(2)}) collective-permute-start(bf16[2,2,128,512]{3,2,1,0:T(8,128)(2,1)} %pad_maximum_fusion.3.refs_5_), channel_id=1, source_target_pairs={{0,4},{4,0},{8,12},{12,8},{16,20},{20,16},{24,28},{28,24},{1,5},{5... | collective-permute-start | bytes 1572872 | tf_op jit(solution)/shard_map/ppermute | solution.py:739
  92.7 13.8 %collective-permute-start.43 = (bf16[128,2048]{1,0:T(8,128)(2,1)}, bf16[128,2048]{1,0:T(8,128)(2,1)S(1)}, u32[]{:S(2)}, u32[]{:S(2)}) collective-permute-start(bf16[128,2048]{1,0:T(8,128)(2,1)} %get-tuple-element.74), channel_id=1, source_target_pairs={{0,1},{1,2},{2,3},{4,5},{5,6},{6,7},{8,9},{9,10},{10,11},{12,13},{... | collective-permute-start | bytes 1572872 | tf_op jit(solution)/shard_map/ppermute | solution.py:724
  98.8 10.1 %collective-permute-start.25 = (bf16[2,2,128,512]{3,2,1,0:T(8,128)(2,1)}, bf16[2,2,128,512]{3,2,1,0:T(8,128)(2,1)S(1)}, u32[]{:S(2)}, u32[]{:S(2)}) collective-permute-start(bf16[2,2,128,512]{3,2,1,0:T(8,128)(2,1)} %collective-permute-done.23.refs_6_), channel_id=1, source_target_pairs={{0,4},{4,0},{8,12},{12,8},{16,20},{20,16},{24,28},{28,24},{1,5},{5... | collective-permute-start | bytes 1572872 | tf_op jit(solution)/shard_map/ppermute | solution.py:739
  104.1 13.6 %collective-permute-start.34 = (bf16[2,2,128,512]{3,2,1,0:T(8,128)(2,1)S(1)}, bf16[2,2,128,512]{3,2,1,0:T(8,128)(2,1)S(1)}, u32[]{:S(2)}, u32[]{:S(2)}) collective-permute-start(bf16[2,2,128,512]{3,2,1,0:T(8,128)(2,1)S(1)} %pad_maximum_fusion.5.refs_13_), channel_id=1, source_target_pairs={{0,8},{4,12},{8,0},{12,4},{16,24},{20,28},{24,16},{28,20},{1,9},{5... | collective-permute-start | bytes 1572872 | tf_op jit(solution)/shard_map/ppermute | solution.py:739
  106.5 12.3 %collective-permute-start.28 = (bf16[2,2,128,512]{3,2,1,0:T(8,128)(2,1)S(1)}, bf16[2,2,128,512]{3,2,1,0:T(8,128)(2,1)S(1)}, u32[]{:S(2)}, u32[]{:S(2)}) collective-permute-start(bf16[2,2,128,512]{3,2,1,0:T(8,128)(2,1)S(1)} %pad_maximum_fusion.4.refs_9_), channel_id=1, source_target_pairs={{0,16},{4,20},{8,24},{12,28},{16,0},{20,4},{24,8},{28,12},{1,17},{... | collective-permute-start | bytes 1572872 | tf_op jit(solution)/shard_map/ppermute | solution.py:739
  107.4 19.9 %collective-permute-start.35 = (bf16[2,2,128,512]{3,2,1,0:T(8,128)(2,1)S(1)}, bf16[2,2,128,512]{3,2,1,0:T(8,128)(2,1)S(1)}, u32[]{:S(2)}, u32[]{:S(2)}) collective-permute-start(bf16[2,2,128,512]{3,2,1,0:T(8,128)(2,1)S(1)} %pad_maximum_fusion.5.refs_13_), channel_id=1, source_target_pairs={{0,4},{4,0},{8,12},{12,8},{16,20},{20,16},{24,28},{28,24},{1,5},{5... | collective-permute-start | bytes 1572872 | tf_op jit(solution)/shard_map/ppermute | solution.py:739
  108.9 18.5 %collective-permute-start.29 = (bf16[2,2,128,512]{3,2,1,0:T(8,128)(2,1)S(1)}, bf16[2,2,128,512]{3,2,1,0:T(8,128)(2,1)S(1)}, u32[]{:S(2)}, u32[]{:S(2)}) collective-permute-start(bf16[2,2,128,512]{3,2,1,0:T(8,128)(2,1)S(1)} %pad_maximum_fusion.4.refs_9_), channel_id=1, source_target_pairs={{0,4},{4,0},{8,12},{12,8},{16,20},{20,16},{24,28},{28,24},{1,5},{5... | collective-permute-start | bytes 1572872 | tf_op jit(solution)/shard_map/ppermute | solution.py:739
  109.0 18.4 %collective-permute-start.44 = (bf16[128,2048]{1,0:T(8,128)(2,1)S(1)}, bf16[128,2048]{1,0:T(8,128)(2,1)S(1)}, u32[]{:S(2)}, u32[]{:S(2)}) collective-permute-start(bf16[128,2048]{1,0:T(8,128)(2,1)S(1)} %multiply_convert_fusion.1), channel_id=1, source_target_pairs={{0,1},{1,2},{2,3},{4,5},{5,6},{6,7},{8,9},{9,10},{10,11},{12,13},{... | collective-permute-start | bytes 1572872 | tf_op jit(solution)/shard_map/ppermute | solution.py:724
  165.8 16.6 %collective-permute-start.45 = (bf16[128,2048]{1,0:T(8,128)(2,1)}, bf16[128,2048]{1,0:T(8,128)(2,1)S(1)}, u32[]{:S(2)}, u32[]{:S(2)}) collective-permute-start(bf16[128,2048]{1,0:T(8,128)(2,1)} %get-tuple-element.85), channel_id=1, source_target_pairs={{1,0},{2,1},{3,2},{5,4},{6,5},{7,6},{9,8},{10,9},{11,10},{13,12},{... | collective-permute-start | bytes 1572872 | tf_op jit(solution)/shard_map/ppermute | solution.py:729
  182.5 15.6 %collective-permute-start.46 = (bf16[128,2048]{1,0:T(8,128)(2,1)S(1)}, bf16[128,2048]{1,0:T(8,128)(2,1)S(1)}, u32[]{:S(2)}, u32[]{:S(2)}) collective-permute-start(bf16[128,2048]{1,0:T(8,128)(2,1)S(1)} %multiply_convert_fusion), channel_id=1, source_target_pairs={{1,0},{2,1},{3,2},{5,4},{6,5},{7,6},{9,8},{10,9},{11,10},{13,12},{... | collective-permute-start | bytes 1572872 | tf_op jit(solution)/shard_map/ppermute | solution.py:729
  225.8 21.1 %all-to-all-start = ((bf16[32,64,128]{2,1,0:T(8,128)(2,1)}), bf16[32,64,128]{2,1,0:T(8,128)(2,1)S(1)}, u32[]{:S(2)}, u32[]{:S(2)}) async-start(bf16[32,64,128]{2,1,0:T(8,128)(2,1)} %bitcast.72), calls=%async_computation | async-start | bytes 1048576 | tf_op jit(solution)/shard_map/all_to_all | solution.py:1175
  (84 other events, 1139.4 us)

commit v6 on v5

--- a/solution.py
+++ b/solution.py
@@ -652,8 +652,12 @@
     g_rank[...] += dot_nt(low[...], a_up[...])
     both = dot_tn(ranks[...], low[...])
     to = sel[8 + g]
-    put_inner_parts(sent, to, p_up_z[0], order, 0)
-    put_inner_parts(sent, to, both[:size] + both[size:], order, width // sent.shape[0])
+    moved = dot(jnp.concatenate([p_up_z[0], both[:size] + both[size:]], axis=0).astype(bf16), order[...]).astype(bf16)
+    hp = width // sent.shape[0]
+    for d in range(sent.shape[0]):
+        for n in range(2):
+            piece = moved[n * size : (n + 1) * size, d * hp : (d + 1) * hp]
+            sent[d, to, size : 2 * size, n * hp : (n + 1) * hp] = piece
 
     @pl.when(g == pl.num_programs(0) - 1)
     def _():
@@ -704,15 +708,14 @@
 def collect_kernel(picks, arrived, up_out, down_out, down_in, up_in, sums):
     dp, tp, rows, _ = arrived.shape
     rank = rows // 4
+    sums[...] = jnp.zeros_like(sums)
     for d in range(dp):
         one = arrived[d, 0].astype(f32)
         for t in range(1, tp):
             one = one + arrived[d, t].astype(f32)
-        sums[d] = one
+        sums[picks[d]] += one
     for b in range(up_out.shape[0]):
-        total = jnp.zeros(arrived.shape[2:], f32)
-        for d in range(dp):
-            total = total + jnp.where(picks[d] == b, sums[d], 0.0)
+        total = sums[b]
         up_out[b] = total[:rank, : up_out.shape[2]]
         down_out[b] = total[rank : 2 * rank].T[: down_out.shape[1]]
         down_in[b] = total[2 * rank : 3 * rank, : down_in.shape[2]]
@@ -1177,7 +1180,7 @@
     shapes = [(adapters, rank, d_rows), (adapters, hp, rank), (adapters, rank, d_rows), (adapters, 2 * hp, rank)]
     grad_out_up, grad_out_down, grad_in_down, grad_in_up = call(
         selecting(collect_kernel), [(s, f32) for s in shapes], [full(*sent.shape)],
-        [full(*s) for s in shapes], [pltpu.VMEM((dp_size,) + sent.shape[2:], f32)], mega, mega, 1,
+        [full(*s) for s in shapes], [pltpu.VMEM((adapters,) + sent.shape[2:], f32)], mega, mega, 1,
     )(picks, arrived)
 
     grad_out_down = grad_out_down.reshape(out_down.shape)

time: 250 us -> 250 us (level)
  no operation moved by 1% of the time
where the time goes in v6:
time: 250 us; the launch traced here: 249 us
  Pallas kernels  120 us (48%)
  starting transfers between devices  64.7 us (26%)
  waiting for transfers between devices  33.2 us (13%)
  other arithmetic  14.7 us (6%)
  local copies, waits for them, and re-layouts  13.9 us (6%)
    pallas_call x1, Pallas kernels, shards(): call(selecting(middle_kernel, weights=n_w, hops=hops, inner=inner), [((bl...  36.8 us
    ppermute x25, starting transfers between devices, swap(): return lax.ppermute(x, 'dp', [(i, i ^ 1 << bit) for i in range(n)])  24.4 us
    ppermute x15, starting transfers between devices, around_tensor(): lax.ppermute(x, 'tensor', [(i, (i + s) % n) for i in range(n)])  19.8 us
    pallas_call x1, Pallas kernels, shards(): call(plain(back_state_kernel, hops=hops), [(big, bf16), ((own, 2 * state)...  15.4 us
    ppermute x3, waiting for transfers between devices, down(): return lax.ppermute(x, 'tensor', [(i + 1, i) for i in range(n - 1)])  12.6 us
    pallas_call x1, Pallas kernels, shards(): call(plain(proj_kernel, weights=n_w), [(big, f32), (big, bf16), ((state,...  12.6 us
    pallas_call x1, Pallas kernels, shards(): call(plain(back_within_kernel), [(big, f32), ((blocks, chunk, chunk), f32...  12 us
    pallas_call x1, Pallas kernels, shards(): call(selecting(tokens_kernel, weights=n_w), [((own, width), f32)], [cols(...  11.9 us
  transfers between devices with their start and end apart: 49, of which 12 were waited for; matrix products, arithmetic and copies ran while one was open for 9% of the time, Pallas kernels for 24%

profile of v6, /device:TPU:1, one launch (start us, length us, event | category | flops | bytes accessed | tf_op | source)
XLA Modules:
  0.0 248.7 jit_solution(13315135054330313940)
XLA Ops:
  2.2 3.2 %collective-permute-start.11 = (bf16[128,512]{1,0:T(8,128)(2,1)S(1)}, bf16[128,512]{1,0:T(8,128)(2,1)S(1)}, u32[]{:S(2)}, u32[]{:S(2)}) collective-permute-start(bf16[128,512]{1,0:T(8,128)(2,1)S(1)} %bitcast.117), channel_id=1, source_target_pairs={{0,2},{1,3},{2,0},{3,1},{4,6},{5,7},{6,4},{7,5},{8,10},{9,11},{10,... | collective-permute-start | bytes 393224 | tf_op jit(solution)/shard_map/ppermute | solution.py:737
  6.7 2.0 collective-permute-start.12
  9.4 1.9 pack_kernel.1
  23.0 3.5 %collective-permute-done.2 = bf16[2,800,128]{2,1,0:T(8,128)(2,1)S(1)} collective-permute-done((bf16[2,800,128]{2,1,0:T(8,128)(2,1)S(1)}, bf16[2,800,128]{2,1,0:T(8,128)(2,1)S(1)}, u32[]{:S(2)}, u32[]{:S(2)}) %collective-permute-start.2) | collective-permute-done | bytes 409632 | tf_op jit(solution)/shard_map/ppermute | solution.py:755
  28.9 3.3 %collective-permute-start.3 = (bf16[4,800,128]{2,1,0:T(8,128)(2,1)}, bf16[4,800,128]{2,1,0:T(8,128)(2,1)}, u32[]{:S(2)}, u32[]{:S(2)}) collective-permute-start(bf16[4,800,128]{2,1,0:T(8,128)(2,1)} %pad_maximum_fusion.1), channel_id=1, source_target_pairs={{0,4},{4,0},{8,12},{12,8},{16,20},{20,16},{24,28},{28,24},{1,5},{5... | collective-permute-start | bytes 2457608 | tf_op jit(solution)/shard_map/ppermute | solution.py:742
  36.4 2.3 collective-permute-start.8
  41.2 2.0 collective-permute-done.7
  49.4 3.1 %collective-permute-start.6 = (bf16[320,128]{1,0:T(8,128)(2,1)S(1)}, bf16[320,128]{1,0:T(8,128)(2,1)S(1)}, u32[]{:S(2)}, u32[]{:S(2)}) collective-permute-start(bf16[320,128]{1,0:T(8,128)(2,1)S(1)} %get-tuple-element.121), channel_id=1, source_target_pairs={{0,3},{1,0},{2,1},{3,2},{4,7},{5,4},{6,5},{7,6},{8,11},{9,8},{10,9... | collective-permute-start | bytes 245768 | tf_op jit(solution)/shard_map/ppermute | solution.py:737
  52.6 1.9 pad_maximum_fusion.3.refs_5_
  55.7 2.5 %collective-permute-done.37.refs_2_ = bf16[2,2,128,512]{3,2,1,0:T(8,128)(2,1)} collective-permute-done((bf16[2,2,128,512]{3,2,1,0:T(8,128)(2,1)S(1)}, bf16[2,2,128,512]{3,2,1,0:T(8,128)(2,1)}, u32[]{:S(2)}, u32[]{:S(2)}) %collective-permute-start.37) | collective-permute-done | bytes 524320 | tf_op jit(solution)/shard_map/ppermute | solution.py:742
  58.3 2.2 collective-permute-start.41
  63.1 8.5 %prep_kernel.1 = (bf16[528,1024]{1,0:T(8,128)(2,1)}, bf16[512,1024]{1,0:T(8,128)(2,1)}, bf16[528,32]{1,0:T(8,128)(2,1)}, bf16[512,32]{1,0:T(8,128)(2,1)}, bf16[5...) custom-call(s32[33]{0:T(128)} %concatenate.42.sel_ref, ...), custom_call_target="tpu_custom_call" | custom-call | flops 536870912 | bytes 6291456 | tf_op jit(solution)/shard_map/prep_kernel/pallas_call | solution.py:1013
  74.2 2.7 %collective-permute-start.32 = (bf16[128,512]{1,0:T(8,128)(2,1)S(1)}, bf16[128,512]{1,0:T(8,128)(2,1)S(1)}, u32[]{:S(2)}, u32[]{:S(2)}) collective-permute-start(bf16[128,512]{1,0:T(8,128)(2,1)S(1)} %bitcast.127), channel_id=1, source_target_pairs={{0,3},{1,0},{2,1},{3,2},{4,7},{5,4},{6,5},{7,6},{8,11},{9,8},{10,9... | collective-permute-start | bytes 393224 | tf_op jit(solution)/shard_map/ppermute | solution.py:737
  78.2 12.6 %proj_kernel.1 = (f32[512,2048]{1,0:T(8,128)}, bf16[512,2048]{1,0:T(8,128)(2,1)}, bf16[128,2048]{1,0:T(8,128)(2,1)}) custom-call(s32[33]{0:T(128)} %concatenate.42.sel_ref, bf16[528,1024]{1,0:T(8,128)(2,1)} %get-tuple-element.62.refs_0_, bf16[2,2,128,512]{3,2,1,0:T(8,128)(2,1)} %copy-done.36, bf16[2,2,128,512]{3,2,1,0:T(8,128)(2,1)} %collective-permute-done.37.refs_2_, ...), custom_call_target="tpu_custom_call" | custom-call | flops 2147483648 | bytes 12582912 | tf_op jit(solution)/shard_map/proj_kernel/pallas_call | solution.py:1039
  90.8 1.9 collective-permute-start.24
  92.7 2.5 collective-permute-start.43
  98.9 3.8 %collective-permute-done.33 = bf16[2,128,512]{2,1,0:T(8,128)(2,1)S(1)} collective-permute-done((bf16[2,128,512]{2,1,0:T(8,128)(2,1)S(1)}, bf16[2,128,512]{2,1,0:T(8,128)(2,1)S(1)}, u32[]{:S(2)}, u32[]{:S(2)}) %collective-permute-start.33) | collective-permute-done | bytes 262176 | tf_op jit(solution)/shard_map/ppermute | solution.py:742
  104.5 2.0 collective-permute-done.43.refs_17_
  109.0 4.4 %collective-permute-start.44 = (bf16[128,2048]{1,0:T(8,128)(2,1)S(1)}, bf16[128,2048]{1,0:T(8,128)(2,1)S(1)}, u32[]{:S(2)}, u32[]{:S(2)}) collective-permute-start(bf16[128,2048]{1,0:T(8,128)(2,1)S(1)} %multiply_convert_fusion.1), channel_id=1, source_target_pairs={{0,1},{1,2},{2,3},{4,5},{5,6},{6,7},{8,9},{9,10},{10,11},{12,13},{... | collective-permute-start | bytes 1572872 | tf_op jit(solution)/shard_map/ppermute | solution.py:727
  113.4 4.4 %collective-permute-done.34.refs_14_ = bf16[2,2,128,512]{3,2,1,0:T(8,128)(2,1)S(1)} collective-permute-done((bf16[2,2,128,512]{3,2,1,0:T(8,128)(2,1)S(1)}, bf16[2,2,128,512]{3,2,1,0:T(8,128)(2,1)S(1)}, u32[]{:S(2)}, u32[]{:S(2)}) %collective-permute-start.34) | collective-permute-done | bytes 524320 | tf_op jit(solution)/shard_map/ppermute | solution.py:742
  118.8 2.0 collective-permute-start.30
  122.1 5.1 %within_kernel.1.refs_22_ = f32[512,2048]{1,0:T(8,128)} custom-call(s32[33]{0:T(128)S(1)} %copy-done.26, bf16[512,2048]{1,0:T(8,128)(2,1)S(1)} %copy-done.1, bf16[512,768]{1,0:T(8,128)(2,1)S(1)} %copy-done.2, f32[4,4,8,128]{3,2,1,0:T(8,128)S(1)} %copy-done.25, f32[2,4,128,128]{3,2,1,0:T(8,128)S(1)} %copy-done.5, bf16[128,4096]{1,0:T(8,128)(2,1)S(1)} %copy-done.10), custom_call_target="tpu_custom_call" | custom-call | flops 2147483648 | bytes 6291456 | tf_op jit(solution)/shard_map/within_kernel/pallas_call | solution.py:1060
  129.0 36.8 %middle_kernel.1 = (bf16[4,128,2048]{2,1,0:T(8,128)(2,1)}, f32[512,1024]{1,0:T(8,128)}, bf16[8,4,32,128]{3,2,1,0:T(8,128)(2,1)}, f32[512,2048]{1,0:T(8,128)}, bf...) custom-call(s32[33]{0:T(128)} %concatenate.42.sel_ref, ...), custom_call_target="tpu_custom_call" | custom-call | flops 8589934592 | bytes 41943040 | tf_op jit(solution)/shard_map/middle_kernel/pallas_call | solution.py:1092
  167.2 12.0 %back_within_kernel.1 = (f32[512,2048]{1,0:T(8,128)}, f32[4,128,128]{2,1,0:T(8,128)}, f32[512,128]{1,0:T(8,128)}) custom-call(s32[33]{0:T(128)} %concatenate.42.sel_ref, f32[512,2048]{1,0:T(8,128)} %get-tuple-element.87.refs_0_.refs_3_, f32[512,128]{1,0:T(8,128)} %get-tuple-element.88.refs_1_, ...), custom_call_target="tpu_custom_call" | custom-call | flops 4294967296 | bytes 14680064 | tf_op jit(solution)/shard_map/back_within_kernel/pallas_call | solution.py:1114
  179.2 3.2 %collective-permute-done.45.refs_0_ = bf16[128,2048]{1,0:T(8,128)(2,1)S(1)} collective-permute-done((bf16[128,2048]{1,0:T(8,128)(2,1)}, bf16[128,2048]{1,0:T(8,128)(2,1)S(1)}, u32[]{:S(2)}, u32[]{:S(2)}) %collective-permute-start.45) | collective-permute-done | bytes 524320 | tf_op jit(solution)/shard_map/ppermute | solution.py:732
  184.2 8.2 %in_z_kernel.1 = (f32[512,1024]{1,0:T(8,128)}, f32[512,16]{1,0:T(8,128)S(1)}, f32[4,16,512]{2,1,0:T(8,128)S(1)}) custom-call(s32[33]{0:T(128)S(1)} %copy-done.27, bf16[512,2048]{1,0:T(8,128)(2,1)} %get-tuple-element.91.refs_0_, bf16[2,2,128,512]{3,2,1,0:T(8,128)(2,1)S(1)} %copy-done.16, bf16[2,2,128,512]{3,2,1,0:T(8,128)(2,1)} %collective-permute-done.17.refs_2_, ...), custom_call_target="tpu_custom_call" | custom-call | flops 2147483648 | bytes 8388608 | tf_op jit(solution)/shard_map/in_z_kernel/pallas_call | solution.py:1125
  192.5 5.6 %collective-permute-done.46.refs_1_ = bf16[128,2048]{1,0:T(8,128)(2,1)S(1)} collective-permute-done((bf16[128,2048]{1,0:T(8,128)(2,1)S(1)}, bf16[128,2048]{1,0:T(8,128)(2,1)S(1)}, u32[]{:S(2)}, u32[]{:S(2)}) %collective-permute-start.46) | collective-permute-done | bytes 524320 | tf_op jit(solution)/shard_map/ppermute | solution.py:732
  198.2 15.4 %back_state_kernel.1 = (bf16[512,2048]{1,0:T(8,128)(2,1)}, f32[512,256]{1,0:T(8,128)S(1)}, bf16[512,32]{1,0:T(8,128)(2,1)S(1)}, bf16[16,2304]{1,0:T(8,128)(2,1)S(1)}, f32[16,2048]{1,0:T(8,128)S(1)}) custom-call(s32[33]{0:T(128)S(1)} %copy-done.27, bf16[128,2048]{1,0:T(8,128)(2,1)S(1)} %collective-permute-done.45.refs_0_, ...), custom_call_target="tpu_custom_call" | custom-call | flops 2147483648 | bytes 25165824 | tf_op jit(solution)/shard_map/back_state_kernel/pallas_call | solution.py:1136
  215.0 3.8 %collective-permute-done.47.refs_2_.refs_12_ = bf16[16,2304]{1,0:T(8,128)(2,1)S(1)} collective-permute-done((bf16[16,2304]{1,0:T(8,128)(2,1)S(1)}, bf16[16,2304]{1,0:T(8,128)(2,1)S(1)}, u32[]{:S(2)}, u32[]{:S(2)}) %collective-permute-start.47) | collective-permute-done | bytes 73760 | tf_op jit(solution)/shard_map/ppermute | solution.py:732
  218.8 5.5 %in_x_kernel.1 = (bf16[512,2048]{1,0:T(8,128)(2,1)}, f32[512,16]{1,0:T(8,128)S(1)}, bf16[8,4,32,128]{3,2,1,0:T(8,128)(2,1)S(1)}) custom-call(s32[33]{0:T(128)S(1)} %copy-done.27, bf16[512,2048]{1,0:T(8,128)(2,1)} %get-tuple-element.99.refs_0_, f32[16,2048]{1,0:T(8,128)S(1)} %get-tuple-element.100.refs_1_, ...), custom_call_target="tpu_custom_call", output_to_operand_aliasing={{0}: (1, {})} | custom-call | flops 268435456 | bytes 8388608 | tf_op jit(solution)/shard_map/in_x_kernel/pallas_call | solution.py:1153
  225.8 5.8 %all-to-all-start = ((bf16[32,64,128]{2,1,0:T(8,128)(2,1)}), bf16[32,64,128]{2,1,0:T(8,128)(2,1)S(1)}, u32[]{:S(2)}, u32[]{:S(2)}) async-start(bf16[32,64,128]{2,1,0:T(8,128)(2,1)} %bitcast.72), calls=%async_computation | async-start | bytes 1048576 | tf_op jit(solution)/shard_map/all_to_all | solution.py:1178
  233.2 11.9 %tokens_kernel.1 = f32[512,1024]{1,0:T(8,128)} custom-call(s32[33]{0:T(128)} %concatenate.42.sel_ref, bf16[512,2048]{1,0:T(8,128)(2,1)} %get-tuple-element.105.refs_0_, bf16[2,2,128,512]{3,2,1,0:T(8,128)(2,1)} %copy-done.36, bf16[2,2,128,512]{3,2,1,0:T(8,128)(2,1)} %collective-permute-done.37.refs_2_, ...), custom_call_target="tpu_custom_call" | custom-call | flops 2147483648 | bytes 14680064 | tf_op jit(solution)/shard_map/tokens_kernel/pallas_call | solution.py:1163
  (286 shorter events, 60.2 us)
Async XLA Ops:
  2.2 16.9 %collective-permute-start.11 = (bf16[128,512]{1,0:T(8,128)(2,1)S(1)}, bf16[128,512]{1,0:T(8,128)(2,1)S(1)}, u32[]{:S(2)}, u32[]{:S(2)}) collective-permute-start(bf16[128,512]{1,0:T(8,128)(2,1)S(1)} %bitcast.117), channel_id=1, source_target_pairs={{0,2},{1,3},{2,0},{3,1},{4,6},{5,7},{6,4},{7,5},{8,10},{9,11},{10,... | collective-permute-start | bytes 393224 | tf_op jit(solution)/shard_map/ppermute | solution.py:737
  5.4 13.7 %collective-permute-start.10 = (bf16[128,512]{1,0:T(8,128)(2,1)S(1)}, bf16[128,512]{1,0:T(8,128)(2,1)S(1)}, u32[]{:S(2)}, u32[]{:S(2)}) collective-permute-start(bf16[128,512]{1,0:T(8,128)(2,1)S(1)} %bitcast.118), channel_id=1, source_target_pairs={{0,1},{1,2},{2,3},{3,0},{4,5},{5,6},{6,7},{7,4},{8,9},{9,10},{10,1... | collective-permute-start | bytes 393224 | tf_op jit(solution)/shard_map/ppermute | solution.py:737
  6.7 12.4 %collective-permute-start.12 = (bf16[128,512]{1,0:T(8,128)(2,1)S(1)}, bf16[128,512]{1,0:T(8,128)(2,1)S(1)}, u32[]{:S(2)}, u32[]{:S(2)}) collective-permute-start(bf16[128,512]{1,0:T(8,128)(2,1)S(1)} %bitcast.119), channel_id=1, source_target_pairs={{0,3},{1,0},{2,1},{3,2},{4,7},{5,4},{6,5},{7,6},{8,11},{9,8},{10,9... | collective-permute-start | bytes 393224 | tf_op jit(solution)/shard_map/ppermute | solution.py:737
  19.1 15.0 %collective-permute-start.21 = (bf16[128,512]{1,0:T(8,128)(2,1)S(1)}, bf16[128,512]{1,0:T(8,128)(2,1)S(1)}, u32[]{:S(2)}, u32[]{:S(2)}) collective-permute-start(bf16[128,512]{1,0:T(8,128)(2,1)S(1)} %bitcast.121), channel_id=1, source_target_pairs={{0,3},{1,0},{2,1},{3,2},{4,7},{5,4},{6,5},{7,6},{8,11},{9,8},{10,9... | collective-permute-start | bytes 393224 | tf_op jit(solution)/shard_map/ppermute | solution.py:737
  19.3 14.9 %collective-permute-start.20 = (bf16[128,512]{1,0:T(8,128)(2,1)S(1)}, bf16[128,512]{1,0:T(8,128)(2,1)S(1)}, u32[]{:S(2)}, u32[]{:S(2)}) collective-permute-start(bf16[128,512]{1,0:T(8,128)(2,1)S(1)} %bitcast.122), channel_id=1, source_target_pairs={{0,2},{1,3},{2,0},{3,1},{4,6},{5,7},{6,4},{7,5},{8,10},{9,11},{10,... | collective-permute-start | bytes 393224 | tf_op jit(solution)/shard_map/ppermute | solution.py:737
  21.7 13.2 %collective-permute-start.14 = (bf16[2,128,512]{2,1,0:T(8,128)(2,1)S(1)}, bf16[2,128,512]{2,1,0:T(8,128)(2,1)S(1)}, u32[]{:S(2)}, u32[]{:S(2)}) collective-permute-start(bf16[2,128,512]{2,1,0:T(8,128)(2,1)S(1)} %pad_maximum_fusion.14), channel_id=1, source_target_pairs={{0,8},{4,12},{8,0},{12,4},{16,24},{20,28},{24,16},{28,20},{1,9},{5... | collective-permute-start | bytes 786440 | tf_op jit(solution)/shard_map/ppermute | solution.py:742
  28.9 15.5 %collective-permute-start.3 = (bf16[4,800,128]{2,1,0:T(8,128)(2,1)}, bf16[4,800,128]{2,1,0:T(8,128)(2,1)}, u32[]{:S(2)}, u32[]{:S(2)}) collective-permute-start(bf16[4,800,128]{2,1,0:T(8,128)(2,1)} %pad_maximum_fusion.1), channel_id=1, source_target_pairs={{0,4},{4,0},{8,12},{12,8},{16,20},{20,16},{24,28},{28,24},{1,5},{5... | collective-permute-start | bytes 2457608 | tf_op jit(solution)/shard_map/ppermute | solution.py:742
  40.9 13.5 %collective-permute-start.40 = (bf16[2,2,128,512]{3,2,1,0:T(8,128)(2,1)S(1)}, bf16[2,2,128,512]{3,2,1,0:T(8,128)(2,1)}, u32[]{:S(2)}, u32[]{:S(2)}) collective-permute-start(bf16[2,2,128,512]{3,2,1,0:T(8,128)(2,1)S(1)} %pad_maximum_fusion.7.refs_5_), channel_id=1, source_target_pairs={{0,8},{4,12},{8,0},{12,4},{16,24},{20,28},{24,16},{28,20},{1,9},{5... | collective-permute-start | bytes 1572872 | tf_op jit(solution)/shard_map/ppermute | solution.py:742
  43.1 15.1 %collective-permute-start.37 = (bf16[2,2,128,512]{3,2,1,0:T(8,128)(2,1)S(1)}, bf16[2,2,128,512]{3,2,1,0:T(8,128)(2,1)}, u32[]{:S(2)}, u32[]{:S(2)}) collective-permute-start(bf16[2,2,128,512]{3,2,1,0:T(8,128)(2,1)S(1)} %pad_maximum_fusion.6.refs_1_), channel_id=1, source_target_pairs={{0,16},{4,20},{8,24},{12,28},{16,0},{20,4},{24,8},{28,12},{1,17},{... | collective-permute-start | bytes 1572872 | tf_op jit(solution)/shard_map/ppermute | solution.py:742
  48.4 12.1 %collective-permute-start.5 = (bf16[320,128]{1,0:T(8,128)(2,1)S(1)}, bf16[320,128]{1,0:T(8,128)(2,1)S(1)}, u32[]{:S(2)}, u32[]{:S(2)}) collective-permute-start(bf16[320,128]{1,0:T(8,128)(2,1)S(1)} %get-tuple-element.121), channel_id=1, source_target_pairs={{0,2},{1,3},{2,0},{3,1},{4,6},{5,7},{6,4},{7,5},{8,10},{9,11},{10,... | collective-permute-start | bytes 245768 | tf_op jit(solution)/shard_map/ppermute | solution.py:737
  49.3 11.3 %collective-permute-start.4 = (bf16[320,128]{1,0:T(8,128)(2,1)S(1)}, bf16[320,128]{1,0:T(8,128)(2,1)S(1)}, u32[]{:S(2)}, u32[]{:S(2)}) collective-permute-start(bf16[320,128]{1,0:T(8,128)(2,1)S(1)} %get-tuple-element.121), channel_id=1, source_target_pairs={{0,1},{1,2},{2,3},{3,0},{4,5},{5,6},{6,7},{7,4},{8,9},{9,10},{10,1... | collective-permute-start | bytes 245768 | tf_op jit(solution)/shard_map/ppermute | solution.py:737
  49.4 11.5 %collective-permute-start.6 = (bf16[320,128]{1,0:T(8,128)(2,1)S(1)}, bf16[320,128]{1,0:T(8,128)(2,1)S(1)}, u32[]{:S(2)}, u32[]{:S(2)}) collective-permute-start(bf16[320,128]{1,0:T(8,128)(2,1)S(1)} %get-tuple-element.121), channel_id=1, source_target_pairs={{0,3},{1,0},{2,1},{3,2},{4,7},{5,4},{6,5},{7,6},{8,11},{9,8},{10,9... | collective-permute-start | bytes 245768 | tf_op jit(solution)/shard_map/ppermute | solution.py:737
  58.3 15.3 %collective-permute-start.41 = (bf16[2,2,128,512]{3,2,1,0:T(8,128)(2,1)S(1)}, bf16[2,2,128,512]{3,2,1,0:T(8,128)(2,1)}, u32[]{:S(2)}, u32[]{:S(2)}) collective-permute-start(bf16[2,2,128,512]{3,2,1,0:T(8,128)(2,1)S(1)} %pad_maximum_fusion.7.refs_5_), channel_id=1, source_target_pairs={{0,4},{4,0},{8,12},{12,8},{16,20},{20,16},{24,28},{28,24},{1,5},{5... | collective-permute-start | bytes 1572872 | tf_op jit(solution)/shard_map/ppermute | solution.py:742
  60.5 13.8 %collective-permute-start.38 = (bf16[2,2,128,512]{3,2,1,0:T(8,128)(2,1)S(1)}, bf16[2,2,128,512]{3,2,1,0:T(8,128)(2,1)}, u32[]{:S(2)}, u32[]{:S(2)}) collective-permute-start(bf16[2,2,128,512]{3,2,1,0:T(8,128)(2,1)S(1)} %pad_maximum_fusion.6.refs_1_), channel_id=1, source_target_pairs={{0,4},{4,0},{8,12},{12,8},{16,20},{20,16},{24,28},{28,24},{1,5},{5... | collective-permute-start | bytes 1572872 | tf_op jit(solution)/shard_map/ppermute | solution.py:742
  60.5 16.4 %collective-permute-start.42 = (bf16[2,2,128,512]{3,2,1,0:T(8,128)(2,1)}, bf16[2,2,128,512]{3,2,1,0:T(8,128)(2,1)}, u32[]{:S(2)}, u32[]{:S(2)}) collective-permute-start(bf16[2,2,128,512]{3,2,1,0:T(8,128)(2,1)} %collective-permute-done.40.refs_6_), channel_id=1, source_target_pairs={{0,4},{4,0},{8,12},{12,8},{16,20},{20,16},{24,28},{28,24},{1,5},{5... | collective-permute-start | bytes 1572872 | tf_op jit(solution)/shard_map/ppermute | solution.py:742
  61.0 15.9 %collective-permute-start.39 = (bf16[2,2,128,512]{3,2,1,0:T(8,128)(2,1)}, bf16[2,2,128,512]{3,2,1,0:T(8,128)(2,1)}, u32[]{:S(2)}, u32[]{:S(2)}) collective-permute-start(bf16[2,2,128,512]{3,2,1,0:T(8,128)(2,1)} %collective-permute-done.37.refs_2_), channel_id=1, source_target_pairs={{0,4},{4,0},{8,12},{12,8},{16,20},{20,16},{24,28},{28,24},{1,5},{5... | collective-permute-start | bytes 1572872 | tf_op jit(solution)/shard_map/ppermute | solution.py:742
  72.5 25.4 %collective-permute-start.23 = (bf16[2,2,128,512]{3,2,1,0:T(8,128)(2,1)}, bf16[2,2,128,512]{3,2,1,0:T(8,128)(2,1)}, u32[]{:S(2)}, u32[]{:S(2)}) collective-permute-start(bf16[2,2,128,512]{3,2,1,0:T(8,128)(2,1)} %pad_maximum_fusion.3.refs_5_), channel_id=1, source_target_pairs={{0,8},{4,12},{8,0},{12,4},{16,24},{20,28},{24,16},{28,20},{1,9},{5... | collective-permute-start | bytes 1572872 | tf_op jit(solution)/shard_map/ppermute | solution.py:742
  73.6 25.2 %collective-permute-start.17 = (bf16[2,2,128,512]{3,2,1,0:T(8,128)(2,1)S(1)}, bf16[2,2,128,512]{3,2,1,0:T(8,128)(2,1)}, u32[]{:S(2)}, u32[]{:S(2)}) collective-permute-start(bf16[2,2,128,512]{3,2,1,0:T(8,128)(2,1)S(1)} %pad_maximum_fusion.2.refs_1_), channel_id=1, source_target_pairs={{0,16},{4,20},{8,24},{12,28},{16,0},{20,4},{24,8},{28,12},{1,17},{... | collective-permute-start | bytes 1572872 | tf_op jit(solution)/shard_map/ppermute | solution.py:742
  74.2 16.6 %collective-permute-start.32 = (bf16[128,512]{1,0:T(8,128)(2,1)S(1)}, bf16[128,512]{1,0:T(8,128)(2,1)S(1)}, u32[]{:S(2)}, u32[]{:S(2)}) collective-permute-start(bf16[128,512]{1,0:T(8,128)(2,1)S(1)} %bitcast.127), channel_id=1, source_target_pairs={{0,3},{1,0},{2,1},{3,2},{4,7},{5,4},{6,5},{7,6},{8,11},{9,8},{10,9... | collective-permute-start | bytes 393224 | tf_op jit(solution)/shard_map/ppermute | solution.py:737
  76.9 15.8 %collective-permute-start.31 = (bf16[128,512]{1,0:T(8,128)(2,1)S(1)}, bf16[128,512]{1,0:T(8,128)(2,1)S(1)}, u32[]{:S(2)}, u32[]{:S(2)}) collective-permute-start(bf16[128,512]{1,0:T(8,128)(2,1)S(1)} %bitcast.128), channel_id=1, source_target_pairs={{0,2},{1,3},{2,0},{3,1},{4,6},{5,7},{6,4},{7,5},{8,10},{9,11},{10,... | collective-permute-start | bytes 393224 | tf_op jit(solution)/shard_map/ppermute | solution.py:737
  76.9 18.4 %collective-permute-start.27 = (bf16[2,128,512]{2,1,0:T(8,128)(2,1)}, bf16[2,128,512]{2,1,0:T(8,128)(2,1)S(1)}, u32[]{:S(2)}, u32[]{:S(2)}) collective-permute-start(bf16[2,128,512]{2,1,0:T(8,128)(2,1)} %pad_maximum_fusion.17), channel_id=1, source_target_pairs={{0,8},{4,12},{8,0},{12,4},{16,24},{20,28},{24,16},{28,20},{1,9},{5... | collective-permute-start | bytes 786440 | tf_op jit(solution)/shard_map/ppermute | solution.py:742
  90.8 13.3 %collective-permute-start.24 = (bf16[2,2,128,512]{3,2,1,0:T(8,128)(2,1)}, bf16[2,2,128,512]{3,2,1,0:T(8,128)(2,1)}, u32[]{:S(2)}, u32[]{:S(2)}) collective-permute-start(bf16[2,2,128,512]{3,2,1,0:T(8,128)(2,1)} %pad_maximum_fusion.3.refs_5_), channel_id=1, source_target_pairs={{0,4},{4,0},{8,12},{12,8},{16,20},{20,16},{24,28},{28,24},{1,5},{5... | collective-permute-start | bytes 1572872 | tf_op jit(solution)/shard_map/ppermute | solution.py:742
  92.7 13.8 %collective-permute-start.43 = (bf16[128,2048]{1,0:T(8,128)(2,1)}, bf16[128,2048]{1,0:T(8,128)(2,1)S(1)}, u32[]{:S(2)}, u32[]{:S(2)}) collective-permute-start(bf16[128,2048]{1,0:T(8,128)(2,1)} %get-tuple-element.74), channel_id=1, source_target_pairs={{0,1},{1,2},{2,3},{4,5},{5,6},{6,7},{8,9},{9,10},{10,11},{12,13},{... | collective-permute-start | bytes 1572872 | tf_op jit(solution)/shard_map/ppermute | solution.py:727
  98.8 10.1 %collective-permute-start.25 = (bf16[2,2,128,512]{3,2,1,0:T(8,128)(2,1)}, bf16[2,2,128,512]{3,2,1,0:T(8,128)(2,1)S(1)}, u32[]{:S(2)}, u32[]{:S(2)}) collective-permute-start(bf16[2,2,128,512]{3,2,1,0:T(8,128)(2,1)} %collective-permute-done.23.refs_6_), channel_id=1, source_target_pairs={{0,4},{4,0},{8,12},{12,8},{16,20},{20,16},{24,28},{28,24},{1,5},{5... | collective-permute-start | bytes 1572872 | tf_op jit(solution)/shard_map/ppermute | solution.py:742
  104.1 13.6 %collective-permute-start.34 = (bf16[2,2,128,512]{3,2,1,0:T(8,128)(2,1)S(1)}, bf16[2,2,128,512]{3,2,1,0:T(8,128)(2,1)S(1)}, u32[]{:S(2)}, u32[]{:S(2)}) collective-permute-start(bf16[2,2,128,512]{3,2,1,0:T(8,128)(2,1)S(1)} %pad_maximum_fusion.5.refs_13_), channel_id=1, source_target_pairs={{0,8},{4,12},{8,0},{12,4},{16,24},{20,28},{24,16},{28,20},{1,9},{5... | collective-permute-start | bytes 1572872 | tf_op jit(solution)/shard_map/ppermute | solution.py:742
  106.5 12.3 %collective-permute-start.28 = (bf16[2,2,128,512]{3,2,1,0:T(8,128)(2,1)S(1)}, bf16[2,2,128,512]{3,2,1,0:T(8,128)(2,1)S(1)}, u32[]{:S(2)}, u32[]{:S(2)}) collective-permute-start(bf16[2,2,128,512]{3,2,1,0:T(8,128)(2,1)S(1)} %pad_maximum_fusion.4.refs_9_), channel_id=1, source_target_pairs={{0,16},{4,20},{8,24},{12,28},{16,0},{20,4},{24,8},{28,12},{1,17},{... | collective-permute-start | bytes 1572872 | tf_op jit(solution)/shard_map/ppermute | solution.py:742
  107.4 19.9 %collective-permute-start.35 = (bf16[2,2,128,512]{3,2,1,0:T(8,128)(2,1)S(1)}, bf16[2,2,128,512]{3,2,1,0:T(8,128)(2,1)S(1)}, u32[]{:S(2)}, u32[]{:S(2)}) collective-permute-start(bf16[2,2,128,512]{3,2,1,0:T(8,128)(2,1)S(1)} %pad_maximum_fusion.5.refs_13_), channel_id=1, source_target_pairs={{0,4},{4,0},{8,12},{12,8},{16,20},{20,16},{24,28},{28,24},{1,5},{5... | collective-permute-start | bytes 1572872 | tf_op jit(solution)/shard_map/ppermute | solution.py:742
  108.9 18.5 %collective-permute-start.29 = (bf16[2,2,128,512]{3,2,1,0:T(8,128)(2,1)S(1)}, bf16[2,2,128,512]{3,2,1,0:T(8,128)(2,1)S(1)}, u32[]{:S(2)}, u32[]{:S(2)}) collective-permute-start(bf16[2,2,128,512]{3,2,1,0:T(8,128)(2,1)S(1)} %pad_maximum_fusion.4.refs_9_), channel_id=1, source_target_pairs={{0,4},{4,0},{8,12},{12,8},{16,20},{20,16},{24,28},{28,24},{1,5},{5... | collective-permute-start | bytes 1572872 | tf_op jit(solution)/shard_map/ppermute | solution.py:742
  109.0 18.4 %collective-permute-start.44 = (bf16[128,2048]{1,0:T(8,128)(2,1)S(1)}, bf16[128,2048]{1,0:T(8,128)(2,1)S(1)}, u32[]{:S(2)}, u32[]{:S(2)}) collective-permute-start(bf16[128,2048]{1,0:T(8,128)(2,1)S(1)} %multiply_convert_fusion.1), channel_id=1, source_target_pairs={{0,1},{1,2},{2,3},{4,5},{5,6},{6,7},{8,9},{9,10},{10,11},{12,13},{... | collective-permute-start | bytes 1572872 | tf_op jit(solution)/shard_map/ppermute | solution.py:727
  165.8 16.6 %collective-permute-start.45 = (bf16[128,2048]{1,0:T(8,128)(2,1)}, bf16[128,2048]{1,0:T(8,128)(2,1)S(1)}, u32[]{:S(2)}, u32[]{:S(2)}) collective-permute-start(bf16[128,2048]{1,0:T(8,128)(2,1)} %get-tuple-element.85), channel_id=1, source_target_pairs={{1,0},{2,1},{3,2},{5,4},{6,5},{7,6},{9,8},{10,9},{11,10},{13,12},{... | collective-permute-start | bytes 1572872 | tf_op jit(solution)/shard_map/ppermute | solution.py:732
  182.5 15.6 %collective-permute-start.46 = (bf16[128,2048]{1,0:T(8,128)(2,1)S(1)}, bf16[128,2048]{1,0:T(8,128)(2,1)S(1)}, u32[]{:S(2)}, u32[]{:S(2)}) collective-permute-start(bf16[128,2048]{1,0:T(8,128)(2,1)S(1)} %multiply_convert_fusion), channel_id=1, source_target_pairs={{1,0},{2,1},{3,2},{5,4},{6,5},{7,6},{9,8},{10,9},{11,10},{13,12},{... | collective-permute-start | bytes 1572872 | tf_op jit(solution)/shard_map/ppermute | solution.py:732
  225.8 21.1 %all-to-all-start = ((bf16[32,64,128]{2,1,0:T(8,128)(2,1)}), bf16[32,64,128]{2,1,0:T(8,128)(2,1)S(1)}, u32[]{:S(2)}, u32[]{:S(2)}) async-start(bf16[32,64,128]{2,1,0:T(8,128)(2,1)} %bitcast.72), calls=%async_computation | async-start | bytes 1048576 | tf_op jit(solution)/shard_map/all_to_all | solution.py:1178
  (84 other events, 1139.4 us)
